TPU v7x, 32 devices: a whole 2x2x4 slice. The times are simulated.
32 devices in a mesh: dp: 16 (over z, x, core), mp: 2 (over y).
Axes of the slice: x: 2, y: 2, z: 4, core: 2. Of those that a mesh axis runs over, the one named last changes fastest.
Arguments:
- tokens: bfloat16 [16384, 768], P('dp'), may hold values from -6 to 6
- mix_blend: float32 [16], P('dp'), may hold values from 0.2 to 0.8
- partner: int32 [16], replicated, may hold values from 0 to 15, as said below
- clip_ids: int32 [16, 1024], P('dp'), may hold values from 0 to 7, never falling along the last dimension, each value on 1 to 256 neighbouring positions
- gain_one: float32 [768], replicated, may hold values from 0.1 to 1.9
- shift_one: float32 [768], replicated, may hold values from -3 to 3
- qkv_weight: bfloat16 [768, 3, 768], P(None, None, 'mp'), may hold values from -0.21875 to 0.21875
- qv_bias: float32 [2, 768], P(None, 'mp'), may hold values from -3 to 3
- proj_weight: bfloat16 [768, 768], P('mp'), may hold values from -1.75 to 1.75
- proj_bias: float32 [768], replicated, may hold values from -3 to 3
- gain_two: float32 [768], replicated, may hold values from 0.1 to 1.9
- shift_two: float32 [768], replicated, may hold values from -3 to 3
- in_weight: bfloat16 [768, 3072], P(None, 'mp'), may hold values from -0.21875 to 0.21875
- in_bias: float32 [3072], P('mp'), may hold values from -3 to 3
- out_weight: bfloat16 [3072, 768], P('mp'), may hold values from -0.109375 to 0.109375
- out_bias: float32 [768], replicated, may hold values from -3 to 3
- cotangent: bfloat16 [16384, 768], P('dp'), may hold values from -6 to 6
Outputs:
- block_out: bfloat16 [16384, 768], P('dp')
- grad_tokens: bfloat16 [16384, 768], P('dp')
- grad_gain_one: float32 [768], P('dp')
- grad_shift_one: float32 [768], P('dp')
- grad_qkv_weight: float32 [768, 3, 768], P('dp', None, 'mp')
- grad_qv_bias: float32 [2, 768], P(None, ('mp', 'dp'))
- grad_proj_weight: float32 [768, 768], P('mp', 'dp')
- grad_proj_bias: float32 [768], P('dp')
- grad_gain_two: float32 [768], P('dp')
- grad_shift_two: float32 [768], P('dp')
- grad_in_weight: float32 [768, 3072], P('dp', 'mp')
- grad_in_bias: float32 [3072], P(('mp', 'dp'))
- grad_out_weight: float32 [3072, 768], P('mp', 'dp')
- grad_out_bias: float32 [768], P('dp')
Inputs may be any that keep to these rules, and one draw needn't show every extreme that they name: partner is a permutation of the 16 sequences in which no sequence is its own partner. `clip_ids`: within a sequence the clip ids never fall; a clip holds at most 256 tokens.
All inputs are finite; a program needn't handle non-finite values.
Results may differ from a plain program's by a relative error of at most 0.017.
Values may be sent and summed in bfloat16 or wider, within the bound.
No kernel may reach another device: no remote copies, remote signals or barrier semaphores. Data moves between devices by JAX's collectives and lax.ppermute only.
A program may use at most 192 MiB of HBM per device.

v0:
```python
import functools

import jax
import jax.numpy as jnp
from jax import lax
from jax.experimental import pallas as pl
from jax.experimental.pallas import tpu as pltpu
from jax.sharding import PartitionSpec as P

HEAD_DIM = 64
NORM_EPS = 1e-06
NEG_FILL = -1e30
SCORE_SCALE = HEAD_DIM ** (-0.5)
MAX_CLIP = 256
LANES = 128
F32 = jnp.float32
BF16 = jnp.bfloat16
MIB = 1 << 20
SMALL = pl.CostEstimate(flops=1 << 20, bytes_accessed=1 << 20, transcendentals=0)


def nn(left, right):
    return lax.dot_general(left, right, (((1,), (0,)), ((), ())), preferred_element_type=F32)


def nt(left, right):
    return lax.dot_general(left, right, (((1,), (1,)), ((), ())), preferred_element_type=F32)


def vmem():
    return pl.BlockSpec(memory_space=pltpu.VMEM)


def hbm():
    return pl.BlockSpec(memory_space=pltpu.HBM)


def anywhere():
    return pl.BlockSpec(memory_space=pl.ANY)


def smem():
    return pl.BlockSpec(memory_space=pltpu.SMEM)


def params(mib):
    return pltpu.CompilerParams(vmem_limit_bytes=mib * MIB)


def shape(dims, dtype):
    return jax.ShapeDtypeStruct(dims, dtype)


def row_stats(vector):
    mean = jnp.mean(vector, axis=-1, keepdims=True)
    centred = vector - mean
    spread = jnp.mean(centred * centred, axis=-1, keepdims=True)
    return centred, lax.rsqrt(spread + NORM_EPS)


def on_lanes(column):
    return jnp.broadcast_to(column, (column.shape[0], LANES))


def wide_rsqrt(inv, here, width):
    return jnp.concatenate([inv[here, :]] * (width // LANES), axis=1)


def row_sum(block):
    return jnp.sum(block, axis=0, keepdims=True)


def fold_rows(block):
    rows, width = block.shape
    return jnp.sum(block.reshape(rows // 8, 8, width), axis=0)


def pick_kernel(index, source, *refs):
    picked = refs[-1]

    def move(i, carry):
        picked[i] = source[index[i]]
        return carry

    lax.fori_loop(0, picked.shape[0], move, 0, unroll=4)


def pick(source, index, *after):
    dims = index.shape + source.shape[1:]
    return pl.pallas_call(
        pick_kernel,
        out_shape=shape(dims, source.dtype),
        in_specs=[smem(), vmem()] + [hbm()] * len(after),
        out_specs=vmem(),
        compiler_params=params(16),
        cost_estimate=SMALL,
        name="pick",
    )(index, source, *after)


def move(source, target, sem):
    return pltpu.make_async_copy(source, target, sem)


PARTS = 4


def part_moves(pairs, sems):
    moves = []
    for c in range(PARTS):
        row = []
        for n, (source, target) in enumerate(pairs):
            count = source.shape[0] // PARTS
            here = pl.ds(c * count, count)
            row.append(move(source.at[here, :], target.at[here, :], sems.at[n, c]))
        moves.append(row)
    return moves


def start_all(moves):
    for one in moves:
        one.start()


def wait_all(moves):
    for one in moves:
        one.wait()


def interleave(*streams):
    order = sorted(
        ((n + 0.5) / len(stream), which, n)
        for which, stream in enumerate(streams)
        for n in range(len(stream))
    )
    for _, which, n in order:
        streams[which][n]()


def spread_clips(seg_row, seg_b):
    for i in range(seg_b.shape[0] // LANES):
        here = pl.ds(i * LANES, LANES)
        seg_b[here, :] = jnp.broadcast_to(seg_row[:, here], (LANES, LANES)).T


def key_window(j, rows):
    window = min(rows, LANES + 2 * MAX_CLIP)
    here = pl.ds(pl.multiple_of(j * LANES, LANES), LANES)
    first = pl.multiple_of(jnp.clip(j * LANES - MAX_CLIP, 0, rows - window), LANES)
    return here, pl.ds(first, window)


def set_bias(bias, seg_b, seg_row, here, keys):
    filled = jnp.where(seg_b[keys, :] == seg_row[:, here], 0.0, NEG_FILL)
    bias[:, pl.ds(0, LANES)] = filled
    bias[:, pl.ds(LANES, LANES)] = filled


def two_heads(block):
    lane = lax.broadcasted_iota(jnp.int32, block.shape, 1)
    return jnp.concatenate(
        [block * (lane // HEAD_DIM == e).astype(BF16) for e in range(2)], axis=0
    )


def attention_kernel(
    blend, flags, seg_row, vecs, biases, tok, own, oth, w3, wp, *refs
):
    mixed, n1, normed, inv, q, k, v, att, part, lse = refs[-32:-22]
    (
        tok_v, own_v, oth_v, w3_v, wp_v, mixed_v, n1_v, q_v, k_v, v_v, att_v, part_v,
        vt, att_t, seg_b, bias, ones, normed_v, inv_v, in_sems, half_sems, out_sems,
    ) = refs[-22:]
    rows, width = tok.shape
    local = wp.shape[0]
    half_rows = rows // 2
    ratio = blend[0]
    blk = 32
    big = 256

    loads = [
        move(source, target, in_sems.at[n])
        for n, (source, target) in enumerate([(tok, tok_v), (w3, w3_v), (wp, wp_v)])
    ]
    halves = part_moves([(own, own_v), (oth, oth_v)], half_sems)
    loads[0].start()
    for part_of in halves:
        start_all(part_of)
    start_all(loads[1:])
    early = [
        move(source, target, out_sems.at[n])
        for n, (source, target) in enumerate(
            [
                (mixed_v, mixed), (n1_v, n1), (normed_v, normed), (inv_v, inv),
                (q_v, q), (k_v, k), (v_v, v),
            ]
        )
    ]
    ones[...] = jnp.ones_like(ones)
    spread_clips(seg_row, seg_b)

    loads[0].wait()
    steps = half_rows // PARTS // blk
    for n, src, half in ((0, own_v, flags[0]), (1, oth_v, 1 - flags[0])):
        for c in range(PARTS):
            halves[c][n].wait()

            def mix(i, carry, src=src, half=half, c=c):
                low = (c * steps + i) * blk
                here = pl.ds(pl.multiple_of(half * half_rows + low, blk), blk)
                there = pl.ds(pl.multiple_of(low, blk), blk)
                mine, other = tok_v[here, :].astype(F32), src[there, :].astype(F32)
                blended = ratio * mine + (1.0 - ratio) * other
                mixed_v[here, :] = blended
                centred, scale = row_stats(blended)
                inv_v[here, :] = on_lanes(scale)
                plain = centred * scale
                normed_v[here, :] = plain.astype(BF16)
                n1_v[here, :] = (plain * vecs[0:1, :] + vecs[1:2, :]).astype(BF16)
                return carry

            lax.fori_loop(0, steps, mix, 0, unroll=True)
    start_all(early[:4])

    loads[1].wait()
    for i in range(rows // big):
        here = pl.ds(i * big, big)
        rows_in = n1_v[here, :]
        queries = (nn(rows_in, w3_v[0]) + biases[0:1, :local]).astype(BF16).astype(F32)
        q_v[here, :] = (queries * SCORE_SCALE).astype(BF16)
        k_v[here, :] = nn(rows_in, w3_v[1]).astype(BF16)
        values = (nn(rows_in, w3_v[2]) + biases[0:1, local:]).astype(BF16)
        v_v[here, :] = values
        vt[:, here] = values.T
    start_all(early[4:])

    def attend(j, carry):
        here, keys = key_window(j, rows)
        set_bias(bias, seg_b, seg_row, here, keys)
        for p in range(local // LANES):
            pair = pl.ds(p * LANES, LANES)
            scores = nt(k_v[keys, pair], two_heads(q_v[here, pair])) + bias[...]
            top = jnp.max(scores, axis=0, keepdims=True)
            grown = jnp.exp(scores - top).astype(BF16)
            total = nn(ones[...], grown)[:1]
            out = (nn(vt[pair, keys], grown) / total).astype(BF16)
            logs = top + jnp.log(total)
            for e in range(2):
                lanes = slice(e * LANES, e * LANES + LANES)
                head = slice(e * HEAD_DIM, e * HEAD_DIM + HEAD_DIM)
                att_t[pl.ds(p * LANES + e * HEAD_DIM, HEAD_DIM), here] = out[head, lanes]
                lse[pl.ds(2 * p + e, 1), here] = logs[:, lanes]
        return carry

    lax.fori_loop(0, rows // LANES, attend, 0)

    loads[2].wait()
    last = []
    for i in range(rows // big):
        here = pl.ds(i * big, big)
        block = att_t[:, here].T
        att_v[here, :] = block
        part_v[here, :] = nn(block, wp_v[...]).astype(BF16)
        last.append(move(part_v.at[here, :], part.at[here, :], out_sems.at[8 + i]))
        last[-1].start()
    last.append(move(att_v, att, out_sems.at[7]))
    last[-1].start()
    wait_all(early + last)


def attention(blend, flags, segment, vecs, biases, tok, own, oth, w3, wp, *before):
    rows, width = tok.shape
    local = wp.shape[0]
    window = min(rows, LANES + 2 * MAX_CLIP)
    thin = shape((rows, local), BF16)
    tall = shape((rows, width), BF16)
    return pl.pallas_call(
        attention_kernel,
        out_shape=(
            shape((rows, width), F32), tall, tall, shape((rows, LANES), F32),
            thin, thin, thin, thin, tall, shape((local // HEAD_DIM, rows), F32),
        ),
        in_specs=[smem(), smem()] + [vmem()] * 3 + [anywhere()] * 3 + [hbm()] * (2 + len(before)),
        out_specs=[hbm()] * 9 + [vmem()],
        scratch_shapes=[
            pltpu.VMEM((rows, width), BF16),
            pltpu.VMEM((rows // 2, width), BF16),
            pltpu.VMEM((rows // 2, width), BF16),
            pltpu.VMEM(w3.shape, BF16),
            pltpu.VMEM(wp.shape, BF16),
            pltpu.VMEM((rows, width), F32),
            pltpu.VMEM((rows, width), BF16),
            pltpu.VMEM((rows, local), BF16),
            pltpu.VMEM((rows, local), BF16),
            pltpu.VMEM((rows, local), BF16),
            pltpu.VMEM((rows, local), BF16),
            pltpu.VMEM((rows, width), BF16),
            pltpu.VMEM((local, rows), BF16),
            pltpu.VMEM((local, rows), BF16),
            pltpu.VMEM((rows, LANES), F32),
            pltpu.VMEM((window, 2 * LANES), F32),
            pltpu.VMEM((16, window), BF16),
            pltpu.VMEM((rows, width), BF16),
            pltpu.VMEM((rows, LANES), F32),
            pltpu.SemaphoreType.DMA((3,)),
            pltpu.SemaphoreType.DMA((2, PARTS)),
            pltpu.SemaphoreType.DMA((8 + rows // 256,)),
        ],
        compiler_params=params(60),
        cost_estimate=SMALL,
        name="attention",
    )(
        blend, flags, segment, vecs, biases, tok, own, oth, w3, wp, *before,
    )


ERFC_SLOPE = 0.47
ERFC_COEFFS = (
    0.2663094668265691,
    0.2480096137831850,
    0.3362712657560771,
    -0.1262288063821733,
    0.6076790117752645,
    -0.4204702410368928,
    0.0884296765518492,
)


def gelu_parts(pre):
    bell = jnp.exp(pre * pre * -0.5)
    t = 1.0 / (1.0 + jnp.abs(pre) * (ERFC_SLOPE * 0.5**0.5))
    poly = 0.5 * ERFC_COEFFS[-1]
    for coeff in ERFC_COEFFS[-2::-1]:
        poly = poly * t + 0.5 * coeff
    tail = poly * t * bell
    cdf = jnp.where(pre >= 0, 1.0 - tail, tail)
    return pre * cdf, cdf + pre * bell * 0.3989422804014327


def turn_into(target, source, blocks):
    rows = source.shape[0]
    big = 256
    for i in range(rows // big):
        here = pl.ds(i * big, big)
        turned = source[here, :].T
        for start, place, count in blocks:
            target[pl.ds(place, count), here] = turned[start : start + count]


def lead_blocks(width, lead_rows):
    runs = width // lead_rows
    return [
        (run * lead_rows, ((run % 2) * (runs // 2) + run // 2) * lead_rows, lead_rows)
        for run in range(runs)
    ]


def feed_kernel(
    in_rows, out_rows, flags, vecs, biases, mixed, p_own, p_oth, cot, cot_t,
    w_in, w_out, w_out_one, w_out_two,
    hidden, part, gn_part, in_keep, in_send, out_keep, out_send, normed, inv, g_bin, g_bout,
    mixed_v, own_v, oth_v, cot_v, cot_tv, w_in_v, w_out_v, n2, n2_t, act, gp,
    g_in, g_out, normed_v, inv_v, in_sems, turn_sems, weight_sems, out_sems, grad_sems,
):
    rows, width = mixed.shape
    units = w_in.shape[1]
    blk = 32
    big = 256
    sub = 16
    home = flags[1] == 1
    across = flags[2]
    kept_out = jnp.where(home, flags[0], 1 - flags[0]) if in_rows != out_rows else across
    sides = (across, kept_out)

    loads = part_moves(
        [(mixed, mixed_v), (p_own, own_v), (p_oth, oth_v), (cot, cot_v)], in_sems
    )
    for part_of in loads:
        start_all(part_of)

    weights = [move(w_in, w_in_v, weight_sems.at[0])]
    weights[0].start()
    half = w_out.shape[0] // 2
    for n, (got, place) in enumerate([(w_out_one, across), (w_out_two, 1 - across)]):
        spot = pl.ds(pl.multiple_of(place * half, half), half)
        sem = weight_sems.at[1 + n]
        weights.append(move(w_out.at[spot, :], w_out_v.at[spot, :], sem))

        @pl.when(home)
        def _(spot=spot, sem=sem):
            move(w_out.at[spot, :], w_out_v.at[spot, :], sem).start()

        @pl.when(jnp.logical_not(home))
        def _(got=got, spot=spot, sem=sem):
            move(got, w_out_v.at[spot, :], sem).start()

    turns = [
        move(cot_t.at[pl.ds(start, count), :], cot_tv.at[pl.ds(place, count), :], turn_sems.at[n])
        for n, (start, place, count) in enumerate(lead_blocks(width, out_rows))
    ]
    start_all(turns)

    g_bout[...] = jnp.zeros_like(g_bout)
    steps = rows // PARTS // blk
    for c in range(PARTS):
        wait_all(loads[c])

        def norm(i, carry, c=c):
            here = pl.ds(pl.multiple_of((c * steps + i) * blk, blk), blk)
            attn = own_v[here, :].astype(F32) + oth_v[here, :].astype(F32)
            total = mixed_v[here, :] + attn + vecs[4:5, :]
            mixed_v[here, :] = total
            centred, scale = row_stats(total)
            inv_v[here, :] = on_lanes(scale)
            plain = centred * scale
            normed_v[here, :] = plain.astype(BF16)
            n2[here, :] = (plain * vecs[2:3, :] + vecs[3:4, :]).astype(BF16)
            g_bout[...] += fold_rows(cot_v[here, :].astype(F32))
            return carry

        lax.fori_loop(0, steps, norm, 0, unroll=4)
    stores = [
        move(source, target, out_sems.at[0, n])
        for n, (source, target) in enumerate(
            [(mixed_v, hidden), (normed_v, normed), (inv_v, inv)]
        )
    ]
    start_all(stores)
    turn_into(n2_t, n2, lead_blocks(width, in_rows))
    wait_all(weights)

    g_bin[...] = jnp.zeros_like(g_bin)

    def row_block(i, carry):
        here = pl.ds(pl.multiple_of(i * big, big), big)
        for j in range(units // width):
            cols = pl.ds(j * width, width)
            pre_all = nn(n2[here, :], w_in_v[:, cols])
            grad_all = nt(cot_v[here, :], w_out_v[cols, :])
            sums = jnp.zeros((8, width), F32)
            for s in range(big // sub):
                rng = slice(s * sub, s * sub + sub)
                value, slope = gelu_parts(pre_all[rng] + biases[1 + j : 2 + j, :])
                grad = grad_all[rng] * slope
                sums += fold_rows(grad)
                spot = pl.ds(pl.multiple_of(i * big + s * sub, sub), sub)
                act[spot, cols] = value.astype(BF16)
                gp[spot, cols] = grad.astype(BF16)
            g_bin[:, cols] += sums
        oth_v[here, :] = nt(gp[here, :], w_in_v[...]).astype(BF16)
        own_v[here, :] = nn(act[here, :], w_out_v[...]).astype(BF16)
        for n, (source, target) in enumerate([(oth_v, gn_part), (own_v, part)]):
            move(source.at[here, :], target.at[here, :], out_sems.at[1 + n, i]).start()
        return carry

    lax.fori_loop(0, rows // big, row_block, 0)
    for i in range(rows // big):
        here = pl.ds(i * big, big)
        for n, (source, target) in enumerate([(oth_v, gn_part), (own_v, part)]):
            stores.append(move(source.at[here, :], target.at[here, :], out_sems.at[1 + n, i]))

    wait_all(turns)
    half = width // 2
    for n, (turned, right, buf, keep, send) in enumerate(
        [(n2_t, gp, g_in, in_keep, in_send), (cot_tv, act, g_out, out_keep, out_send)]
    ):
        for side in range(2):
            lines = pl.ds(side * half, half)
            for j in range(units // width):
                cols = pl.ds(j * width, width)
                buf[side, :, cols] = nn(turned[lines, :], right[:, cols]).astype(BF16)
        for m, (side, target) in enumerate([(1 - sides[n], send), (sides[n], keep)]):
            stores.append(move(buf.at[side], target, grad_sems.at[n, m]))
            stores[-1].start()
    wait_all(stores)


def feed(
    in_rows, out_rows, flags, vecs, biases, mixed, p_own, p_oth, cot, cot_t,
    w_in, w_out, w_out_one, w_out_two,
):
    rows, width = mixed.shape
    units = w_in.shape[1]
    tall = shape((rows, width), BF16)
    grad = shape((width // 2, units), BF16)
    return pl.pallas_call(
        functools.partial(feed_kernel, in_rows, out_rows),
        out_shape=(
            shape((rows, width), F32), tall, tall, grad, grad, grad, grad,
            tall, shape((rows, LANES), F32), shape((8, units), F32), shape((8, width), F32),
        ),
        in_specs=[smem()] + [vmem()] * 2 + [hbm()] * 2 + [anywhere()] + [hbm()] * 6,
        out_specs=[hbm()] * 9 + [vmem()] * 2,
        scratch_shapes=[
            pltpu.VMEM((rows, width), F32),
            pltpu.VMEM((rows, width), BF16),
            pltpu.VMEM((rows, width), BF16),
            pltpu.VMEM((rows, width), BF16),
            pltpu.VMEM((width, rows), BF16),
            pltpu.VMEM(w_in.shape, BF16),
            pltpu.VMEM(w_out.shape, BF16),
            pltpu.VMEM((rows, width), BF16),
            pltpu.VMEM((width, rows), BF16),
            pltpu.VMEM((rows, units), BF16),
            pltpu.VMEM((rows, units), BF16),
            pltpu.VMEM((2, width // 2, units), BF16),
            pltpu.VMEM((2, width // 2, units), BF16),
            pltpu.VMEM((rows, width), BF16),
            pltpu.VMEM((rows, LANES), F32),
            pltpu.SemaphoreType.DMA((4, PARTS)),
            pltpu.SemaphoreType.DMA((width // out_rows,)),
            pltpu.SemaphoreType.DMA((3,)),
            pltpu.SemaphoreType.DMA((3, rows // 256)),
            pltpu.SemaphoreType.DMA((2, 2)),
        ],
        compiler_params=params(60),
        cost_estimate=SMALL,
        name="feed",
    )(
        flags, vecs, biases, mixed, p_own, p_oth, cot, cot_t,
        w_in, w_out, w_out_one, w_out_two,
    )


def attention_back_kernel(
    lead_rows, part_rows, flags, vecs, seg_row, lse, g_bin, g_bout, g_own, g_oth, cot, normed, inv,
    wp, att, k, q, v, w3, n1, normed_one,
    gh, part, keep, send, short,
    gh_v, own_v, oth_v, cot_v, normed_v, inv_v, wp_v, att_v, k_v, q_v, v_v, w3_v, n1_v, one_v, low_v, part_v,
    sums, tails, d_out, kt, dq_t, dk, dv, delta, seg_b, bias, raw, raw_g, low_p, low_g, n1_t, gh_t, grad_v, out,
    in_sems, row_sems, out_sems, last_sems,
):
    rows, width = cot.shape
    local = wp.shape[0]
    blk = 32
    big = 256
    blocks = lead_blocks(width, lead_rows)
    kept_side = flags[2]
    row_loads = part_moves(
        [(g_own, own_v), (g_oth, oth_v), (cot, cot_v), (normed, normed_v), (inv, inv_v)],
        row_sems,
    )
    for part_of in row_loads:
        start_all(part_of)
    loads = [
        move(source, target, in_sems.at[n])
        for n, (source, target) in enumerate(
            [
                (wp, wp_v), (att, att_v), (k, k_v), (q, q_v), (v, v_v), (w3, w3_v), (n1, n1_v),
                (normed_one, one_v),
            ]
        )
    ]
    start_all(loads)
    sums[...] = jnp.zeros_like(sums)
    dk[...] = jnp.zeros_like(dk)
    dv[...] = jnp.zeros_like(dv)
    spread_clips(seg_row, seg_b)

    steps = rows // PARTS // blk
    for c in range(PARTS):
        wait_all(row_loads[c])

        def norm(i, carry, c=c):
            here = pl.ds(pl.multiple_of((c * steps + i) * blk, blk), blk)
            grad = own_v[here, :].astype(F32) + oth_v[here, :].astype(F32)
            plain = normed_v[here, :].astype(F32)
            scaled = grad * vecs[2:3, :]
            mean_one = jnp.mean(scaled, axis=-1, keepdims=True)
            mean_two = jnp.mean(scaled * plain, axis=-1, keepdims=True)
            scale = wide_rsqrt(inv_v, here, width)
            back = cot_v[here, :].astype(F32) + scale * (scaled - mean_one - plain * mean_two)
            gh_v[here, :] = back
            low_v[here, :] = back.astype(BF16)
            sums[0] += fold_rows(grad * plain)
            sums[1] += fold_rows(grad)
            sums[2] += fold_rows(back)
            return carry

        lax.fori_loop(0, steps, norm, 0, unroll=2)
    stores = [move(gh_v, gh, out_sems.at[0])]
    stores[0].start()

    wait_all(loads[:3])
    heads = local // HEAD_DIM
    lane = lax.broadcasted_iota(jnp.int32, (delta.shape[0], local), 1)
    row = lax.broadcasted_iota(jnp.int32, (delta.shape[0], local), 0)
    of_head = (lane // HEAD_DIM == row).astype(BF16)

    def project(i, carry):
        here = pl.ds(pl.multiple_of(i * big, big), big)
        grad_out = nt(low_v[here, :], wp_v[...]).astype(BF16)
        d_out[here, :] = grad_out
        product = grad_out.astype(F32) * att_v[here, :].astype(F32)
        coarse = product.astype(BF16)
        fine = (product - coarse.astype(F32)).astype(BF16)
        delta[:, here] = nt(of_head, coarse) + nt(of_head, fine)
        kt[:, here] = k_v[here, :].T
        return carry

    lax.fori_loop(0, rows // big, project, 0)
    wait_all(loads[3:])

    pairs = heads // 2
    window = bias.shape[0]
    strip = 128
    strips = window // strip

    def attend(j, carry):
        here, keys = key_window(j, rows)
        first = pl.multiple_of(keys.start, LANES)
        set_bias(bias, seg_b, seg_row, here, keys)
        blocks_two = {}

        def two(p):
            if p not in blocks_two:
                pair = pl.ds(p * LANES, LANES)
                blocks_two[p] = (two_heads(q_v[here, pair]), two_heads(d_out[here, pair]))
            return blocks_two[p]

        def at_strip(n):
            return (
                pl.ds(pl.multiple_of(first + n * strip, strip), strip),
                pl.ds(n * strip, strip),
            )

        def products(p):
            pair = pl.ds(p * LANES, LANES)

            def scores(n):
                def run():
                    some, at = at_strip(n)
                    raw[p % 2, at, :] = nt(k_v[some, pair], two(p)[0])

                return run

            def grads(n):
                def run():
                    some, at = at_strip(n)
                    raw_g[p % 2, at, :] = nt(v_v[some, pair], two(p)[1])

                return run

            return [make(n) for n in range(strips) for make in (scores, grads)]

        def softmax_back(p):
            tops = jnp.concatenate([lse[pl.ds(2 * p + e, 1), here] for e in range(2)], axis=1)
            inner = jnp.concatenate([delta[pl.ds(2 * p + e, 1), here] for e in range(2)], axis=1)
            half = strip // 2

            def run_at(n):
                def run():
                    at = pl.ds(n * half, half)
                    probs = jnp.exp(raw[p % 2, at, :] + bias[at, :] - tops)
                    low_p[p % 2, at, :] = probs.astype(BF16)
                    low_g[p % 2, at, :] = (probs * (raw_g[p % 2, at, :] - inner)).astype(BF16)

                return run

            return [run_at(n) for n in range(2 * strips)]

        def sums_of(p):
            pair = pl.ds(p * LANES, LANES)

            def keys_of(n):
                def run():
                    some, at = at_strip(n)
                    dk[some, pair] += nn(low_g[p % 2, at, :], two(p)[0])

                return run

            def values_of(n):
                def run():
                    some, at = at_strip(n)
                    dv[some, pair] += nn(low_p[p % 2, at, :], two(p)[1])

                return run

            def queries():
                grad_q = nn(kt[pair, keys], low_g[p % 2]) * SCORE_SCALE
                for e in range(2):
                    lanes = slice(e * LANES, e * LANES + LANES)
                    head = slice(e * HEAD_DIM, e * HEAD_DIM + HEAD_DIM)
                    dq_t[pl.ds(p * LANES + e * HEAD_DIM, HEAD_DIM), here] = grad_q[head, lanes]

            return [make(n) for n in range(strips) for make in (keys_of, values_of)] + [queries]

        def turns():
            for target, source in ((n1_t, n1_v), (gh_t, low_v)):
                turned = source[here, :].T
                for start, place, count in blocks:
                    target[pl.ds(place, count), here] = turned[start : start + count]

        interleave(products(0), [turns])
        for p in range(pairs):
            matrix = (products(p + 1) if p + 1 < pairs else []) + (sums_of(p - 1) if p else [])
            interleave(softmax_back(p), matrix)
        interleave(sums_of(pairs - 1))
        return carry

    lax.fori_loop(0, rows // LANES, attend, 0)

    tails[...] = jnp.zeros_like(tails)

    def finish(i, carry):
        here = pl.ds(pl.multiple_of(i * big, big), big)
        grad_q, grad_k, grad_val = dq_t[:, here].T, dk[here, :], dv[here, :]
        tails[2, :, pl.ds(0, local)] += fold_rows(grad_q)
        tails[2, :, pl.ds(local, local)] += fold_rows(grad_val)
        lows = [grad.astype(BF16) for grad in (grad_q, grad_k, grad_val)]
        total = sum(nt(low, w3_v[n]) for n, low in enumerate(lows))
        part_v[here, :] = total.astype(BF16)
        tails[0] += fold_rows(total * one_v[here, :].astype(F32))
        tails[1] += fold_rows(total)
        for n, low in enumerate(lows):
            grad_v[here, pl.ds(n * local, local)] = low
        move(part_v.at[here, :], part.at[here, :], last_sems.at[i]).start()
        return carry

    lax.fori_loop(0, rows // big, finish, 0)
    for i in range(rows // big):
        here = pl.ds(i * big, big)
        stores.append(move(part_v.at[here, :], part.at[here, :], last_sems.at[i]))
    units = g_bin.shape[1]
    listed = [tails[0], tails[1], sums[0], sums[1], sums[2], g_bout[...], tails[2]]
    listed += [g_bin[:, pl.ds(n, width)] for n in range(0, units, width)]
    half = width // 2
    listed = [row_sum(block) for block in listed]
    for n, block in enumerate(listed):
        short[pl.ds(n, 1), :] = block
    if part_rows:
        sources = [
            (jnp.concatenate(listed[:6] + [jnp.zeros((2, width), F32)], axis=0), part_rows),
            (jnp.broadcast_to(listed[6][:, :local], (8, local)), local * part_rows // width),
            (jnp.broadcast_to(listed[6][:, local:], (8, local)), local * part_rows // width),
            (
                jnp.broadcast_to(jnp.concatenate(listed[7:], axis=1), (8, units)),
                units * part_rows // width,
            ),
        ]
        rest = jnp.zeros((part_rows - 8 * len(sources), LANES), F32)
        for start, place, count in blocks:
            for row in range(0, count, part_rows):
                d = (start + row) // part_rows
                parts = [
                    pltpu.roll(source, (source.shape[1] - d * size) % source.shape[1], 1)[:, :LANES]
                    for source, size in sources
                ]
                side, at = divmod(place + row, half)
                out[side, pl.ds(at, part_rows), pl.ds(4 * local, LANES)] = jnp.concatenate(
                    parts + [rest], axis=0
                ).astype(BF16)
    for side in range(2):
        lines = pl.ds(side * half, half)
        for n in range(3):
            cols = pl.ds(n * local, local)
            out[side, :, cols] = nn(n1_t[lines, :], grad_v[:, cols]).astype(BF16)
        out[side, :, pl.ds(3 * local, local)] = nn(gh_t[lines, :], att_v[...]).astype(BF16)
    for n, (side, target) in enumerate([(1 - kept_side, send), (kept_side, keep)]):
        stores.append(move(out.at[side], target, out_sems.at[1 + n]))
        stores[-1].start()
    wait_all(stores)


def attention_back(
    lead_rows, part_rows, flags, vecs, segment, lse, g_bin, g_bout, g_own, g_oth, cot, normed, inv,
    wp, att, k, q, v, w3, n1, normed_one,
):
    rows, width = cot.shape
    local = wp.shape[0]
    window = min(rows, LANES + 2 * MAX_CLIP)
    tall, thin = pltpu.VMEM((rows, width), BF16), pltpu.VMEM((rows, local), BF16)
    turned = pltpu.VMEM((width, rows), BF16)
    half = (width // 2, 4 * local + (LANES if part_rows else 0))
    return pl.pallas_call(
        functools.partial(attention_back_kernel, lead_rows, part_rows),
        out_shape=(
            shape((rows, width), F32),
            shape((rows, width), BF16),
            shape(half, BF16),
            shape(half, BF16),
            shape((7 + g_bin.shape[1] // width, width), F32),
        ),
        in_specs=[smem()] + [vmem()] * 5 + [hbm()] + [anywhere()] + [hbm()] * 11,
        out_specs=[hbm()] * 4 + [vmem()],
        scratch_shapes=[
            pltpu.VMEM((rows, width), F32),
            tall, tall, tall, tall,
            pltpu.VMEM((rows, LANES), F32),
            pltpu.VMEM(wp.shape, BF16),
            thin, thin, thin, thin,
            pltpu.VMEM(w3.shape, BF16),
            tall, tall, tall, tall,
            pltpu.VMEM((3, 8, width), F32),
            pltpu.VMEM((3, 8, width), F32),
            thin,
            pltpu.VMEM((local, rows), BF16),
            pltpu.VMEM((local, rows), F32),
            pltpu.VMEM((rows, local), F32),
            pltpu.VMEM((rows, local), F32),
            pltpu.VMEM((8, rows), F32),
            pltpu.VMEM((rows, LANES), F32),
            pltpu.VMEM((window, 2 * LANES), F32),
            pltpu.VMEM((2, window, 2 * LANES), F32),
            pltpu.VMEM((2, window, 2 * LANES), F32),
            pltpu.VMEM((2, window, 2 * LANES), BF16),
            pltpu.VMEM((2, window, 2 * LANES), BF16),
            turned, turned,
            pltpu.VMEM((rows, 3 * local), BF16),
            pltpu.VMEM((2,) + half, BF16),
            pltpu.SemaphoreType.DMA((8,)),
            pltpu.SemaphoreType.DMA((5, PARTS)),
            pltpu.SemaphoreType.DMA((3,)),
            pltpu.SemaphoreType.DMA((rows // 256,)),
        ],
        compiler_params=params(60),
        cost_estimate=SMALL,
        name="attention_back",
    )(
        flags, vecs, segment, lse, g_bin, g_bout, g_own, g_oth, cot, normed, inv,
        wp, att, k, q, v, w3, n1, normed_one,
    )


def mixed_back_kernel(blend, vecs, gh, g_own, g_oth, normed, inv, outgoing, kept, *refs):
    gh_v, own_v, oth_v, normed_v, inv_v, leave_v, kept_v, in_sems, out_sems = refs
    ratio = blend[0]
    rows, width = gh.shape
    blk = 32
    loads = part_moves(
        [(gh, gh_v), (g_own, own_v), (g_oth, oth_v), (normed, normed_v), (inv, inv_v)], in_sems
    )
    stores = part_moves([(leave_v, outgoing), (kept_v, kept)], out_sems)
    for part_of in loads:
        start_all(part_of)
    steps = rows // PARTS // blk
    for c in range(PARTS):
        wait_all(loads[c])

        def norm(i, carry, c=c):
            here = pl.ds(pl.multiple_of((c * steps + i) * blk, blk), blk)
            grad = own_v[here, :].astype(F32) + oth_v[here, :].astype(F32)
            plain = normed_v[here, :].astype(F32)
            scaled = grad * vecs[0:1, :]
            mean_one = jnp.mean(scaled, axis=-1, keepdims=True)
            mean_two = jnp.mean(scaled * plain, axis=-1, keepdims=True)
            scale = wide_rsqrt(inv_v, here, width)
            back = gh_v[here, :] + scale * (scaled - mean_one - plain * mean_two)
            leave_v[here, :] = ((1.0 - ratio) * back).astype(BF16)
            kept_v[here, :] = (ratio * back).astype(BF16)
            return carry

        lax.fori_loop(0, steps, norm, 0, unroll=4)
        start_all(stores[c])
    for part_of in stores:
        wait_all(part_of)


def mixed_back(blend, vecs, gh, g_own, g_oth, normed, inv):
    rows, width = gh.shape
    tall = pltpu.VMEM((rows, width), BF16)
    return pl.pallas_call(
        mixed_back_kernel,
        out_shape=(shape((rows, width), BF16), shape((rows, width), BF16)),
        in_specs=[smem(), vmem()] + [hbm()] * 2 + [anywhere()] + [hbm()] * 2,
        out_specs=[hbm(), hbm()],
        scratch_shapes=[
            pltpu.VMEM((rows, width), F32),
            tall, tall, tall, pltpu.VMEM((rows, LANES), F32), tall, tall,
            pltpu.SemaphoreType.DMA((5, PARTS)),
            pltpu.SemaphoreType.DMA((2, PARTS)),
        ],
        compiler_params=params(60),
        cost_estimate=SMALL,
        name="mixed_back",
    )(blend, vecs, gh, g_own, g_oth, normed, inv)


def shards(
    tokens,
    mix_blend,
    partner,
    clip_ids,
    gain_one,
    shift_one,
    qkv_weight,
    qv_bias,
    proj_weight,
    proj_bias,
    gain_two,
    shift_two,
    in_weight,
    in_bias,
    out_weight,
    out_bias,
    cotangent,
):
    rows, width = tokens.shape
    dp_count = lax.axis_size("dp")
    both = ("dp", "mp")
    bits = dp_count.bit_length() - 1
    seq = lax.axis_index("dp")
    mp = lax.axis_index("mp")
    core = lax.rem(seq, 2)
    home = core == mp
    all_dp = range(dp_count)

    def joint(d, m):
        return 2 * d + m

    core_swap = [(d, d ^ 1) for d in all_dp]
    home_to_pair = [(joint(d, d & 1), joint(d, 1 - (d & 1))) for d in all_dp]
    pair_to_home = [(joint(d, 1 - (d & 1)), joint(d, d & 1)) for d in all_dp]
    weight_move = home_to_pair + [
        (joint(d, 1 - (d & 1)), joint(d ^ 1, 1 - (d & 1))) for d in all_dp
    ]

    def swap(value):
        return lax.ppermute(value, "dp", core_swap)

    def chip_value(value):
        return jnp.where(home, value, swap(value))

    def after(value, *others):
        return lax.optimization_barrier((value,) + others)[0]

    def half_weight(value):
        return lax.ppermute(value, both, weight_move)

    part_rows = width // dp_count
    lead = min(n for n in range(1, bits) if (part_rows << n) % 16 == 0)
    lead_rows = part_rows << lead
    across = lax.rem(seq >> lead, 2)
    flags = jnp.stack([core, home.astype(jnp.int32), across]).astype(jnp.int32)

    def taken(value, index, axis):
        return lax.dynamic_index_in_dim(value, index, axis, keepdims=False)

    seq_small = chip_value(jnp.concatenate([mix_blend, clip_ids[0].astype(F32)]))
    blend, segment = seq_small[:1], seq_small[1:].reshape(1, rows)
    local = proj_weight.shape[0]
    units = in_bias.shape[0]
    half_small = jnp.concatenate([qv_bias.reshape(-1), in_bias])
    half_small = jnp.where(home, half_small, half_weight(half_small))
    biases = half_small.reshape(-1, width)
    vecs = jnp.stack([gain_one, shift_one, gain_two, shift_two, proj_bias])

    w3 = half_weight(qkv_weight.transpose(1, 0, 2))
    wp = half_weight(proj_weight)

    def two_way(value):
        halves = value.reshape(2, value.shape[0] // 2, value.shape[1])
        one = half_weight(taken(halves, across, 0))
        moves = [(joint(d, 1 - (d & 1)), joint(d ^ (1 << lead), 1 - (d & 1))) for d in all_dp]
        return value, one, lax.ppermute(one, both, moves)

    ids = jnp.arange(2 * dp_count, dtype=jnp.int32)
    piece = rows // (2 * 2 * dp_count)
    sent = tokens.reshape(2, dp_count, 2, piece, width)
    sent = lax.dynamic_index_in_dim(sent, mp, 2, keepdims=False)
    spread = lax.all_to_all(sent.transpose(1, 0, 2, 3), "dp", 0, 0, tiled=True)
    wanted = partner[(ids // 4) * 2 + ids % 2] * 2 + (ids // 2) % 2
    source_of = jnp.sum(
        jnp.where(partner[:, None] == ids[None, :dp_count], ids[:dp_count, None], 0),
        axis=0,
        dtype=jnp.int32,
    )
    source = source_of[ids // 2]
    wanted_back = (source // 2) * 4 + (ids % 2) * 2 + source % 2
    chosen = pick(spread.reshape(2 * dp_count, piece, width), wanted, w3, wp, half_small)
    partner_own = lax.all_to_all(chosen, both, 0, 0, tiled=True).reshape(rows // 2, width)
    w_out = two_way(out_weight)
    w_in = half_weight(after(in_weight, w_out[1]))

    tok = chip_value(tokens)
    cot = chip_value(cotangent)
    cot_t = cot.T
    partner_oth = swap(after(partner_own, tok, cot, vecs, segment, wanted_back))

    mixed, n1, normed_one, inv_one, q, k, v, att, attn_part, lse = attention(
        blend, flags, segment, vecs, biases, tok, partner_own, partner_oth, w3, wp, w_out[2], cot_t
    )
    pair_first = part_rows % 16 == 0
    fed = feed(
        lead_rows, part_rows if pair_first else lead_rows, flags, vecs, biases,
        mixed, attn_part, swap(attn_part), cot, cot_t, w_in, *w_out,
    )
    hidden, out_part, gn2_part, in_keep, in_send, out_keep, out_send = fed[:7]
    normed_two, inv_two, g_bin, g_bout = fed[7:]
    gn2_oth = swap(gn2_part)

    high, mid = dp_count >> (lead + 1), 1 << (lead - 1)
    pair_and_core = pair_to_home + [(joint(d, d & 1), joint(d ^ 1, d & 1)) for d in all_dp]
    pair_diagonal = [(joint(d, 1 - (d & 1)), joint(d ^ 1, d & 1)) for d in all_dp]

    def total(*terms):
        return sum(term.astype(F32) for term in terms)

    def send_across(value):
        return lax.ppermute(value, "dp", [(d, d ^ (1 << lead)) for d in all_dp])

    def send_pair(value):
        value = value.reshape(high, mid, 2, part_rows, -1)
        one = lax.ppermute(taken(value, jnp.where(home, 1 - core, core), 2), both, pair_and_core)
        two = lax.ppermute(taken(value, 1 - core, 2), both, pair_diagonal)
        held = taken(value, core, 2)
        return jnp.where(home, held, jnp.zeros_like(held)), one, two

    def far(value, *others):
        for shift, left in ((1, mid), (lead + 1, high)):
            while left > 1:
                radix = min(4, left)
                left //= radix
                value = value.reshape((-1, left, radix) + value.shape[-2:]).astype(BF16)
                spot = lax.rem(seq >> shift, radix)
                got = [
                    lax.ppermute(
                        taken(value, spot ^ flip, 2),
                        "dp",
                        [(d, d ^ (flip << shift)) for d in all_dp],
                    )
                    for flip in range(1, radix)
                ]
                value = total(taken(value, spot, 2), *after(got, *others))
                shift += radix.bit_length() - 1
        return value.reshape(value.shape[-2:])

    def send_first(keep, send):
        if not pair_first:
            return [keep, send_across(send)]
        one = lax.ppermute(send, both, pair_and_core)
        two = lax.ppermute(keep, both, pair_diagonal)
        return [jnp.where(home, keep, jnp.zeros_like(keep)), one, two]

    def send_second(value):
        if not pair_first:
            return send_pair(value)
        value = value.reshape(high, 2, mid, part_rows, -1)
        return taken(value, across, 1), send_across(taken(value, 1 - across, 1))

    in_got = send_across(in_send)
    out_first = send_first(out_keep, out_send)
    gh, gn1_part, attn_keep, attn_send, short = attention_back(
        lead_rows, part_rows if pair_first else 0, flags, vecs, segment, lse, g_bin, g_bout,
        gn2_part, gn2_oth, cot, normed_two, inv_two, wp, att, k, q, v, w3, n1, normed_one,
    )
    gn1_oth = swap(after(gn1_part, in_got, *out_first))
    attn_first = [attn_keep, send_across(attn_send)]
    in_terms = send_pair(total(in_keep, in_got).astype(BF16))
    outgoing, kept = mixed_back(blend, vecs, gh, gn1_part, gn1_oth, normed_one, inv_one)

    leaving = taken(outgoing.reshape(2, 2, dp_count, piece, width), core, 1)
    leaving = leaving.transpose(1, 0, 2, 3).reshape(2 * dp_count, piece, width)
    back = lax.all_to_all(leaving, both, 0, 0, tiled=True)

    in_value = total(*after(in_terms, leaving)).astype(BF16)
    sum_in = far(in_value)
    out_oth = swap(after(out_part, leaving))
    out_value = total(*after(out_first, in_value)).astype(BF16)
    out_terms = send_second(out_value)
    attn_value = total(*after(attn_first, out_value)).astype(BF16)
    attn_terms = send_pair(attn_value)
    block = hidden + (out_part.astype(F32) + after(out_oth, attn_value).astype(F32)) + out_bias
    block = block.astype(BF16)
    kept = kept.reshape(2, rows // 2, width)
    kept_got = half_weight(taken(kept, 1 - mp, 0))
    block_got = half_weight(block)

    def side_by_side(*groups):
        values = [total(*terms).reshape(high * mid, part_rows, -1) for terms in groups]
        return jnp.concatenate(values, axis=2).astype(BF16)

    returning = pick(back, wanted_back, attn_value, sum_in)
    returned = lax.all_to_all(
        returning.reshape(dp_count, 2, piece, width), "dp", 0, 0, tiled=True
    )
    returned = after(returned, kept_got)
    kept = jnp.where(home, taken(kept, mp, 0), kept_got)
    returned = returned.transpose(1, 0, 2, 3).reshape(rows // 2, width)
    mine = (kept.astype(F32) + returned.astype(F32)).astype(BF16)
    other = lax.ppermute(mine, "mp", [(0, 1), (1, 0)])
    block_out = jnp.where(home, block, after(block_got, mine))
    grad_tokens = jnp.where(
        jnp.arange(2)[:, None, None] == mp, mine[None], other[None]
    ).reshape(rows, width)

    marker = swap(returning[0, :, :LANES])
    summed = far(
        side_by_side(*(after(terms, marker) for terms in (out_terms, attn_terms))),
        mine,
    )
    summed = after(summed, other)
    sum_out, sum_attn = summed[:, :units], summed[:, units:]
    sum_qkv = sum_attn[:, : 3 * local].reshape(-1, 3, local)
    sum_proj = sum_attn[:, 3 * local : 4 * local].T
    quarter, eighth = local // dp_count, units // dp_count
    if pair_first:
        extra = sum_attn[:, 4 * local :]
        plain = extra[:6, :part_rows]
        ours = plain[:2] + lax.ppermute(plain[:2], "mp", [(0, 1), (1, 0)])
        plain = jnp.concatenate([ours, plain[2:]])
        sum_qv = jnp.stack([extra[8, :quarter], extra[16, :quarter]])
        sum_bin = extra[24, :eighth]
    else:
        counts = jnp.where((core == 0) | (jnp.arange(6) < 2), 1.0, 0.0).astype(F32)
        wide = (short[:6] * counts[:, None]).reshape(6, dp_count, 1, part_rows)
        wide = jnp.broadcast_to(wide, (6, dp_count, 2, part_rows)).transpose(1, 2, 0, 3)
        to_half = (jnp.arange(2) == core)[None, :, None]

        def half_terms(vectors):
            terms = vectors.reshape(vectors.shape[0], dp_count, -1).transpose(1, 0, 2)
            return jnp.where(to_half, terms.reshape(dp_count, 1, -1), 0.0)

        short = jnp.concatenate(
            [
                wide.reshape(dp_count, 2, -1),
                half_terms(short[6].reshape(2, local)),
                half_terms(short[7:].reshape(1, units)),
            ],
            axis=-1,
        ).reshape(2 * dp_count, -1)
        short = jnp.sum(lax.all_to_all(short, both, 0, 0, tiled=True), axis=0)
        plain = short[: 6 * part_rows].reshape(6, part_rows)
        sum_qv = short[6 * part_rows : 6 * part_rows + 2 * quarter].reshape(2, -1)
        sum_bin = short[6 * part_rows + 2 * quarter :]
    return (
        block_out,
        grad_tokens,
        plain[0],
        plain[1],
        sum_qkv,
        sum_qv,
        sum_proj,
        plain[4],
        plain[2],
        plain[3],
        sum_in,
        sum_bin,
        sum_out.T,
        plain[5],
    )


def solution(mesh):
    return jax.shard_map(
        shards,
        mesh=mesh,
        in_specs=(
            P("dp", None),
            P("dp"),
            P(),
            P("dp", None),
            P(),
            P(),
            P(None, None, "mp"),
            P(None, "mp"),
            P("mp", None),
            P(),
            P(),
            P(),
            P(None, "mp"),
            P("mp"),
            P("mp", None),
            P(),
            P("dp", None),
        ),
        out_specs=(
            P("dp", None),
            P("dp", None),
            P("dp"),
            P("dp"),
            P("dp", None, "mp"),
            P(None, ("mp", "dp")),
            P("mp", "dp"),
            P("dp"),
            P("dp"),
            P("dp"),
            P("dp", "mp"),
            P(("mp", "dp")),
            P("mp", "dp"),
            P("dp"),
        ),
        check_vma=False,
    )
```

profile of v0, /device:TPU:8, one launch (start us, length us, event | category | flops | bytes accessed | tf_op | source)
XLA Modules:
  0.0 280.0 jit_solution(8680681682783265217)
XLA Ops:
  2.2 2.1 copy_bitcast_fusion
  4.3 6.3 %all-to-all-start = ((bf16[16,2,16,768]{3,2,1,0:T(8,128)(2,1)}), bf16[16,2,16,768]{3,2,1,0:T(8,128)(2,1)S(1)}, u32[]{:S(2)}, u32[]{:S(2)}) async-start(bf16[16,2,16,768]{3,2,1,0:T(8,128)(2,1)} %copy_bitcast_fusion), calls=%async_computation | async-start | bytes 1572864 | tf_op jit(solution)/shard_map/all_to_all | solution.py:961
  11.4 2.4 dynamic-slice_bitcast_fusion
  14.5 8.1 %collective-permute-done = f32[2304]{0:T(1024)S(1)} collective-permute-done((f32[2304]{0:T(1024)S(1)}, f32[2304]{0:T(1024)S(1)}, u32[]{:S(2)}, u32[]{:S(2)}) %collective-permute-start) | collective-permute-done | bytes 9248 | tf_op jit(solution)/shard_map/ppermute | solution.py:928
  22.6 2.5 collective-permute-start.7
  25.1 3.9 %collective-permute-done.4.refs_1_.wp = bf16[384,768]{1,0:T(8,128)(2,1)S(1)} collective-permute-done((bf16[384,768]{1,0:T(8,128)(2,1)}, bf16[384,768]{1,0:T(8,128)(2,1)S(1)}, u32[]{:S(2)}, u32[]{:S(2)}) %collective-permute-start.4) | collective-permute-done | bytes 589856 | tf_op jit(solution)/shard_map/ppermute | solution.py:928
  31.8 6.6 %all-to-all-start.1 = ((bf16[32,16,768]{2,1,0:T(8,128)(2,1)}), bf16[32,16,768]{2,1,0:T(8,128)(2,1)}, u32[]{:S(2)}, u32[]{:S(2)}) async-start(bf16[32,16,768]{2,1,0:T(8,128)(2,1)} %copy-done.2), calls=%async_computation.1 | async-start | bytes 1572864 | tf_op jit(solution)/shard_map/all_to_all | solution.py:971
  41.6 3.5 %collective-permute-done.7.w_out_one = bf16[768,768]{1,0:T(8,128)(2,1)} collective-permute-done((bf16[768,768]{1,0:T(8,128)(2,1)}, bf16[768,768]{1,0:T(8,128)(2,1)}, u32[]{:S(2)}, u32[]{:S(2)}) %collective-permute-start.7) | collective-permute-done | bytes 1179680 | tf_op jit(solution)/shard_map/ppermute | solution.py:928
  48.9 8.8 %all-to-all-done.1 = bf16[32,16,768]{2,1,0:T(8,128)(2,1)} async-done(((bf16[32,16,768]{2,1,0:T(8,128)(2,1)}), bf16[32,16,768]{2,1,0:T(8,128)(2,1)}, u32[]{:S(2)}, u32[]{:S(2)}) %all-to-all-start.1) | async-done | bytes 786464 | tf_op jit(solution)/shard_map/all_to_all | solution.py:971
  64.4 20.7 %attention.1 = (f32[1024,768]{1,0:T(8,128)}, bf16[1024,768]{1,0:T(8,128)(2,1)}, bf16[1024,768]{1,0:T(8,128)(2,1)}, f32[1024,128]{1,0:T(8,128)}, bf16[1024,384]{1...) custom-call(f32[1]{0:T(128)} %slice.93.blend, ...), custom_call_target="tpu_custom_call" | custom-call | flops 1048576 | bytes 1048576 | tf_op jit(solution)/shard_map/attention/pallas_call | solution.py:277
  86.8 2.6 collective-permute-done.9.p_oth
  90.5 30.0 %feed.1 = (f32[1024,768]{1,0:T(8,128)}, bf16[1024,768]{1,0:T(8,128)(2,1)}, bf16[1024,768]{1,0:T(8,128)(2,1)}, bf16[384,1536]{1,0:T(8,128)(2,1)}, bf16[384,1536]{...) custom-call(s32[3]{0:T(128)} %pad_add_fusion.flags, ...), custom_call_target="tpu_custom_call" | custom-call | flops 1048576 | bytes 1048576 | tf_op jit(solution)/shard_map/feed/pallas_call | solution.py:486
  121.7 1.7 collective-permute-start.14
  125.9 30.1 %attention_back.1 = (f32[1024,768]{1,0:T(8,128)}, bf16[1024,768]{1,0:T(8,128)(2,1)}, bf16[384,1664]{1,0:T(8,128)(2,1)}, bf16[384,1664]{1,0:T(8,128)(2,1)}, f32[9,768]{1,0:T(8,128)}) custom-call(s32[3]{0:T(128)} %pad_add_fusion.flags, f32[5,768]{1,0:T(8,128)} %stack.46.vecs, f32[1,1024]{1,0:T(1,128)} %bitcast.133, f32[6,1024]{1,0:T(8,128)} %get-tuple-element.74.lse, ...), custom_call_target="tpu_custom_call" | custom-call | flops 1048576 | bytes 1048576 | tf_op jit(solution)/shard_map/attention_back/pallas_call | solution.py:775
  156.0 4.1 %collective-permute-start.15 = (bf16[1024,768]{1,0:T(8,128)(2,1)}, bf16[1024,768]{1,0:T(8,128)(2,1)}, u32[]{:S(2)}, u32[]{:S(2)}) collective-permute-start(bf16[1024,768]{1,0:T(8,128)(2,1)} %get-tuple-element.91.g_own), channel_id=1, source_target_pairs={{0,2},{2,0},{4,6},{6,4},{8,10},{10,8},{12,14},{14,12},{16,18},{18,... | collective-permute-start | bytes 4718600 | tf_op jit(solution)/shard_map/ppermute | solution.py:919
  160.1 1.9 add_convert_fusion.3
  165.3 6.9 %mixed_back.1 = (bf16[1024,768]{1,0:T(8,128)(2,1)}, bf16[1024,768]{1,0:T(8,128)(2,1)}) custom-call(f32[1]{0:T(128)} %slice.93.blend, f32[5,768]{1,0:T(8,128)} %stack.46.vecs, f32[1024,768]{1,0:T(8,128)} %get-tuple-element.86.gh, bf16[1024,768]{1,0:T(8,128)(2,1)} %get-tuple-element.91.g_own, bf16[1024,768]{1,0:T(8,128)(2,1)} %collective-permute-done.15.g_oth, ...), custom_call_target="tpu_custom_call" | custom-call | flops 1048576 | bytes 1048576 | tf_op jit(solution)/shard_map/mixed_back/pallas_call | solution.py:862
  174.3 8.6 %all-to-all-start.2 = ((bf16[32,16,768]{2,1,0:T(8,128)(2,1)}), bf16[32,16,768]{2,1,0:T(8,128)(2,1)S(1)}, u32[]{:S(2)}, u32[]{:S(2)}) async-start(bf16[32,16,768]{2,1,0:T(8,128)(2,1)} %bitcast.19), calls=%async_computation.2 | async-start | bytes 1572864 | tf_op jit(solution)/shard_map/all_to_all | solution.py:1054
  184.7 2.7 collective-permute-start.23
  187.9 2.2 add_convert_fusion.2
  190.1 9.6 %collective-permute-done.17 = bf16[384,1664]{1,0:T(8,128)(2,1)} collective-permute-done((bf16[384,1664]{1,0:T(8,128)(2,1)}, bf16[384,1664]{1,0:T(8,128)(2,1)}, u32[]{:S(2)}, u32[]{:S(2)}) %collective-permute-start.17) | collective-permute-done | bytes 1277984 | tf_op jit(solution)/shard_map/ppermute | solution.py:1000
  204.0 3.6 %collective-permute-start.28 = (bf16[4,1,48,1664]{3,2,0,1:T(8,128)(2,1)}, bf16[4,1,48,1664]{3,2,0,1:T(8,128)(2,1)}, u32[]{:S(2)}, u32[]{:S(2)}) collective-permute-start(bf16[4,1,48,1664]{3,2,0,1:T(8,128)(2,1)} %get-tuple-element.165), channel_id=1, source_target_pairs={{1,0},{2,3},{5,4},{6,7},{9,8},{10,11},{13,12},{14,15},{17,16},{18,... | collective-permute-start | bytes 1916936 | tf_op jit(solution)/shard_map/ppermute | solution.py:1004
  210.0 1.8 collective-permute-start.16
  211.8 3.2 %collective-permute-done.24 = bf16[1,1,48,1536]{3,2,1,0:T(8,128)(2,1)S(1)} collective-permute-done((bf16[1,1,48,1536]{3,2,1,0:T(8,128)(2,1)S(1)}, bf16[1,1,48,1536]{3,2,1,0:T(8,128)(2,1)S(1)}, u32[]{:S(2)}, u32[]{:S(2)}) %collective-permute-start.24) | collective-permute-done | bytes 147488 | tf_op jit(solution)/shard_map/ppermute | solution.py:1017
  218.3 4.5 %all-to-all-start.3 = ((bf16[16,2,16,768]{3,2,1,0:T(8,128)(2,1)}), bf16[16,2,16,768]{3,2,1,0:T(8,128)(2,1)}, u32[]{:S(2)}, u32[]{:S(2)}) async-start(bf16[16,2,16,768]{3,2,1,0:T(8,128)(2,1)} %bitcast.30), calls=%async_computation.3 | async-start | bytes 1572864 | tf_op jit(solution)/shard_map/all_to_all | solution.py:1074
  227.3 2.6 add_convert_fusion
  231.3 2.6 collective-permute-start.31
  234.6 7.2 %all-to-all-done.3 = bf16[16,2,16,768]{3,2,1,0:T(8,128)(2,1)} async-done(((bf16[16,2,16,768]{3,2,1,0:T(8,128)(2,1)}), bf16[16,2,16,768]{3,2,1,0:T(8,128)(2,1)}, u32[]{:S(2)}, u32[]{:S(2)}) %all-to-all-start.3) | async-done | bytes 786464 | tf_op jit(solution)/shard_map/all_to_all | solution.py:1074
  243.9 2.7 collective-permute-start.25
  246.5 14.3 %collective-permute-done.31 = bf16[1,1,48,3200]{3,2,1,0:T(8,128)(2,1)} collective-permute-done((bf16[1,1,48,3200]{3,2,1,0:T(8,128)(2,1)}, bf16[1,1,48,3200]{3,2,1,0:T(8,128)(2,1)}, u32[]{:S(2)}, u32[]{:S(2)}) %collective-permute-start.31) | collective-permute-done | bytes 307232 | tf_op jit(solution)/shard_map/ppermute | solution.py:1017
  260.8 8.0 %collective-permute-done.32 = bf16[1,1,48,3200]{3,2,1,0:T(8,128)(2,1)} collective-permute-done((bf16[1,1,48,3200]{3,2,1,0:T(8,128)(2,1)S(1)}, bf16[1,1,48,3200]{3,2,1,0:T(8,128)(2,1)}, u32[]{:S(2)}, u32[]{:S(2)}) %collective-permute-start.32) | collective-permute-done | bytes 307232 | tf_op jit(solution)/shard_map/ppermute | solution.py:1017
  273.9 2.9 %collective-permute-start.33 = (f32[2,48]{1,0:T(2,128)S(1)}, f32[2,48]{1,0:T(2,128)S(1)}, u32[]{:S(2)}, u32[]{:S(2)}) collective-permute-start(f32[2,48]{1,0:T(2,128)S(1)} %slice.76), channel_id=1, source_target_pairs={{0,1},{1,0},{2,3},{3,2},{4,5},{5,4},{6,7},{7,6},{8,9},{9,8},{10,11... | collective-permute-start | bytes 1160 | tf_op jit(solution)/shard_map/ppermute | solution.py:1100
  (171 shorter events, 59.8 us)
Async XLA Ops:
  0.6 28.9 %collective-permute-start.3 = (bf16[3,768,384]{2,1,0:T(8,128)(2,1)}, bf16[3,768,384]{2,1,0:T(8,128)(2,1)S(1)}, u32[]{:S(2)}, u32[]{:S(2)}) collective-permute-start(bf16[3,768,384]{2,1,0:T(8,128)(2,1)} %bitcast.135), channel_id=1, source_target_pairs={{0,1},{3,2},{4,5},{7,6},{8,9},{11,10},{12,13},{15,14},{16,17},{19,... | collective-permute-start | bytes 5308424 | tf_op jit(solution)/shard_map/ppermute | solution.py:928
  4.3 25.2 %all-to-all-start = ((bf16[16,2,16,768]{3,2,1,0:T(8,128)(2,1)}), bf16[16,2,16,768]{3,2,1,0:T(8,128)(2,1)S(1)}, u32[]{:S(2)}, u32[]{:S(2)}) async-start(bf16[16,2,16,768]{3,2,1,0:T(8,128)(2,1)} %copy_bitcast_fusion), calls=%async_computation | async-start | bytes 1572864 | tf_op jit(solution)/shard_map/all_to_all | solution.py:961
  10.6 36.8 %collective-permute-start.2 = (bf16[1024,768]{1,0:T(8,128)(2,1)}, bf16[1024,768]{1,0:T(8,128)(2,1)}, u32[]{:S(2)}, u32[]{:S(2)}) collective-permute-start(bf16[1024,768]{1,0:T(8,128)(2,1)} %param.17), channel_id=1, source_target_pairs={{0,2},{2,0},{4,6},{6,4},{8,10},{10,8},{12,14},{14,12},{16,18},{18,... | collective-permute-start | bytes 4718600 | tf_op jit(solution)/shard_map/ppermute | solution.py:919
  10.8 11.7 %collective-permute-start = (f32[2304]{0:T(1024)S(1)}, f32[2304]{0:T(1024)S(1)}, u32[]{:S(2)}, u32[]{:S(2)}) collective-permute-start(f32[2304]{0:T(1024)S(1)} %constant_dynamic-update-slice_fusion), channel_id=1, source_target_pairs={{0,1},{3,2},{4,5},{7,6},{8,9},{11,10},{12,13},{15,14},{16,17},{19,... | collective-permute-start | bytes 27656 | tf_op jit(solution)/shard_map/ppermute | solution.py:928
  10.9 18.1 %collective-permute-start.4 = (bf16[384,768]{1,0:T(8,128)(2,1)}, bf16[384,768]{1,0:T(8,128)(2,1)S(1)}, u32[]{:S(2)}, u32[]{:S(2)}) collective-permute-start(bf16[384,768]{1,0:T(8,128)(2,1)} %param.25), channel_id=1, source_target_pairs={{0,1},{3,2},{4,5},{7,6},{8,9},{11,10},{12,13},{15,14},{16,17},{19,... | collective-permute-start | bytes 1769480 | tf_op jit(solution)/shard_map/ppermute | solution.py:928
  11.2 34.6 %collective-permute-start.5 = (bf16[1024,768]{1,0:T(8,128)(2,1)}, bf16[1024,768]{1,0:T(8,128)(2,1)}, u32[]{:S(2)}, u32[]{:S(2)}) collective-permute-start(bf16[1024,768]{1,0:T(8,128)(2,1)} %param.33), channel_id=1, source_target_pairs={{0,2},{2,0},{4,6},{6,4},{8,10},{10,8},{12,14},{14,12},{16,18},{18,... | collective-permute-start | bytes 4718600 | tf_op jit(solution)/shard_map/ppermute | solution.py:919
  22.6 22.5 %collective-permute-start.7 = (bf16[768,768]{1,0:T(8,128)(2,1)}, bf16[768,768]{1,0:T(8,128)(2,1)}, u32[]{:S(2)}, u32[]{:S(2)}) collective-permute-start(bf16[768,768]{1,0:T(8,128)(2,1)} %dynamic-slice_bitcast_fusion), channel_id=1, source_target_pairs={{0,1},{3,2},{4,5},{7,6},{8,9},{11,10},{12,13},{15,14},{16,17},{19,... | collective-permute-start | bytes 3538952 | tf_op jit(solution)/shard_map/ppermute | solution.py:928
  31.8 26.0 %all-to-all-start.1 = ((bf16[32,16,768]{2,1,0:T(8,128)(2,1)}), bf16[32,16,768]{2,1,0:T(8,128)(2,1)}, u32[]{:S(2)}, u32[]{:S(2)}) async-start(bf16[32,16,768]{2,1,0:T(8,128)(2,1)} %copy-done.2), calls=%async_computation.1 | async-start | bytes 1572864 | tf_op jit(solution)/shard_map/all_to_all | solution.py:971
  45.1 18.3 %collective-permute-start.8 = (bf16[768,768]{1,0:T(8,128)(2,1)}, bf16[768,768]{1,0:T(8,128)(2,1)S(1)}, u32[]{:S(2)}, u32[]{:S(2)}) collective-permute-start(bf16[768,768]{1,0:T(8,128)(2,1)} %collective-permute-done.7.w_out_one), channel_id=1, source_target_pairs={{1,5},{2,6},{5,1},{6,2},{9,13},{10,14},{13,9},{14,10},{17,21},{18,... | collective-permute-start | bytes 3538952 | tf_op jit(solution)/shard_map/ppermute | solution.py:955
  59.3 27.4 %collective-permute-start.10 = (bf16[768,1536]{1,0:T(8,128)(2,1)}, bf16[768,1536]{1,0:T(8,128)(2,1)}, u32[]{:S(2)}, u32[]{:S(2)}) collective-permute-start(bf16[768,1536]{1,0:T(8,128)(2,1)} %param.29), channel_id=1, source_target_pairs={{0,1},{3,2},{4,5},{7,6},{8,9},{11,10},{12,13},{15,14},{16,17},{19,... | collective-permute-start | bytes 7077896 | tf_op jit(solution)/shard_map/ppermute | solution.py:928
  120.6 35.4 %collective-permute-start.12 = (bf16[384,1536]{1,0:T(8,128)(2,1)}, bf16[384,1536]{1,0:T(8,128)(2,1)}, u32[]{:S(2)}, u32[]{:S(2)}) collective-permute-start(bf16[384,1536]{1,0:T(8,128)(2,1)} %get-tuple-element.88), channel_id=1, source_target_pairs={{0,4},{2,6},{4,0},{6,2},{8,12},{10,14},{12,8},{14,10},{16,20},{18,... | collective-permute-start | bytes 3538952 | tf_op jit(solution)/shard_map/ppermute | solution.py:1000
  121.6 34.4 %collective-permute-start.13 = (bf16[384,1536]{1,0:T(8,128)(2,1)}, bf16[384,1536]{1,0:T(8,128)(2,1)}, u32[]{:S(2)}, u32[]{:S(2)}) collective-permute-start(bf16[384,1536]{1,0:T(8,128)(2,1)} %get-tuple-element.90), channel_id=1, source_target_pairs={{1,0},{2,3},{5,4},{6,7},{9,8},{10,11},{13,12},{14,15},{17,16},{18,... | collective-permute-start | bytes 3538952 | tf_op jit(solution)/shard_map/ppermute | solution.py:1031
  121.7 34.3 %collective-permute-start.14 = (bf16[384,1536]{1,0:T(8,128)(2,1)}, bf16[384,1536]{1,0:T(8,128)(2,1)}, u32[]{:S(2)}, u32[]{:S(2)}) collective-permute-start(bf16[384,1536]{1,0:T(8,128)(2,1)} %get-tuple-element.89), channel_id=1, source_target_pairs={{1,2},{2,1},{5,6},{6,5},{9,10},{10,9},{13,14},{14,13},{17,18},{18,... | collective-permute-start | bytes 3538952 | tf_op jit(solution)/shard_map/ppermute | solution.py:1032
  156.0 9.3 %collective-permute-start.15 = (bf16[1024,768]{1,0:T(8,128)(2,1)}, bf16[1024,768]{1,0:T(8,128)(2,1)}, u32[]{:S(2)}, u32[]{:S(2)}) collective-permute-start(bf16[1024,768]{1,0:T(8,128)(2,1)} %get-tuple-element.91.g_own), channel_id=1, source_target_pairs={{0,2},{2,0},{4,6},{6,4},{8,10},{10,8},{12,14},{14,12},{16,18},{18,... | collective-permute-start | bytes 4718600 | tf_op jit(solution)/shard_map/ppermute | solution.py:919
  163.2 19.8 %collective-permute-start.18 = (bf16[4,1,48,1536]{3,2,1,0:T(8,128)(2,1)}, bf16[4,1,48,1536]{3,2,1,0:T(8,128)(2,1)S(1)}, u32[]{:S(2)}, u32[]{:S(2)}) collective-permute-start(bf16[4,1,48,1536]{3,2,1,0:T(8,128)(2,1)} %get-tuple-element.172), channel_id=1, source_target_pairs={{1,0},{2,3},{5,4},{6,7},{9,8},{10,11},{13,12},{14,15},{17,16},{18,... | collective-permute-start | bytes 1769480 | tf_op jit(solution)/shard_map/ppermute | solution.py:1004
  163.2 19.8 %collective-permute-start.19 = (bf16[4,1,48,1536]{3,2,1,0:T(8,128)(2,1)}, bf16[4,1,48,1536]{3,2,1,0:T(8,128)(2,1)}, u32[]{:S(2)}, u32[]{:S(2)}) collective-permute-start(bf16[4,1,48,1536]{3,2,1,0:T(8,128)(2,1)} %get-tuple-element.171), channel_id=1, source_target_pairs={{1,2},{2,1},{5,6},{6,5},{9,10},{10,9},{13,14},{14,13},{17,18},{18,... | collective-permute-start | bytes 1769480 | tf_op jit(solution)/shard_map/ppermute | solution.py:1005
  164.9 34.8 %collective-permute-start.17 = (bf16[384,1664]{1,0:T(8,128)(2,1)}, bf16[384,1664]{1,0:T(8,128)(2,1)}, u32[]{:S(2)}, u32[]{:S(2)}) collective-permute-start(bf16[384,1664]{1,0:T(8,128)(2,1)} %get-tuple-element.96), channel_id=1, source_target_pairs={{0,4},{2,6},{4,0},{6,2},{8,12},{10,14},{12,8},{14,10},{16,20},{18,... | collective-permute-start | bytes 3833864 | tf_op jit(solution)/shard_map/ppermute | solution.py:1000
  174.3 40.8 %all-to-all-start.2 = ((bf16[32,16,768]{2,1,0:T(8,128)(2,1)}), bf16[32,16,768]{2,1,0:T(8,128)(2,1)S(1)}, u32[]{:S(2)}, u32[]{:S(2)}) async-start(bf16[32,16,768]{2,1,0:T(8,128)(2,1)} %bitcast.19), calls=%async_computation.2 | async-start | bytes 1572864 | tf_op jit(solution)/shard_map/all_to_all | solution.py:1054
  184.4 24.2 %collective-permute-start.22 = (bf16[1,1,48,1536]{3,2,1,0:T(8,128)(2,1)S(1)}, bf16[1,1,48,1536]{3,2,1,0:T(8,128)(2,1)S(1)}, u32[]{:S(2)}, u32[]{:S(2)}) collective-permute-start(bf16[1,1,48,1536]{3,2,1,0:T(8,128)(2,1)S(1)} %get-tuple-element.181), channel_id=1, source_target_pairs={{0,8},{2,10},{4,12},{6,14},{8,0},{10,2},{12,4},{14,6},{16,24},{18,... | collective-permute-start | bytes 442376 | tf_op jit(solution)/shard_map/ppermute | solution.py:1017
  184.7 25.4 %collective-permute-start.23 = (bf16[1,1,48,1536]{3,2,1,0:T(8,128)(2,1)S(1)}, bf16[1,1,48,1536]{3,2,1,0:T(8,128)(2,1)S(1)}, u32[]{:S(2)}, u32[]{:S(2)}) collective-permute-start(bf16[1,1,48,1536]{3,2,1,0:T(8,128)(2,1)S(1)} %get-tuple-element.180), channel_id=1, source_target_pairs={{0,16},{2,18},{4,20},{6,22},{8,24},{10,26},{12,28},{14,30},{16,0},... | collective-permute-start | bytes 442376 | tf_op jit(solution)/shard_map/ppermute | solution.py:1017
  187.4 27.7 %collective-permute-start.24 = (bf16[1,1,48,1536]{3,2,1,0:T(8,128)(2,1)S(1)}, bf16[1,1,48,1536]{3,2,1,0:T(8,128)(2,1)S(1)}, u32[]{:S(2)}, u32[]{:S(2)}) collective-permute-start(bf16[1,1,48,1536]{3,2,1,0:T(8,128)(2,1)S(1)} %get-tuple-element.179), channel_id=1, source_target_pairs={{0,24},{2,26},{4,28},{6,30},{8,16},{10,18},{12,20},{14,22},{16,8},... | collective-permute-start | bytes 442376 | tf_op jit(solution)/shard_map/ppermute | solution.py:1017
  200.8 22.0 %collective-permute-start.26 = (bf16[4,1,48,1536]{3,2,0,1:T(8,128)(2,1)}, bf16[4,1,48,1536]{3,2,0,1:T(8,128)(2,1)}, u32[]{:S(2)}, u32[]{:S(2)}) collective-permute-start(bf16[4,1,48,1536]{3,2,0,1:T(8,128)(2,1)} %get-tuple-element.169), channel_id=1, source_target_pairs={{0,4},{2,6},{4,0},{6,2},{8,12},{10,14},{12,8},{14,10},{16,20},{18,... | collective-permute-start | bytes 1769480 | tf_op jit(solution)/shard_map/ppermute | solution.py:1000
  204.0 21.7 %collective-permute-start.28 = (bf16[4,1,48,1664]{3,2,0,1:T(8,128)(2,1)}, bf16[4,1,48,1664]{3,2,0,1:T(8,128)(2,1)}, u32[]{:S(2)}, u32[]{:S(2)}) collective-permute-start(bf16[4,1,48,1664]{3,2,0,1:T(8,128)(2,1)} %get-tuple-element.165), channel_id=1, source_target_pairs={{1,0},{2,3},{5,4},{6,7},{9,8},{10,11},{13,12},{14,15},{17,16},{18,... | collective-permute-start | bytes 1916936 | tf_op jit(solution)/shard_map/ppermute | solution.py:1004
  208.5 17.2 %collective-permute-start.29 = (bf16[4,1,48,1664]{3,2,0,1:T(8,128)(2,1)}, bf16[4,1,48,1664]{3,2,0,1:T(8,128)(2,1)}, u32[]{:S(2)}, u32[]{:S(2)}) collective-permute-start(bf16[4,1,48,1664]{3,2,0,1:T(8,128)(2,1)} %get-tuple-element.164), channel_id=1, source_target_pairs={{1,2},{2,1},{5,6},{6,5},{9,10},{10,9},{13,14},{14,13},{17,18},{18,... | collective-permute-start | bytes 1916936 | tf_op jit(solution)/shard_map/ppermute | solution.py:1005
  210.0 17.2 %collective-permute-start.16 = (bf16[1024,768]{1,0:T(8,128)(2,1)}, bf16[1024,768]{1,0:T(8,128)(2,1)}, u32[]{:S(2)}, u32[]{:S(2)}) collective-permute-start(bf16[1024,768]{1,0:T(8,128)(2,1)} %get-tuple-element.94), channel_id=1, source_target_pairs={{0,2},{2,0},{4,6},{6,4},{8,10},{10,8},{12,14},{14,12},{16,18},{18,... | collective-permute-start | bytes 4718600 | tf_op jit(solution)/shard_map/ppermute | solution.py:919
  218.3 23.6 %all-to-all-start.3 = ((bf16[16,2,16,768]{3,2,1,0:T(8,128)(2,1)}), bf16[16,2,16,768]{3,2,1,0:T(8,128)(2,1)}, u32[]{:S(2)}, u32[]{:S(2)}) async-start(bf16[16,2,16,768]{3,2,1,0:T(8,128)(2,1)} %bitcast.30), calls=%async_computation.3 | async-start | bytes 1572864 | tf_op jit(solution)/shard_map/all_to_all | solution.py:1074
  222.8 11.8 %collective-permute-start.21 = (bf16[512,768]{1,0:T(8,128)(2,1)}, bf16[512,768]{1,0:T(8,128)(2,1)}, u32[]{:S(2)}, u32[]{:S(2)}) collective-permute-start(bf16[512,768]{1,0:T(8,128)(2,1)} %dynamic-slice_bitcast_fusion.1), channel_id=1, source_target_pairs={{0,1},{3,2},{4,5},{7,6},{8,9},{11,10},{12,13},{15,14},{16,17},{19,... | collective-permute-start | bytes 2359304 | tf_op jit(solution)/shard_map/ppermute | solution.py:928
  229.8 40.2 %collective-permute-start.20 = (bf16[1024,768]{1,0:T(8,128)(2,1)S(1)}, bf16[1024,768]{1,0:T(8,128)(2,1)}, u32[]{:S(2)}, u32[]{:S(2)}) collective-permute-start(bf16[1024,768]{1,0:T(8,128)(2,1)S(1)} %add_convert_fusion), channel_id=1, source_target_pairs={{0,1},{3,2},{4,5},{7,6},{8,9},{11,10},{12,13},{15,14},{16,17},{19,... | collective-permute-start | bytes 4718600 | tf_op jit(solution)/shard_map/ppermute | solution.py:928
  231.1 15.4 %collective-permute-start.30 = (bf16[1,1,48,3200]{3,2,1,0:T(8,128)(2,1)}, bf16[1,1,48,3200]{3,2,1,0:T(8,128)(2,1)S(1)}, u32[]{:S(2)}, u32[]{:S(2)}) collective-permute-start(bf16[1,1,48,3200]{3,2,1,0:T(8,128)(2,1)} %get-tuple-element.167), channel_id=1, source_target_pairs={{0,8},{2,10},{4,12},{6,14},{8,0},{10,2},{12,4},{14,6},{16,24},{18,... | collective-permute-start | bytes 921608 | tf_op jit(solution)/shard_map/ppermute | solution.py:1017
  231.3 29.5 %collective-permute-start.31 = (bf16[1,1,48,3200]{3,2,1,0:T(8,128)(2,1)}, bf16[1,1,48,3200]{3,2,1,0:T(8,128)(2,1)}, u32[]{:S(2)}, u32[]{:S(2)}) collective-permute-start(bf16[1,1,48,3200]{3,2,1,0:T(8,128)(2,1)} %get-tuple-element.168), channel_id=1, source_target_pairs={{0,16},{2,18},{4,20},{6,22},{8,24},{10,26},{12,28},{14,30},{16,0},... | collective-permute-start | bytes 921608 | tf_op jit(solution)/shard_map/ppermute | solution.py:1017
  233.9 35.0 %collective-permute-start.32 = (bf16[1,1,48,3200]{3,2,1,0:T(8,128)(2,1)S(1)}, bf16[1,1,48,3200]{3,2,1,0:T(8,128)(2,1)}, u32[]{:S(2)}, u32[]{:S(2)}) collective-permute-start(bf16[1,1,48,3200]{3,2,1,0:T(8,128)(2,1)S(1)} %get-tuple-element.166), channel_id=1, source_target_pairs={{0,24},{2,26},{4,28},{6,30},{8,16},{10,18},{12,20},{14,22},{16,8},... | collective-permute-start | bytes 921608 | tf_op jit(solution)/shard_map/ppermute | solution.py:1017
  243.9 27.6 %collective-permute-start.25 = (bf16[512,768]{1,0:T(8,128)(2,1)S(1)}, bf16[512,768]{1,0:T(8,128)(2,1)S(1)}, u32[]{:S(2)}, u32[]{:S(2)}) collective-permute-start(bf16[512,768]{1,0:T(8,128)(2,1)S(1)} %fusion), channel_id=1, source_target_pairs={{0,1},{1,0},{2,3},{3,2},{4,5},{5,4},{6,7},{7,6},{8,9},{9,8},{10,11... | collective-permute-start | bytes 2359304 | tf_op jit(solution)/shard_map/ppermute | solution.py:1081
  (31 other events, 160.0 us)
where the time goes:
time: 281 us; the launch traced here: 280 us
  Pallas kernels  89.8 us (32%)
  waiting for transfers between devices  70.5 us (25%)
  starting transfers between devices  65.5 us (23%)
  local copies, waits for them, and re-layouts  26.2 us (9%)
  other arithmetic  26.1 us (9%)
    pallas_call x1, Pallas kernels, attention_back(): pl.pallas_call(functools.partial(attention_back_kernel, lead_rows, part_r...  30.1 us
    pallas_call x1, Pallas kernels, feed(): pl.pallas_call(functools.partial(feed_kernel, in_rows, out_rows), out_sha...  30 us
    ppermute x6, waiting for transfers between devices, far(): lax.ppermute(taken(value, spot ^ flip, 2), 'dp', [(d, d ^ flip << shift)...  25.5 us
    pallas_call x1, Pallas kernels, attention(): pl.pallas_call(attention_kernel, out_shape=(shape((rows, width), F32), ta...  20.7 us
    ppermute x7, waiting for transfers between devices, half_weight(): return lax.ppermute(value, both, weight_move)  16.2 us
    ppermute x3, waiting for transfers between devices, send_across(): return lax.ppermute(value, 'dp', [(d, d ^ 1 << lead) for d in all_dp])  9.59 us
    ppermute x9, starting transfers between devices, swap(): return lax.ppermute(value, 'dp', core_swap)  9.05 us
    all_to_all x1, waiting for transfers between devices, shards(): lax.all_to_all(chosen, both, 0, 0, tiled=True).reshape(rows // 2, width)  8.83 us
  transfers between devices with their start and end apart: 38, of which 12 were waited for; matrix products, arithmetic and copies ran while one was open for 16% of the time, Pallas kernels for 21%

commit v1 on v0

--- a/solution.py
+++ b/solution.py
@@ -1058,39 +1058,31 @@
     out_oth = swap(after(out_part, leaving))
     out_value = total(*after(out_first, in_value)).astype(BF16)
     out_terms = send_second(out_value)
-    attn_value = total(*after(attn_first, out_value)).astype(BF16)
-    attn_terms = send_pair(attn_value)
-    block = hidden + (out_part.astype(F32) + after(out_oth, attn_value).astype(F32)) + out_bias
+    block = hidden + (out_part.astype(F32) + after(out_oth, out_value).astype(F32)) + out_bias
     block = block.astype(BF16)
     kept = kept.reshape(2, rows // 2, width)
-    kept_got = half_weight(taken(kept, 1 - mp, 0))
+    kept_away = taken(kept, 1 - mp, 0)
+    kept_got = half_weight(kept_away)
     block_got = half_weight(block)
 
-    def side_by_side(*groups):
-        values = [total(*terms).reshape(high * mid, part_rows, -1) for terms in groups]
-        return jnp.concatenate(values, axis=2).astype(BF16)
-
-    returning = pick(back, wanted_back, attn_value, sum_in)
+    returning = pick(back, wanted_back, sum_in, block, kept_got)
     returned = lax.all_to_all(
         returning.reshape(dp_count, 2, piece, width), "dp", 0, 0, tiled=True
     )
-    returned = after(returned, kept_got)
+    returned = after(returned, kept_got, block_got)
     kept = jnp.where(home, taken(kept, mp, 0), kept_got)
     returned = returned.transpose(1, 0, 2, 3).reshape(rows // 2, width)
     mine = (kept.astype(F32) + returned.astype(F32)).astype(BF16)
     other = lax.ppermute(mine, "mp", [(0, 1), (1, 0)])
-    block_out = jnp.where(home, block, after(block_got, mine))
+    block_out = jnp.where(home, block, block_got)
     grad_tokens = jnp.where(
         jnp.arange(2)[:, None, None] == mp, mine[None], other[None]
     ).reshape(rows, width)
 
     marker = swap(returning[0, :, :LANES])
-    summed = far(
-        side_by_side(*(after(terms, marker) for terms in (out_terms, attn_terms))),
-        mine,
-    )
-    summed = after(summed, other)
-    sum_out, sum_attn = summed[:, :units], summed[:, units:]
+    attn_terms = send_pair(total(*after(attn_first, marker)).astype(BF16))
+    sum_out = far(total(*after(out_terms, marker)), mine)
+    sum_attn = after(far(total(*after(attn_terms, mine))), other)
     sum_qkv = sum_attn[:, : 3 * local].reshape(-1, 3, local)
     sum_proj = sum_attn[:, 3 * local : 4 * local].T
     quarter, eighth = local // dp_count, units // dp_count

time: 281 us -> 282 us (level)
  waiting for transfers between devices: 70.5 us -> 74.2 us
    ppermute x7, waiting for transfers between devices: 16.2 us -> 26.5 us  [half_weight(): return lax.ppermute(value, both, weight_move)]
    ppermute x6 -> x9, waiting for transfers between devices: 25.5 us -> 35.2 us  [far(): lax.ppermute(taken(value, spot ^ flip, 2), 'dp', [(d, d ^ flip << shift)...]
    ppermute x3, waiting for transfers between devices: 9.59 us -> 0.01 us  [send_across(): return lax.ppermute(value, 'dp', [(d, d ^ 1 << lead) for d in all_dp])]
    all_to_all x1, waiting for transfers between devices: 7.22 us -> 0.01 us  [shards(): lax.all_to_all(returning.reshape(dp_count, 2, piece, width), 'dp', 0, 0,...]
    ppermute x6 -> x9, starting transfers between devices: 7.04 us -> 12.3 us  [far(): lax.ppermute(taken(value, spot ^ flip, 2), 'dp', [(d, d ^ flip << shift)...]
    ppermute x2, starting transfers between devices: 3.57 us -> 0.2 us  [send_pair(): lax.ppermute(taken(value, jnp.where(home, 1 - core, core), 2), both, pair...]
    convert_element_type x1 -> x3, other arithmetic: 1.64 us -> 4.72 us  [the longest x2 2.73 us: far(): value = value.reshape((-1, left, radix) + value.shape[-2:]).astype(BF16)]
    reshape x2 -> x0, other arithmetic: 2.93 us -> none  [side_by_side(): total(*terms).reshape(high * mid, part_rows, -1)]
  transfers between devices with their start and end apart: 38 -> 41, of which waited for: 12 -> 16; matrix products, arithmetic and copies ran while one was open for 16% -> 15% of each run, Pallas kernels for 21% -> 21%
where the time goes in v1:
time: 282 us; the launch traced here: 280 us
  Pallas kernels  88.7 us (31%)
  waiting for transfers between devices  74.2 us (26%)
  starting transfers between devices  65.4 us (23%)
  local copies, waits for them, and re-layouts  26.5 us (9%)
  other arithmetic  23.7 us (8%)
    ppermute x9, waiting for transfers between devices, far(): lax.ppermute(taken(value, spot ^ flip, 2), 'dp', [(d, d ^ flip << shift)...  35.2 us
    pallas_call x1, Pallas kernels, feed(): pl.pallas_call(functools.partial(feed_kernel, in_rows, out_rows), out_sha...  29.9 us
    pallas_call x1, Pallas kernels, attention_back(): pl.pallas_call(functools.partial(attention_back_kernel, lead_rows, part_r...  29.3 us
    ppermute x7, waiting for transfers between devices, half_weight(): return lax.ppermute(value, both, weight_move)  26.5 us
    pallas_call x1, Pallas kernels, attention(): pl.pallas_call(attention_kernel, out_shape=(shape((rows, width), F32), ta...  20.6 us
    ppermute x9, starting transfers between devices, far(): lax.ppermute(taken(value, spot ^ flip, 2), 'dp', [(d, d ^ flip << shift)...  12.3 us
    all_to_all x1, starting transfers between devices, shards(): back = lax.all_to_all(leaving, both, 0, 0, tiled=True)  8.73 us
    all_to_all x1, waiting for transfers between devices, shards(): lax.all_to_all(chosen, both, 0, 0, tiled=True).reshape(rows // 2, width)  8.52 us
  transfers between devices with their start and end apart: 41, of which 16 were waited for; matrix products, arithmetic and copies ran while one was open for 15% of the time, Pallas kernels for 21%

profile of v1, /device:TPU:8, one launch (start us, length us, event | category | flops | bytes accessed | tf_op | source)
XLA Modules:
  0.0 280.4 jit_solution(15166726132004920893)
XLA Ops:
  2.2 2.1 copy_bitcast_fusion
  4.3 6.3 %all-to-all-start = ((bf16[16,2,16,768]{3,2,1,0:T(8,128)(2,1)}), bf16[16,2,16,768]{3,2,1,0:T(8,128)(2,1)S(1)}, u32[]{:S(2)}, u32[]{:S(2)}) async-start(bf16[16,2,16,768]{3,2,1,0:T(8,128)(2,1)} %copy_bitcast_fusion), calls=%async_computation | async-start | bytes 1572864 | tf_op jit(solution)/shard_map/all_to_all | solution.py:961
  11.4 2.4 dynamic-slice_bitcast_fusion
  14.5 8.1 %collective-permute-done = f32[2304]{0:T(1024)S(1)} collective-permute-done((f32[2304]{0:T(1024)S(1)}, f32[2304]{0:T(1024)S(1)}, u32[]{:S(2)}, u32[]{:S(2)}) %collective-permute-start) | collective-permute-done | bytes 9248 | tf_op jit(solution)/shard_map/ppermute | solution.py:928
  22.6 2.5 collective-permute-start.7
  25.1 3.9 %collective-permute-done.4.refs_1_.wp = bf16[384,768]{1,0:T(8,128)(2,1)S(1)} collective-permute-done((bf16[384,768]{1,0:T(8,128)(2,1)}, bf16[384,768]{1,0:T(8,128)(2,1)S(1)}, u32[]{:S(2)}, u32[]{:S(2)}) %collective-permute-start.4) | collective-permute-done | bytes 589856 | tf_op jit(solution)/shard_map/ppermute | solution.py:928
  31.6 6.6 %all-to-all-start.1 = ((bf16[32,16,768]{2,1,0:T(8,128)(2,1)}), bf16[32,16,768]{2,1,0:T(8,128)(2,1)}, u32[]{:S(2)}, u32[]{:S(2)}) async-start(bf16[32,16,768]{2,1,0:T(8,128)(2,1)} %copy-done.2), calls=%async_computation.1 | async-start | bytes 1572864 | tf_op jit(solution)/shard_map/all_to_all | solution.py:971
  41.4 3.8 %collective-permute-done.7.w_out_one = bf16[768,768]{1,0:T(8,128)(2,1)} collective-permute-done((bf16[768,768]{1,0:T(8,128)(2,1)}, bf16[768,768]{1,0:T(8,128)(2,1)}, u32[]{:S(2)}, u32[]{:S(2)}) %collective-permute-start.7) | collective-permute-done | bytes 1179680 | tf_op jit(solution)/shard_map/ppermute | solution.py:928
  49.1 8.5 %all-to-all-done.1 = bf16[32,16,768]{2,1,0:T(8,128)(2,1)} async-done(((bf16[32,16,768]{2,1,0:T(8,128)(2,1)}), bf16[32,16,768]{2,1,0:T(8,128)(2,1)}, u32[]{:S(2)}, u32[]{:S(2)}) %all-to-all-start.1) | async-done | bytes 786464 | tf_op jit(solution)/shard_map/all_to_all | solution.py:971
  64.3 20.6 %attention.1 = (f32[1024,768]{1,0:T(8,128)}, bf16[1024,768]{1,0:T(8,128)(2,1)}, bf16[1024,768]{1,0:T(8,128)(2,1)}, f32[1024,128]{1,0:T(8,128)}, bf16[1024,384]{1...) custom-call(f32[1]{0:T(128)} %slice.85.blend, ...), custom_call_target="tpu_custom_call" | custom-call | flops 1048576 | bytes 1048576 | tf_op jit(solution)/shard_map/attention/pallas_call | solution.py:277
  86.6 2.6 collective-permute-done.9.p_oth
  90.4 29.9 %feed.1 = (f32[1024,768]{1,0:T(8,128)}, bf16[1024,768]{1,0:T(8,128)(2,1)}, bf16[1024,768]{1,0:T(8,128)(2,1)}, bf16[384,1536]{1,0:T(8,128)(2,1)}, bf16[384,1536]{...) custom-call(s32[3]{0:T(128)} %pad_add_fusion.flags, ...), custom_call_target="tpu_custom_call" | custom-call | flops 1048576 | bytes 1048576 | tf_op jit(solution)/shard_map/feed/pallas_call | solution.py:486
  126.0 29.3 %attention_back.1 = (f32[1024,768]{1,0:T(8,128)}, bf16[1024,768]{1,0:T(8,128)(2,1)}, bf16[384,1664]{1,0:T(8,128)(2,1)}, bf16[384,1664]{1,0:T(8,128)(2,1)}, f32[9,768]{1,0:T(8,128)}) custom-call(s32[3]{0:T(128)} %pad_add_fusion.flags, f32[5,768]{1,0:T(8,128)} %stack.46.vecs, f32[1,1024]{1,0:T(1,128)} %bitcast.120, f32[6,1024]{1,0:T(8,128)} %get-tuple-element.76.lse, ...), custom_call_target="tpu_custom_call" | custom-call | flops 1048576 | bytes 1048576 | tf_op jit(solution)/shard_map/attention_back/pallas_call | solution.py:775
  155.3 3.8 %collective-permute-start.15 = (bf16[1024,768]{1,0:T(8,128)(2,1)}, bf16[1024,768]{1,0:T(8,128)(2,1)}, u32[]{:S(2)}, u32[]{:S(2)}) collective-permute-start(bf16[1024,768]{1,0:T(8,128)(2,1)} %get-tuple-element.93.g_own), channel_id=1, source_target_pairs={{0,2},{2,0},{4,6},{6,4},{8,10},{10,8},{12,14},{14,12},{16,18},{18,... | collective-permute-start | bytes 4718600 | tf_op jit(solution)/shard_map/ppermute | solution.py:919
  159.1 1.9 add_convert_fusion.3
  164.7 6.9 %mixed_back.1 = (bf16[1024,768]{1,0:T(8,128)(2,1)}, bf16[1024,768]{1,0:T(8,128)(2,1)}) custom-call(f32[1]{0:T(128)} %slice.85.blend, f32[5,768]{1,0:T(8,128)} %stack.46.vecs, f32[1024,768]{1,0:T(8,128)} %get-tuple-element.88.gh, bf16[1024,768]{1,0:T(8,128)(2,1)} %get-tuple-element.93.g_own, bf16[1024,768]{1,0:T(8,128)(2,1)} %collective-permute-done.15.g_oth, ...), custom_call_target="tpu_custom_call" | custom-call | flops 1048576 | bytes 1048576 | tf_op jit(solution)/shard_map/mixed_back/pallas_call | solution.py:862
  173.8 8.7 %all-to-all-start.2 = ((bf16[32,16,768]{2,1,0:T(8,128)(2,1)}), bf16[32,16,768]{2,1,0:T(8,128)(2,1)S(1)}, u32[]{:S(2)}, u32[]{:S(2)}) async-start(bf16[32,16,768]{2,1,0:T(8,128)(2,1)} %bitcast.19), calls=%async_computation.2 | async-start | bytes 1572864 | tf_op jit(solution)/shard_map/all_to_all | solution.py:1054
  184.7 2.6 collective-permute-start.22
  187.8 2.2 add_convert_fusion.2
  191.2 8.9 %collective-permute-done.21 = bf16[1,1,48,1536]{3,2,1,0:T(8,128)(2,1)S(1)} collective-permute-done((bf16[1,1,48,1536]{3,2,1,0:T(8,128)(2,1)S(1)}, bf16[1,1,48,1536]{3,2,1,0:T(8,128)(2,1)S(1)}, u32[]{:S(2)}, u32[]{:S(2)}) %collective-permute-start.21) | collective-permute-done | bytes 147488 | tf_op jit(solution)/shard_map/ppermute | solution.py:1017
  200.0 1.8 collective-permute-start.20
  201.9 7.6 %collective-permute-done.22 = bf16[1,1,48,1536]{3,2,1,0:T(8,128)(2,1)S(1)} collective-permute-done((bf16[1,1,48,1536]{3,2,1,0:T(8,128)(2,1)S(1)}, bf16[1,1,48,1536]{3,2,1,0:T(8,128)(2,1)S(1)}, u32[]{:S(2)}, u32[]{:S(2)}) %collective-permute-start.22) | collective-permute-done | bytes 147488 | tf_op jit(solution)/shard_map/ppermute | solution.py:1017
  211.0 3.6 %collective-permute-done.23 = bf16[1,1,48,1536]{3,2,1,0:T(8,128)(2,1)S(1)} collective-permute-done((bf16[1,1,48,1536]{3,2,1,0:T(8,128)(2,1)S(1)}, bf16[1,1,48,1536]{3,2,1,0:T(8,128)(2,1)S(1)}, u32[]{:S(2)}, u32[]{:S(2)}) %collective-permute-start.23) | collective-permute-done | bytes 147488 | tf_op jit(solution)/shard_map/ppermute | solution.py:1017
  219.1 4.3 %all-to-all-start.3 = ((bf16[16,2,16,768]{3,2,1,0:T(8,128)(2,1)}), bf16[16,2,16,768]{3,2,1,0:T(8,128)(2,1)S(1)}, u32[]{:S(2)}, u32[]{:S(2)}) async-start(bf16[16,2,16,768]{3,2,1,0:T(8,128)(2,1)} %bitcast.30), calls=%async_computation.3 | async-start | bytes 1572864 | tf_op jit(solution)/shard_map/all_to_all | solution.py:1069
  223.4 2.0 add_convert_fusion.1
  231.2 5.2 %collective-permute-start.34 = (bf16[1,1,48,1536]{3,2,1,0:T(8,128)(2,1)}, bf16[1,1,48,1536]{3,2,1,0:T(8,128)(2,1)S(1)}, u32[]{:S(2)}, u32[]{:S(2)}) collective-permute-start(bf16[1,1,48,1536]{3,2,1,0:T(8,128)(2,1)} %get-tuple-element.179), channel_id=1, source_target_pairs={{0,8},{2,10},{4,12},{6,14},{8,0},{10,2},{12,4},{14,6},{16,24},{18,... | collective-permute-start | bytes 442376 | tf_op jit(solution)/shard_map/ppermute | solution.py:1017
  236.4 10.1 %collective-permute-done.19 = bf16[1024,768]{1,0:T(8,128)(2,1)} collective-permute-done((bf16[1024,768]{1,0:T(8,128)(2,1)S(1)}, bf16[1024,768]{1,0:T(8,128)(2,1)}, u32[]{:S(2)}, u32[]{:S(2)}) %collective-permute-start.19) | collective-permute-done | bytes 1572896 | tf_op jit(solution)/shard_map/ppermute | solution.py:928
  248.5 2.7 collective-permute-start.24
  251.1 4.6 %collective-permute-done.36 = bf16[1,1,48,1536]{3,2,1,0:T(8,128)(2,1)} collective-permute-done((bf16[1,1,48,1536]{3,2,1,0:T(8,128)(2,1)}, bf16[1,1,48,1536]{3,2,1,0:T(8,128)(2,1)}, u32[]{:S(2)}, u32[]{:S(2)}) %collective-permute-start.36) | collective-permute-done | bytes 147488 | tf_op jit(solution)/shard_map/ppermute | solution.py:1017
  257.4 2.0 collective-permute-start.30
  264.4 6.4 %collective-permute-done.30 = bf16[1,1,48,1664]{3,2,1,0:T(8,128)(2,1)S(1)} collective-permute-done((bf16[1,1,48,1664]{3,2,1,0:T(8,128)(2,1)S(1)}, bf16[1,1,48,1664]{3,2,1,0:T(8,128)(2,1)S(1)}, u32[]{:S(2)}, u32[]{:S(2)}) %collective-permute-start.30) | collective-permute-done | bytes 159776 | tf_op jit(solution)/shard_map/ppermute | solution.py:1017
  270.8 3.7 %collective-permute-done.31 = bf16[1,1,48,1664]{3,2,1,0:T(8,128)(2,1)S(1)} collective-permute-done((bf16[1,1,48,1664]{3,2,1,0:T(8,128)(2,1)S(1)}, bf16[1,1,48,1664]{3,2,1,0:T(8,128)(2,1)S(1)}, u32[]{:S(2)}, u32[]{:S(2)}) %collective-permute-start.31) | collective-permute-done | bytes 159776 | tf_op jit(solution)/shard_map/ppermute | solution.py:1017
  (183 shorter events, 63.2 us)
Async XLA Ops:
  0.6 28.9 %collective-permute-start.3 = (bf16[3,768,384]{2,1,0:T(8,128)(2,1)}, bf16[3,768,384]{2,1,0:T(8,128)(2,1)S(1)}, u32[]{:S(2)}, u32[]{:S(2)}) collective-permute-start(bf16[3,768,384]{2,1,0:T(8,128)(2,1)} %bitcast.122), channel_id=1, source_target_pairs={{0,1},{3,2},{4,5},{7,6},{8,9},{11,10},{12,13},{15,14},{16,17},{19,... | collective-permute-start | bytes 5308424 | tf_op jit(solution)/shard_map/ppermute | solution.py:928
  4.3 25.2 %all-to-all-start = ((bf16[16,2,16,768]{3,2,1,0:T(8,128)(2,1)}), bf16[16,2,16,768]{3,2,1,0:T(8,128)(2,1)S(1)}, u32[]{:S(2)}, u32[]{:S(2)}) async-start(bf16[16,2,16,768]{3,2,1,0:T(8,128)(2,1)} %copy_bitcast_fusion), calls=%async_computation | async-start | bytes 1572864 | tf_op jit(solution)/shard_map/all_to_all | solution.py:961
  10.6 37.0 %collective-permute-start.2 = (bf16[1024,768]{1,0:T(8,128)(2,1)}, bf16[1024,768]{1,0:T(8,128)(2,1)}, u32[]{:S(2)}, u32[]{:S(2)}) collective-permute-start(bf16[1024,768]{1,0:T(8,128)(2,1)} %param.17), channel_id=1, source_target_pairs={{0,2},{2,0},{4,6},{6,4},{8,10},{10,8},{12,14},{14,12},{16,18},{18,... | collective-permute-start | bytes 4718600 | tf_op jit(solution)/shard_map/ppermute | solution.py:919
  10.8 11.7 %collective-permute-start = (f32[2304]{0:T(1024)S(1)}, f32[2304]{0:T(1024)S(1)}, u32[]{:S(2)}, u32[]{:S(2)}) collective-permute-start(f32[2304]{0:T(1024)S(1)} %constant_dynamic-update-slice_fusion), channel_id=1, source_target_pairs={{0,1},{3,2},{4,5},{7,6},{8,9},{11,10},{12,13},{15,14},{16,17},{19,... | collective-permute-start | bytes 27656 | tf_op jit(solution)/shard_map/ppermute | solution.py:928
  10.9 18.1 %collective-permute-start.4 = (bf16[384,768]{1,0:T(8,128)(2,1)}, bf16[384,768]{1,0:T(8,128)(2,1)S(1)}, u32[]{:S(2)}, u32[]{:S(2)}) collective-permute-start(bf16[384,768]{1,0:T(8,128)(2,1)} %param.25), channel_id=1, source_target_pairs={{0,1},{3,2},{4,5},{7,6},{8,9},{11,10},{12,13},{15,14},{16,17},{19,... | collective-permute-start | bytes 1769480 | tf_op jit(solution)/shard_map/ppermute | solution.py:928
  11.2 34.7 %collective-permute-start.5 = (bf16[1024,768]{1,0:T(8,128)(2,1)}, bf16[1024,768]{1,0:T(8,128)(2,1)}, u32[]{:S(2)}, u32[]{:S(2)}) collective-permute-start(bf16[1024,768]{1,0:T(8,128)(2,1)} %param.33), channel_id=1, source_target_pairs={{0,2},{2,0},{4,6},{6,4},{8,10},{10,8},{12,14},{14,12},{16,18},{18,... | collective-permute-start | bytes 4718600 | tf_op jit(solution)/shard_map/ppermute | solution.py:919
  22.6 22.7 %collective-permute-start.7 = (bf16[768,768]{1,0:T(8,128)(2,1)}, bf16[768,768]{1,0:T(8,128)(2,1)}, u32[]{:S(2)}, u32[]{:S(2)}) collective-permute-start(bf16[768,768]{1,0:T(8,128)(2,1)} %dynamic-slice_bitcast_fusion), channel_id=1, source_target_pairs={{0,1},{3,2},{4,5},{7,6},{8,9},{11,10},{12,13},{15,14},{16,17},{19,... | collective-permute-start | bytes 3538952 | tf_op jit(solution)/shard_map/ppermute | solution.py:928
  31.6 26.0 %all-to-all-start.1 = ((bf16[32,16,768]{2,1,0:T(8,128)(2,1)}), bf16[32,16,768]{2,1,0:T(8,128)(2,1)}, u32[]{:S(2)}, u32[]{:S(2)}) async-start(bf16[32,16,768]{2,1,0:T(8,128)(2,1)} %copy-done.2), calls=%async_computation.1 | async-start | bytes 1572864 | tf_op jit(solution)/shard_map/all_to_all | solution.py:971
  45.2 18.1 %collective-permute-start.8 = (bf16[768,768]{1,0:T(8,128)(2,1)}, bf16[768,768]{1,0:T(8,128)(2,1)S(1)}, u32[]{:S(2)}, u32[]{:S(2)}) collective-permute-start(bf16[768,768]{1,0:T(8,128)(2,1)} %collective-permute-done.7.w_out_one), channel_id=1, source_target_pairs={{1,5},{2,6},{5,1},{6,2},{9,13},{10,14},{13,9},{14,10},{17,21},{18,... | collective-permute-start | bytes 3538952 | tf_op jit(solution)/shard_map/ppermute | solution.py:955
  59.2 27.4 %collective-permute-start.10 = (bf16[768,1536]{1,0:T(8,128)(2,1)}, bf16[768,1536]{1,0:T(8,128)(2,1)}, u32[]{:S(2)}, u32[]{:S(2)}) collective-permute-start(bf16[768,1536]{1,0:T(8,128)(2,1)} %param.29), channel_id=1, source_target_pairs={{0,1},{3,2},{4,5},{7,6},{8,9},{11,10},{12,13},{15,14},{16,17},{19,... | collective-permute-start | bytes 7077896 | tf_op jit(solution)/shard_map/ppermute | solution.py:928
  120.3 34.9 %collective-permute-start.12 = (bf16[384,1536]{1,0:T(8,128)(2,1)}, bf16[384,1536]{1,0:T(8,128)(2,1)}, u32[]{:S(2)}, u32[]{:S(2)}) collective-permute-start(bf16[384,1536]{1,0:T(8,128)(2,1)} %get-tuple-element.90), channel_id=1, source_target_pairs={{0,4},{2,6},{4,0},{6,2},{8,12},{10,14},{12,8},{14,10},{16,20},{18,... | collective-permute-start | bytes 3538952 | tf_op jit(solution)/shard_map/ppermute | solution.py:1000
  121.6 33.6 %collective-permute-start.13 = (bf16[384,1536]{1,0:T(8,128)(2,1)}, bf16[384,1536]{1,0:T(8,128)(2,1)}, u32[]{:S(2)}, u32[]{:S(2)}) collective-permute-start(bf16[384,1536]{1,0:T(8,128)(2,1)} %get-tuple-element.92), channel_id=1, source_target_pairs={{1,0},{2,3},{5,4},{6,7},{9,8},{10,11},{13,12},{14,15},{17,16},{18,... | collective-permute-start | bytes 3538952 | tf_op jit(solution)/shard_map/ppermute | solution.py:1031
  121.8 33.5 %collective-permute-start.14 = (bf16[384,1536]{1,0:T(8,128)(2,1)}, bf16[384,1536]{1,0:T(8,128)(2,1)}, u32[]{:S(2)}, u32[]{:S(2)}) collective-permute-start(bf16[384,1536]{1,0:T(8,128)(2,1)} %get-tuple-element.91), channel_id=1, source_target_pairs={{1,2},{2,1},{5,6},{6,5},{9,10},{10,9},{13,14},{14,13},{17,18},{18,... | collective-permute-start | bytes 3538952 | tf_op jit(solution)/shard_map/ppermute | solution.py:1032
  162.1 20.4 %collective-permute-start.17 = (bf16[4,1,48,1536]{3,2,1,0:T(8,128)(2,1)}, bf16[4,1,48,1536]{3,2,1,0:T(8,128)(2,1)}, u32[]{:S(2)}, u32[]{:S(2)}) collective-permute-start(bf16[4,1,48,1536]{3,2,1,0:T(8,128)(2,1)} %get-tuple-element.173), channel_id=1, source_target_pairs={{1,0},{2,3},{5,4},{6,7},{9,8},{10,11},{13,12},{14,15},{17,16},{18,... | collective-permute-start | bytes 1769480 | tf_op jit(solution)/shard_map/ppermute | solution.py:1004
  162.2 20.3 %collective-permute-start.18 = (bf16[4,1,48,1536]{3,2,1,0:T(8,128)(2,1)}, bf16[4,1,48,1536]{3,2,1,0:T(8,128)(2,1)}, u32[]{:S(2)}, u32[]{:S(2)}) collective-permute-start(bf16[4,1,48,1536]{3,2,1,0:T(8,128)(2,1)} %get-tuple-element.172), channel_id=1, source_target_pairs={{1,2},{2,1},{5,6},{6,5},{9,10},{10,9},{13,14},{14,13},{17,18},{18,... | collective-permute-start | bytes 1769480 | tf_op jit(solution)/shard_map/ppermute | solution.py:1005
  164.5 58.9 %collective-permute-start.25 = (bf16[384,1664]{1,0:T(8,128)(2,1)}, bf16[384,1664]{1,0:T(8,128)(2,1)}, u32[]{:S(2)}, u32[]{:S(2)}) collective-permute-start(bf16[384,1664]{1,0:T(8,128)(2,1)} %get-tuple-element.111), channel_id=1, source_target_pairs={{0,4},{2,6},{4,0},{6,2},{8,12},{10,14},{12,8},{14,10},{16,20},{18,... | collective-permute-start | bytes 3833864 | tf_op jit(solution)/shard_map/ppermute | solution.py:1000
  173.8 41.5 %all-to-all-start.2 = ((bf16[32,16,768]{2,1,0:T(8,128)(2,1)}), bf16[32,16,768]{2,1,0:T(8,128)(2,1)S(1)}, u32[]{:S(2)}, u32[]{:S(2)}) async-start(bf16[32,16,768]{2,1,0:T(8,128)(2,1)} %bitcast.19), calls=%async_computation.2 | async-start | bytes 1572864 | tf_op jit(solution)/shard_map/all_to_all | solution.py:1054
  182.5 32.1 %collective-permute-start.16 = (bf16[1024,768]{1,0:T(8,128)(2,1)}, bf16[1024,768]{1,0:T(8,128)(2,1)S(1)}, u32[]{:S(2)}, u32[]{:S(2)}) collective-permute-start(bf16[1024,768]{1,0:T(8,128)(2,1)} %get-tuple-element.96), channel_id=1, source_target_pairs={{0,2},{2,0},{4,6},{6,4},{8,10},{10,8},{12,14},{14,12},{16,18},{18,... | collective-permute-start | bytes 4718600 | tf_op jit(solution)/shard_map/ppermute | solution.py:919
  184.2 15.8 %collective-permute-start.21 = (bf16[1,1,48,1536]{3,2,1,0:T(8,128)(2,1)S(1)}, bf16[1,1,48,1536]{3,2,1,0:T(8,128)(2,1)S(1)}, u32[]{:S(2)}, u32[]{:S(2)}) collective-permute-start(bf16[1,1,48,1536]{3,2,1,0:T(8,128)(2,1)S(1)} %get-tuple-element.182), channel_id=1, source_target_pairs={{0,8},{2,10},{4,12},{6,14},{8,0},{10,2},{12,4},{14,6},{16,24},{18,... | collective-permute-start | bytes 442376 | tf_op jit(solution)/shard_map/ppermute | solution.py:1017
  184.7 24.9 %collective-permute-start.22 = (bf16[1,1,48,1536]{3,2,1,0:T(8,128)(2,1)S(1)}, bf16[1,1,48,1536]{3,2,1,0:T(8,128)(2,1)S(1)}, u32[]{:S(2)}, u32[]{:S(2)}) collective-permute-start(bf16[1,1,48,1536]{3,2,1,0:T(8,128)(2,1)S(1)} %get-tuple-element.181), channel_id=1, source_target_pairs={{0,16},{2,18},{4,20},{6,22},{8,24},{10,26},{12,28},{14,30},{16,0},... | collective-permute-start | bytes 442376 | tf_op jit(solution)/shard_map/ppermute | solution.py:1017
  187.2 27.3 %collective-permute-start.23 = (bf16[1,1,48,1536]{3,2,1,0:T(8,128)(2,1)S(1)}, bf16[1,1,48,1536]{3,2,1,0:T(8,128)(2,1)S(1)}, u32[]{:S(2)}, u32[]{:S(2)}) collective-permute-start(bf16[1,1,48,1536]{3,2,1,0:T(8,128)(2,1)S(1)} %get-tuple-element.180), channel_id=1, source_target_pairs={{0,24},{2,26},{4,28},{6,30},{8,16},{10,18},{12,20},{14,22},{16,8},... | collective-permute-start | bytes 442376 | tf_op jit(solution)/shard_map/ppermute | solution.py:1017
  200.0 15.2 %collective-permute-start.20 = (bf16[512,768]{1,0:T(8,128)(2,1)S(1)}, bf16[512,768]{1,0:T(8,128)(2,1)S(1)}, u32[]{:S(2)}, u32[]{:S(2)}) collective-permute-start(bf16[512,768]{1,0:T(8,128)(2,1)S(1)} %dynamic-slice_bitcast_fusion.1), channel_id=1, source_target_pairs={{0,1},{3,2},{4,5},{7,6},{8,9},{11,10},{12,13},{15,14},{16,17},{19,... | collective-permute-start | bytes 2359304 | tf_op jit(solution)/shard_map/ppermute | solution.py:928
  209.5 15.9 %collective-permute-start.33 = (bf16[4,1,48,1536]{3,2,1,0:T(8,128)(2,1)}, bf16[4,1,48,1536]{3,2,1,0:T(8,128)(2,1)}, u32[]{:S(2)}, u32[]{:S(2)}) collective-permute-start(bf16[4,1,48,1536]{3,2,1,0:T(8,128)(2,1)} %get-tuple-element.170), channel_id=1, source_target_pairs={{0,4},{2,6},{4,0},{6,2},{8,12},{10,14},{12,8},{14,10},{16,20},{18,... | collective-permute-start | bytes 1769480 | tf_op jit(solution)/shard_map/ppermute | solution.py:1000
  217.6 28.9 %collective-permute-start.19 = (bf16[1024,768]{1,0:T(8,128)(2,1)S(1)}, bf16[1024,768]{1,0:T(8,128)(2,1)}, u32[]{:S(2)}, u32[]{:S(2)}) collective-permute-start(bf16[1024,768]{1,0:T(8,128)(2,1)S(1)} %add_convert_fusion.refs_1_), channel_id=1, source_target_pairs={{0,1},{3,2},{4,5},{7,6},{8,9},{11,10},{12,13},{15,14},{16,17},{19,... | collective-permute-start | bytes 4718600 | tf_op jit(solution)/shard_map/ppermute | solution.py:928
  219.1 27.4 %all-to-all-start.3 = ((bf16[16,2,16,768]{3,2,1,0:T(8,128)(2,1)}), bf16[16,2,16,768]{3,2,1,0:T(8,128)(2,1)S(1)}, u32[]{:S(2)}, u32[]{:S(2)}) async-start(bf16[16,2,16,768]{3,2,1,0:T(8,128)(2,1)} %bitcast.30), calls=%async_computation.3 | async-start | bytes 1572864 | tf_op jit(solution)/shard_map/all_to_all | solution.py:1069
  226.6 29.2 %collective-permute-start.27 = (bf16[4,1,48,1664]{3,2,1,0:T(8,128)(2,1)}, bf16[4,1,48,1664]{3,2,1,0:T(8,128)(2,1)}, u32[]{:S(2)}, u32[]{:S(2)}) collective-permute-start(bf16[4,1,48,1664]{3,2,1,0:T(8,128)(2,1)} %get-tuple-element.169), channel_id=1, source_target_pairs={{1,0},{2,3},{5,4},{6,7},{9,8},{10,11},{13,12},{14,15},{17,16},{18,... | collective-permute-start | bytes 1916936 | tf_op jit(solution)/shard_map/ppermute | solution.py:1004
  226.7 29.0 %collective-permute-start.28 = (bf16[4,1,48,1664]{3,2,1,0:T(8,128)(2,1)}, bf16[4,1,48,1664]{3,2,1,0:T(8,128)(2,1)}, u32[]{:S(2)}, u32[]{:S(2)}) collective-permute-start(bf16[4,1,48,1664]{3,2,1,0:T(8,128)(2,1)} %get-tuple-element.168), channel_id=1, source_target_pairs={{1,2},{2,1},{5,6},{6,5},{9,10},{10,9},{13,14},{14,13},{17,18},{18,... | collective-permute-start | bytes 1916936 | tf_op jit(solution)/shard_map/ppermute | solution.py:1005
  231.2 17.3 %collective-permute-start.34 = (bf16[1,1,48,1536]{3,2,1,0:T(8,128)(2,1)}, bf16[1,1,48,1536]{3,2,1,0:T(8,128)(2,1)S(1)}, u32[]{:S(2)}, u32[]{:S(2)}) collective-permute-start(bf16[1,1,48,1536]{3,2,1,0:T(8,128)(2,1)} %get-tuple-element.179), channel_id=1, source_target_pairs={{0,8},{2,10},{4,12},{6,14},{8,0},{10,2},{12,4},{14,6},{16,24},{18,... | collective-permute-start | bytes 442376 | tf_op jit(solution)/shard_map/ppermute | solution.py:1017
  236.4 14.7 %collective-permute-start.35 = (bf16[1,1,48,1536]{3,2,1,0:T(8,128)(2,1)}, bf16[1,1,48,1536]{3,2,1,0:T(8,128)(2,1)S(1)}, u32[]{:S(2)}, u32[]{:S(2)}) collective-permute-start(bf16[1,1,48,1536]{3,2,1,0:T(8,128)(2,1)} %get-tuple-element.178), channel_id=1, source_target_pairs={{0,16},{2,18},{4,20},{6,22},{8,24},{10,26},{12,28},{14,30},{16,0},... | collective-permute-start | bytes 442376 | tf_op jit(solution)/shard_map/ppermute | solution.py:1017
  248.5 26.1 %collective-permute-start.24 = (bf16[512,768]{1,0:T(8,128)(2,1)S(1)}, bf16[512,768]{1,0:T(8,128)(2,1)S(1)}, u32[]{:S(2)}, u32[]{:S(2)}) collective-permute-start(bf16[512,768]{1,0:T(8,128)(2,1)S(1)} %fusion), channel_id=1, source_target_pairs={{0,1},{1,0},{2,3},{3,2},{4,5},{5,4},{6,7},{7,6},{8,9},{9,8},{10,11... | collective-permute-start | bytes 2359304 | tf_op jit(solution)/shard_map/ppermute | solution.py:1076
  257.4 13.4 %collective-permute-start.30 = (bf16[1,1,48,1664]{3,2,1,0:T(8,128)(2,1)S(1)}, bf16[1,1,48,1664]{3,2,1,0:T(8,128)(2,1)S(1)}, u32[]{:S(2)}, u32[]{:S(2)}) collective-permute-start(bf16[1,1,48,1664]{3,2,1,0:T(8,128)(2,1)S(1)} %get-tuple-element.175), channel_id=1, source_target_pairs={{0,16},{2,18},{4,20},{6,22},{8,24},{10,26},{12,28},{14,30},{16,0},... | collective-permute-start | bytes 479240 | tf_op jit(solution)/shard_map/ppermute | solution.py:1017
  259.4 15.1 %collective-permute-start.31 = (bf16[1,1,48,1664]{3,2,1,0:T(8,128)(2,1)S(1)}, bf16[1,1,48,1664]{3,2,1,0:T(8,128)(2,1)S(1)}, u32[]{:S(2)}, u32[]{:S(2)}) collective-permute-start(bf16[1,1,48,1664]{3,2,1,0:T(8,128)(2,1)S(1)} %get-tuple-element.174), channel_id=1, source_target_pairs={{0,24},{2,26},{4,28},{6,30},{8,16},{10,18},{12,20},{14,22},{16,8},... | collective-permute-start | bytes 479240 | tf_op jit(solution)/shard_map/ppermute | solution.py:1017
  (36 other events, 262.1 us)

commit v2 on v0

--- a/solution.py
+++ b/solution.py
@@ -105,16 +105,33 @@
 PARTS = 4
 
 
-def part_moves(pairs, sems):
+def part_move(pairs, sems, c, first=0):
     moves = []
+    for n, (source, target) in enumerate(pairs):
+        count = source.shape[0] // PARTS
+        here = pl.ds(pl.multiple_of(c * count, count), count)
+        moves.append(move(source.at[here, :], target.at[here, :], sems.at[first + n, c]))
+    return moves
+
+
+def start_parts(pairs, sems):
     for c in range(PARTS):
-        row = []
-        for n, (source, target) in enumerate(pairs):
-            count = source.shape[0] // PARTS
-            here = pl.ds(c * count, count)
-            row.append(move(source.at[here, :], target.at[here, :], sems.at[n, c]))
-        moves.append(row)
-    return moves
+        start_all(part_move(pairs, sems, c))
+
+
+def row_parts(rows, blk, wait, body):
+    steps = rows // PARTS // blk
+
+    def part(c, carry):
+        wait(c)
+
+        def step(i, carry):
+            body(pl.multiple_of((c * steps + i) * blk, blk))
+            return carry
+
+        return lax.fori_loop(0, steps, step, carry, unroll=4)
+
+    lax.fori_loop(0, PARTS, part, 0)
 
 
 def start_all(moves):
@@ -182,10 +199,9 @@
         move(source, target, in_sems.at[n])
         for n, (source, target) in enumerate([(tok, tok_v), (w3, w3_v), (wp, wp_v)])
     ]
-    halves = part_moves([(own, own_v), (oth, oth_v)], half_sems)
+    halves = [(own, own_v), (oth, oth_v)]
     loads[0].start()
-    for part_of in halves:
-        start_all(part_of)
+    start_parts(halves, half_sems)
     start_all(loads[1:])
     early = [
         move(source, target, out_sems.at[n])
@@ -200,26 +216,23 @@
     spread_clips(seg_row, seg_b)
 
     loads[0].wait()
-    steps = half_rows // PARTS // blk
     for n, src, half in ((0, own_v, flags[0]), (1, oth_v, 1 - flags[0])):
-        for c in range(PARTS):
-            halves[c][n].wait()
-
-            def mix(i, carry, src=src, half=half, c=c):
-                low = (c * steps + i) * blk
-                here = pl.ds(pl.multiple_of(half * half_rows + low, blk), blk)
-                there = pl.ds(pl.multiple_of(low, blk), blk)
-                mine, other = tok_v[here, :].astype(F32), src[there, :].astype(F32)
-                blended = ratio * mine + (1.0 - ratio) * other
-                mixed_v[here, :] = blended
-                centred, scale = row_stats(blended)
-                inv_v[here, :] = on_lanes(scale)
-                plain = centred * scale
-                normed_v[here, :] = plain.astype(BF16)
-                n1_v[here, :] = (plain * vecs[0:1, :] + vecs[1:2, :]).astype(BF16)
-                return carry
-
-            lax.fori_loop(0, steps, mix, 0, unroll=True)
+
+        def mix(low, src=src, half=half):
+            here = pl.ds(pl.multiple_of(half * half_rows + low, blk), blk)
+            there = pl.ds(low, blk)
+            mine, other = tok_v[here, :].astype(F32), src[there, :].astype(F32)
+            blended = ratio * mine + (1.0 - ratio) * other
+            mixed_v[here, :] = blended
+            centred, scale = row_stats(blended)
+            inv_v[here, :] = on_lanes(scale)
+            plain = centred * scale
+            normed_v[here, :] = plain.astype(BF16)
+            n1_v[here, :] = (plain * vecs[0:1, :] + vecs[1:2, :]).astype(BF16)
+
+        row_parts(
+            half_rows, blk, lambda c, n=n: wait_all(part_move([halves[n]], half_sems, c, n)), mix
+        )
     start_all(early[:4])
 
     loads[1].wait()
@@ -372,11 +385,8 @@
     kept_out = jnp.where(home, flags[0], 1 - flags[0]) if in_rows != out_rows else across
     sides = (across, kept_out)
 
-    loads = part_moves(
-        [(mixed, mixed_v), (p_own, own_v), (p_oth, oth_v), (cot, cot_v)], in_sems
-    )
-    for part_of in loads:
-        start_all(part_of)
+    loads = [(mixed, mixed_v), (p_own, own_v), (p_oth, oth_v), (cot, cot_v)]
+    start_parts(loads, in_sems)
 
     weights = [move(w_in, w_in_v, weight_sems.at[0])]
     weights[0].start()
@@ -401,24 +411,20 @@
     start_all(turns)
 
     g_bout[...] = jnp.zeros_like(g_bout)
-    steps = rows // PARTS // blk
-    for c in range(PARTS):
-        wait_all(loads[c])
-
-        def norm(i, carry, c=c):
-            here = pl.ds(pl.multiple_of((c * steps + i) * blk, blk), blk)
-            attn = own_v[here, :].astype(F32) + oth_v[here, :].astype(F32)
-            total = mixed_v[here, :] + attn + vecs[4:5, :]
-            mixed_v[here, :] = total
-            centred, scale = row_stats(total)
-            inv_v[here, :] = on_lanes(scale)
-            plain = centred * scale
-            normed_v[here, :] = plain.astype(BF16)
-            n2[here, :] = (plain * vecs[2:3, :] + vecs[3:4, :]).astype(BF16)
-            g_bout[...] += fold_rows(cot_v[here, :].astype(F32))
-            return carry
-
-        lax.fori_loop(0, steps, norm, 0, unroll=4)
+
+    def norm(low):
+        here = pl.ds(low, blk)
+        attn = own_v[here, :].astype(F32) + oth_v[here, :].astype(F32)
+        total = mixed_v[here, :] + attn + vecs[4:5, :]
+        mixed_v[here, :] = total
+        centred, scale = row_stats(total)
+        inv_v[here, :] = on_lanes(scale)
+        plain = centred * scale
+        normed_v[here, :] = plain.astype(BF16)
+        n2[here, :] = (plain * vecs[2:3, :] + vecs[3:4, :]).astype(BF16)
+        g_bout[...] += fold_rows(cot_v[here, :].astype(F32))
+
+    row_parts(rows, blk, lambda c: wait_all(part_move(loads, in_sems, c)), norm)
     stores = [
         move(source, target, out_sems.at[0, n])
         for n, (source, target) in enumerate(
@@ -431,7 +437,7 @@
 
     g_bin[...] = jnp.zeros_like(g_bin)
 
-    def row_block(i, carry):
+    def row_block(i):
         here = pl.ds(pl.multiple_of(i * big, big), big)
         for j in range(units // width):
             cols = pl.ds(j * width, width)
@@ -451,9 +457,13 @@
         own_v[here, :] = nn(act[here, :], w_out_v[...]).astype(BF16)
         for n, (source, target) in enumerate([(oth_v, gn_part), (own_v, part)]):
             move(source.at[here, :], target.at[here, :], out_sems.at[1 + n, i]).start()
+
+    def two_blocks(i, carry):
+        row_block(2 * i)
+        row_block(2 * i + 1)
         return carry
 
-    lax.fori_loop(0, rows // big, row_block, 0)
+    lax.fori_loop(0, rows // big // 2, two_blocks, 0)
     for i in range(rows // big):
         here = pl.ds(i * big, big)
         for n, (source, target) in enumerate([(oth_v, gn_part), (own_v, part)]):
@@ -536,12 +546,8 @@
     big = 256
     blocks = lead_blocks(width, lead_rows)
     kept_side = flags[2]
-    row_loads = part_moves(
-        [(g_own, own_v), (g_oth, oth_v), (cot, cot_v), (normed, normed_v), (inv, inv_v)],
-        row_sems,
-    )
-    for part_of in row_loads:
-        start_all(part_of)
+    row_loads = [(g_own, own_v), (g_oth, oth_v), (cot, cot_v), (normed, normed_v), (inv, inv_v)]
+    start_parts(row_loads, row_sems)
     loads = [
         move(source, target, in_sems.at[n])
         for n, (source, target) in enumerate(
@@ -557,27 +563,22 @@
     dv[...] = jnp.zeros_like(dv)
     spread_clips(seg_row, seg_b)
 
-    steps = rows // PARTS // blk
-    for c in range(PARTS):
-        wait_all(row_loads[c])
-
-        def norm(i, carry, c=c):
-            here = pl.ds(pl.multiple_of((c * steps + i) * blk, blk), blk)
-            grad = own_v[here, :].astype(F32) + oth_v[here, :].astype(F32)
-            plain = normed_v[here, :].astype(F32)
-            scaled = grad * vecs[2:3, :]
-            mean_one = jnp.mean(scaled, axis=-1, keepdims=True)
-            mean_two = jnp.mean(scaled * plain, axis=-1, keepdims=True)
-            scale = wide_rsqrt(inv_v, here, width)
-            back = cot_v[here, :].astype(F32) + scale * (scaled - mean_one - plain * mean_two)
-            gh_v[here, :] = back
-            low_v[here, :] = back.astype(BF16)
-            sums[0] += fold_rows(grad * plain)
-            sums[1] += fold_rows(grad)
-            sums[2] += fold_rows(back)
-            return carry
-
-        lax.fori_loop(0, steps, norm, 0, unroll=2)
+    def norm(low):
+        here = pl.ds(low, blk)
+        grad = own_v[here, :].astype(F32) + oth_v[here, :].astype(F32)
+        plain = normed_v[here, :].astype(F32)
+        scaled = grad * vecs[2:3, :]
+        mean_one = jnp.mean(scaled, axis=-1, keepdims=True)
+        mean_two = jnp.mean(scaled * plain, axis=-1, keepdims=True)
+        scale = wide_rsqrt(inv_v, here, width)
+        back = cot_v[here, :].astype(F32) + scale * (scaled - mean_one - plain * mean_two)
+        gh_v[here, :] = back
+        low_v[here, :] = back.astype(BF16)
+        sums[0] += fold_rows(grad * plain)
+        sums[1] += fold_rows(grad)
+        sums[2] += fold_rows(back)
+
+    row_parts(rows, blk, lambda c: wait_all(part_move(row_loads, row_sems, c)), norm)
     stores = [move(gh_v, gh, out_sems.at[0])]
     stores[0].start()
 
@@ -822,58 +823,72 @@
     )
 
 
-def mixed_back_kernel(blend, vecs, gh, g_own, g_oth, normed, inv, outgoing, kept, *refs):
-    gh_v, own_v, oth_v, normed_v, inv_v, leave_v, kept_v, in_sems, out_sems = refs
+def mixed_back_kernel(blend, flags, vecs, gh, g_own, g_oth, normed, inv, outgoing, kept, *refs):
+    gh_v, own_v, oth_v, normed_v, inv_v, leave_v, kept_v, in_sems, out_sems, leave_sems = refs
     ratio = blend[0]
     rows, width = gh.shape
     blk = 32
-    loads = part_moves(
-        [(gh, gh_v), (g_own, own_v), (g_oth, oth_v), (normed, normed_v), (inv, inv_v)], in_sems
-    )
-    stores = part_moves([(leave_v, outgoing), (kept_v, kept)], out_sems)
-    for part_of in loads:
-        start_all(part_of)
-    steps = rows // PARTS // blk
+    piece = leave_v.shape[1]
+    loads = [(gh, gh_v), (g_own, own_v), (g_oth, oth_v), (normed, normed_v), (inv, inv_v)]
+    stores = [(kept_v, kept)]
+    start_parts(loads, in_sems)
+
+    def norm(low):
+        here = pl.ds(low, blk)
+        grad = own_v[here, :].astype(F32) + oth_v[here, :].astype(F32)
+        plain = normed_v[here, :].astype(F32)
+        scaled = grad * vecs[0:1, :]
+        mean_one = jnp.mean(scaled, axis=-1, keepdims=True)
+        mean_two = jnp.mean(scaled * plain, axis=-1, keepdims=True)
+        scale = wide_rsqrt(inv_v, here, width)
+        back = gh_v[here, :] + scale * (scaled - mean_one - plain * mean_two)
+        leave = ((1.0 - ratio) * back).astype(BF16)
+        leave_v[pl.ds(low // piece, blk // piece)] = leave.reshape(blk // piece, piece, width)
+        kept_v[here, :] = (ratio * back).astype(BF16)
+
+    row_parts(rows, blk, lambda c: wait_all(part_move(loads, in_sems, c)), norm)
+    start_parts(stores, out_sems)
+    if len(outgoing.shape) == 3:
+        leaves = [move(leave_v, outgoing, leave_sems.at[0])]
+    else:
+        count = outgoing.shape[0]
+        leaves = [
+            move(
+                leave_v.at[pl.ds(pl.multiple_of((2 * m + flags[0]) * count, count), count)],
+                outgoing.at[:, m],
+                leave_sems.at[m],
+            )
+            for m in range(2)
+        ]
+    start_all(leaves)
     for c in range(PARTS):
-        wait_all(loads[c])
-
-        def norm(i, carry, c=c):
-            here = pl.ds(pl.multiple_of((c * steps + i) * blk, blk), blk)
-            grad = own_v[here, :].astype(F32) + oth_v[here, :].astype(F32)
-            plain = normed_v[here, :].astype(F32)
-            scaled = grad * vecs[0:1, :]
-            mean_one = jnp.mean(scaled, axis=-1, keepdims=True)
-            mean_two = jnp.mean(scaled * plain, axis=-1, keepdims=True)
-            scale = wide_rsqrt(inv_v, here, width)
-            back = gh_v[here, :] + scale * (scaled - mean_one - plain * mean_two)
-            leave_v[here, :] = ((1.0 - ratio) * back).astype(BF16)
-            kept_v[here, :] = (ratio * back).astype(BF16)
-            return carry
-
-        lax.fori_loop(0, steps, norm, 0, unroll=4)
-        start_all(stores[c])
-    for part_of in stores:
-        wait_all(part_of)
-
-
-def mixed_back(blend, vecs, gh, g_own, g_oth, normed, inv):
+        wait_all(part_move(stores, out_sems, c))
+    wait_all(leaves)
+
+
+def mixed_back(piece, ordered, blend, flags, vecs, gh, g_own, g_oth, normed, inv):
     rows, width = gh.shape
     tall = pltpu.VMEM((rows, width), BF16)
+    runs = rows // piece
+    dims = (runs // 4, 2, piece, width) if ordered else (runs, piece, width)
     return pl.pallas_call(
         mixed_back_kernel,
-        out_shape=(shape((rows, width), BF16), shape((rows, width), BF16)),
-        in_specs=[smem(), vmem()] + [hbm()] * 2 + [anywhere()] + [hbm()] * 2,
+        out_shape=(shape(dims, BF16), shape((rows, width), BF16)),
+        in_specs=[smem(), smem(), vmem()] + [hbm()] * 2 + [anywhere()] + [hbm()] * 2,
         out_specs=[hbm(), hbm()],
         scratch_shapes=[
             pltpu.VMEM((rows, width), F32),
-            tall, tall, tall, pltpu.VMEM((rows, LANES), F32), tall, tall,
+            tall, tall, tall, pltpu.VMEM((rows, LANES), F32),
+            pltpu.VMEM((runs, piece, width), BF16),
+            tall,
             pltpu.SemaphoreType.DMA((5, PARTS)),
-            pltpu.SemaphoreType.DMA((2, PARTS)),
+            pltpu.SemaphoreType.DMA((1, PARTS)),
+            pltpu.SemaphoreType.DMA((2,)),
         ],
         compiler_params=params(60),
         cost_estimate=SMALL,
         name="mixed_back",
-    )(blend, vecs, gh, g_own, g_oth, normed, inv)
+    )(blend, flags, vecs, gh, g_own, g_oth, normed, inv)
 
 
 def shards(
@@ -1047,10 +1062,16 @@
     gn1_oth = swap(after(gn1_part, in_got, *out_first))
     attn_first = [attn_keep, send_across(attn_send)]
     in_terms = send_pair(total(in_keep, in_got).astype(BF16))
-    outgoing, kept = mixed_back(blend, vecs, gh, gn1_part, gn1_oth, normed_one, inv_one)
-
-    leaving = taken(outgoing.reshape(2, 2, dp_count, piece, width), core, 1)
-    leaving = leaving.transpose(1, 0, 2, 3).reshape(2 * dp_count, piece, width)
+    ordered = piece % 16 == 0
+    outgoing, kept = mixed_back(
+        piece if ordered else 16, ordered, blend, flags, vecs, gh, gn1_part, gn1_oth, normed_one, inv_one
+    )
+
+    if ordered:
+        leaving = outgoing.reshape(2 * dp_count, piece, width)
+    else:
+        leaving = taken(outgoing.reshape(2, 2, dp_count, piece, width), core, 1)
+        leaving = leaving.transpose(1, 0, 2, 3).reshape(2 * dp_count, piece, width)
     back = lax.all_to_all(leaving, both, 0, 0, tiled=True)
 
     in_value = total(*after(in_terms, leaving)).astype(BF16)
@@ -1089,8 +1110,7 @@
         side_by_side(*(after(terms, marker) for terms in (out_terms, attn_terms))),
         mine,
     )
-    summed = after(summed, other)
-    sum_out, sum_attn = summed[:, :units], summed[:, units:]
+    sum_out, sum_attn = after(summed[:, :units], other), summed[:, units:]
     sum_qkv = sum_attn[:, : 3 * local].reshape(-1, 3, local)
     sum_proj = sum_attn[:, 3 * local : 4 * local].T
     quarter, eighth = local // dp_count, units // dp_count

time: 281 us -> 279 us (level)
    ppermute x3, waiting for transfers between devices: 9.59 us -> 12.7 us  [send_across(): return lax.ppermute(value, 'dp', [(d, d ^ 1 << lead) for d in all_dp])]
  transfers between devices with their start and end apart: 38 -> 38, of which waited for: 12 -> 13; matrix products, arithmetic and copies ran while one was open for 16% -> 16% of each run, Pallas kernels for 21% -> 22%
where the time goes in v2:
time: 279 us; the launch traced here: 277 us
  Pallas kernels  89.1 us (32%)
  waiting for transfers between devices  73 us (26%)
  starting transfers between devices  62.9 us (23%)
  other arithmetic  26.1 us (9%)
  local copies, waits for them, and re-layouts  24 us (9%)
    pallas_call x1, Pallas kernels, attention_back(): pl.pallas_call(functools.partial(attention_back_kernel, lead_rows, part_r...  29.9 us
    pallas_call x1, Pallas kernels, feed(): pl.pallas_call(functools.partial(feed_kernel, in_rows, out_rows), out_sha...  29.5 us
    ppermute x6, waiting for transfers between devices, far(): lax.ppermute(taken(value, spot ^ flip, 2), 'dp', [(d, d ^ flip << shift)...  24 us
    pallas_call x1, Pallas kernels, attention(): pl.pallas_call(attention_kernel, out_shape=(shape((rows, width), F32), ta...  20.7 us
    ppermute x7, waiting for transfers between devices, half_weight(): return lax.ppermute(value, both, weight_move)  16.2 us
    ppermute x3, waiting for transfers between devices, send_across(): return lax.ppermute(value, 'dp', [(d, d ^ 1 << lead) for d in all_dp])  12.7 us
    ppermute x9, starting transfers between devices, swap(): return lax.ppermute(value, 'dp', core_swap)  9.08 us
    all_to_all x1, waiting for transfers between devices, shards(): lax.all_to_all(chosen, both, 0, 0, tiled=True).reshape(rows // 2, width)  8.83 us
  transfers between devices with their start and end apart: 38, of which 13 were waited for; matrix products, arithmetic and copies ran while one was open for 16% of the time, Pallas kernels for 22%

profile of v2, /device:TPU:8, one launch (start us, length us, event | category | flops | bytes accessed | tf_op | source)
XLA Modules:
  0.0 276.9 jit_solution(5988115989147952535)
XLA Ops:
  2.2 2.1 copy_bitcast_fusion
  4.3 6.3 %all-to-all-start = ((bf16[16,2,16,768]{3,2,1,0:T(8,128)(2,1)}), bf16[16,2,16,768]{3,2,1,0:T(8,128)(2,1)S(1)}, u32[]{:S(2)}, u32[]{:S(2)}) async-start(bf16[16,2,16,768]{3,2,1,0:T(8,128)(2,1)} %copy_bitcast_fusion), calls=%async_computation | async-start | bytes 1572864 | tf_op jit(solution)/shard_map/all_to_all | solution.py:976
  11.4 2.4 dynamic-slice_bitcast_fusion
  14.5 8.1 %collective-permute-done = f32[2304]{0:T(1024)S(1)} collective-permute-done((f32[2304]{0:T(1024)S(1)}, f32[2304]{0:T(1024)S(1)}, u32[]{:S(2)}, u32[]{:S(2)}) %collective-permute-start) | collective-permute-done | bytes 9248 | tf_op jit(solution)/shard_map/ppermute | solution.py:943
  22.6 2.5 collective-permute-start.7
  25.1 3.9 %collective-permute-done.4.refs_1_.wp = bf16[384,768]{1,0:T(8,128)(2,1)S(1)} collective-permute-done((bf16[384,768]{1,0:T(8,128)(2,1)}, bf16[384,768]{1,0:T(8,128)(2,1)S(1)}, u32[]{:S(2)}, u32[]{:S(2)}) %collective-permute-start.4) | collective-permute-done | bytes 589856 | tf_op jit(solution)/shard_map/ppermute | solution.py:943
  31.8 6.6 %all-to-all-start.1 = ((bf16[32,16,768]{2,1,0:T(8,128)(2,1)}), bf16[32,16,768]{2,1,0:T(8,128)(2,1)}, u32[]{:S(2)}, u32[]{:S(2)}) async-start(bf16[32,16,768]{2,1,0:T(8,128)(2,1)} %copy-done.2), calls=%async_computation.1 | async-start | bytes 1572864 | tf_op jit(solution)/shard_map/all_to_all | solution.py:986
  41.6 3.5 %collective-permute-done.7.w_out_one = bf16[768,768]{1,0:T(8,128)(2,1)} collective-permute-done((bf16[768,768]{1,0:T(8,128)(2,1)}, bf16[768,768]{1,0:T(8,128)(2,1)}, u32[]{:S(2)}, u32[]{:S(2)}) %collective-permute-start.7) | collective-permute-done | bytes 1179680 | tf_op jit(solution)/shard_map/ppermute | solution.py:943
  48.9 8.8 %all-to-all-done.1 = bf16[32,16,768]{2,1,0:T(8,128)(2,1)} async-done(((bf16[32,16,768]{2,1,0:T(8,128)(2,1)}), bf16[32,16,768]{2,1,0:T(8,128)(2,1)}, u32[]{:S(2)}, u32[]{:S(2)}) %all-to-all-start.1) | async-done | bytes 786464 | tf_op jit(solution)/shard_map/all_to_all | solution.py:986
  64.4 20.7 %attention.1 = (f32[1024,768]{1,0:T(8,128)}, bf16[1024,768]{1,0:T(8,128)(2,1)}, bf16[1024,768]{1,0:T(8,128)(2,1)}, f32[1024,128]{1,0:T(8,128)}, bf16[1024,384]{1...) custom-call(f32[1]{0:T(128)} %slice.93.blend, ...), custom_call_target="tpu_custom_call" | custom-call | flops 1048576 | bytes 1048576 | tf_op jit(solution)/shard_map/attention/pallas_call | solution.py:290
  86.8 2.6 collective-permute-done.9.p_oth
  90.5 29.5 %feed.1 = (f32[1024,768]{1,0:T(8,128)}, bf16[1024,768]{1,0:T(8,128)(2,1)}, bf16[1024,768]{1,0:T(8,128)(2,1)}, bf16[384,1536]{1,0:T(8,128)(2,1)}, bf16[384,1536]{...) custom-call(s32[3]{0:T(128)} %pad_add_fusion.flags, ...), custom_call_target="tpu_custom_call" | custom-call | flops 1048576 | bytes 1048576 | tf_op jit(solution)/shard_map/feed/pallas_call | solution.py:496
  121.2 1.7 collective-permute-start.14
  125.4 29.9 %attention_back.1 = (f32[1024,768]{1,0:T(8,128)}, bf16[1024,768]{1,0:T(8,128)(2,1)}, bf16[384,1664]{1,0:T(8,128)(2,1)}, bf16[384,1664]{1,0:T(8,128)(2,1)}, f32[9,768]{1,0:T(8,128)}) custom-call(s32[3]{0:T(128)} %pad_add_fusion.flags, f32[5,768]{1,0:T(8,128)} %stack.46.vecs, f32[1,1024]{1,0:T(1,128)} %bitcast.128, f32[6,1024]{1,0:T(8,128)} %get-tuple-element.74.lse, ...), custom_call_target="tpu_custom_call" | custom-call | flops 1048576 | bytes 1048576 | tf_op jit(solution)/shard_map/attention_back/pallas_call | solution.py:776
  155.3 4.1 %collective-permute-start.15 = (bf16[1024,768]{1,0:T(8,128)(2,1)}, bf16[1024,768]{1,0:T(8,128)(2,1)}, u32[]{:S(2)}, u32[]{:S(2)}) collective-permute-start(bf16[1024,768]{1,0:T(8,128)(2,1)} %get-tuple-element.91.g_own), channel_id=1, source_target_pairs={{0,2},{2,0},{4,6},{6,4},{8,10},{10,8},{12,14},{14,12},{16,18},{18,... | collective-permute-start | bytes 4718600 | tf_op jit(solution)/shard_map/ppermute | solution.py:934
  159.5 1.9 add_convert_fusion.3
  164.6 6.9 %mixed_back.1 = (bf16[16,2,16,768]{3,2,1,0:T(8,128)(2,1)}, bf16[1024,768]{1,0:T(8,128)(2,1)}) custom-call(f32[1]{0:T(128)} %slice.93.blend, s32[3]{0:T(128)} %pad_add_fusion.flags, f32[5,768]{1,0:T(8,128)} %stack.46.vecs, f32[1024,768]{1,0:T(8,128)} %get-tuple-element.86.gh, bf16[1024,768]{1,0:T(8,128)(2,1)} %get-tuple-element.91.g_own, ...), custom_call_target="tpu_custom_call" | custom-call | flops 1048576 | bytes 1048576 | tf_op jit(solution)/shard_map/mixed_back/pallas_call | solution.py:874
  171.5 8.6 %all-to-all-start.2 = ((bf16[32,16,768]{2,1,0:T(8,128)(2,1)}), bf16[32,16,768]{2,1,0:T(8,128)(2,1)S(1)}, u32[]{:S(2)}, u32[]{:S(2)}) async-start(bf16[32,16,768]{2,1,0:T(8,128)(2,1)} %bitcast.122), calls=%async_computation.2 | async-start | bytes 1572864 | tf_op jit(solution)/shard_map/all_to_all | solution.py:1075
  181.8 2.7 collective-permute-start.23
  185.1 2.2 add_convert_fusion.2
  187.2 12.7 %collective-permute-done.17 = bf16[384,1664]{1,0:T(8,128)(2,1)} collective-permute-done((bf16[384,1664]{1,0:T(8,128)(2,1)}, bf16[384,1664]{1,0:T(8,128)(2,1)}, u32[]{:S(2)}, u32[]{:S(2)}) %collective-permute-start.17) | collective-permute-done | bytes 1277984 | tf_op jit(solution)/shard_map/ppermute | solution.py:1015
  201.6 1.6 add_convert_fusion.1.refs_0_
  204.5 2.5 collective-permute-start.28
  209.4 1.7 collective-permute-start.16
  215.5 6.3 %all-to-all-start.3 = ((bf16[16,2,16,768]{3,2,1,0:T(8,128)(2,1)}), bf16[16,2,16,768]{3,2,1,0:T(8,128)(2,1)}, u32[]{:S(2)}, u32[]{:S(2)}) async-start(bf16[16,2,16,768]{3,2,1,0:T(8,128)(2,1)} %bitcast.25), calls=%async_computation.3 | async-start | bytes 1572864 | tf_op jit(solution)/shard_map/all_to_all | solution.py:1095
  223.8 1.7 fusion.1
  226.6 2.8 %collective-permute-start.31 = (bf16[1,1,48,3200]{3,2,1,0:T(8,128)(2,1)}, bf16[1,1,48,3200]{3,2,1,0:T(8,128)(2,1)}, u32[]{:S(2)}, u32[]{:S(2)}) collective-permute-start(bf16[1,1,48,3200]{3,2,1,0:T(8,128)(2,1)} %get-tuple-element.168), channel_id=1, source_target_pairs={{0,16},{2,18},{4,20},{6,22},{8,24},{10,26},{12,28},{14,30},{16,0},... | collective-permute-start | bytes 921608 | tf_op jit(solution)/shard_map/ppermute | solution.py:1032
  229.9 2.6 add_convert_fusion
  232.7 8.1 %all-to-all-done.3 = bf16[16,2,16,768]{3,2,1,0:T(8,128)(2,1)} async-done(((bf16[16,2,16,768]{3,2,1,0:T(8,128)(2,1)}), bf16[16,2,16,768]{3,2,1,0:T(8,128)(2,1)}, u32[]{:S(2)}, u32[]{:S(2)}) %all-to-all-start.3) | async-done | bytes 786464 | tf_op jit(solution)/shard_map/all_to_all | solution.py:1095
  242.8 2.0 collective-permute-start.25
  245.2 14.6 %collective-permute-done.31 = bf16[1,1,48,3200]{3,2,1,0:T(8,128)(2,1)} collective-permute-done((bf16[1,1,48,3200]{3,2,1,0:T(8,128)(2,1)}, bf16[1,1,48,3200]{3,2,1,0:T(8,128)(2,1)}, u32[]{:S(2)}, u32[]{:S(2)}) %collective-permute-start.31) | collective-permute-done | bytes 307232 | tf_op jit(solution)/shard_map/ppermute | solution.py:1032
  259.8 8.0 %collective-permute-done.32 = bf16[1,1,48,3200]{3,2,1,0:T(8,128)(2,1)} collective-permute-done((bf16[1,1,48,3200]{3,2,1,0:T(8,128)(2,1)S(1)}, bf16[1,1,48,3200]{3,2,1,0:T(8,128)(2,1)}, u32[]{:S(2)}, u32[]{:S(2)}) %collective-permute-start.32) | collective-permute-done | bytes 307232 | tf_op jit(solution)/shard_map/ppermute | solution.py:1032
  (169 shorter events, 55.7 us)
Async XLA Ops:
  0.6 28.9 %collective-permute-start.3 = (bf16[3,768,384]{2,1,0:T(8,128)(2,1)}, bf16[3,768,384]{2,1,0:T(8,128)(2,1)S(1)}, u32[]{:S(2)}, u32[]{:S(2)}) collective-permute-start(bf16[3,768,384]{2,1,0:T(8,128)(2,1)} %bitcast.130), channel_id=1, source_target_pairs={{0,1},{3,2},{4,5},{7,6},{8,9},{11,10},{12,13},{15,14},{16,17},{19,... | collective-permute-start | bytes 5308424 | tf_op jit(solution)/shard_map/ppermute | solution.py:943
  4.3 25.2 %all-to-all-start = ((bf16[16,2,16,768]{3,2,1,0:T(8,128)(2,1)}), bf16[16,2,16,768]{3,2,1,0:T(8,128)(2,1)S(1)}, u32[]{:S(2)}, u32[]{:S(2)}) async-start(bf16[16,2,16,768]{3,2,1,0:T(8,128)(2,1)} %copy_bitcast_fusion), calls=%async_computation | async-start | bytes 1572864 | tf_op jit(solution)/shard_map/all_to_all | solution.py:976
  10.6 36.8 %collective-permute-start.2 = (bf16[1024,768]{1,0:T(8,128)(2,1)}, bf16[1024,768]{1,0:T(8,128)(2,1)}, u32[]{:S(2)}, u32[]{:S(2)}) collective-permute-start(bf16[1024,768]{1,0:T(8,128)(2,1)} %param.17), channel_id=1, source_target_pairs={{0,2},{2,0},{4,6},{6,4},{8,10},{10,8},{12,14},{14,12},{16,18},{18,... | collective-permute-start | bytes 4718600 | tf_op jit(solution)/shard_map/ppermute | solution.py:934
  10.8 11.7 %collective-permute-start = (f32[2304]{0:T(1024)S(1)}, f32[2304]{0:T(1024)S(1)}, u32[]{:S(2)}, u32[]{:S(2)}) collective-permute-start(f32[2304]{0:T(1024)S(1)} %constant_dynamic-update-slice_fusion), channel_id=1, source_target_pairs={{0,1},{3,2},{4,5},{7,6},{8,9},{11,10},{12,13},{15,14},{16,17},{19,... | collective-permute-start | bytes 27656 | tf_op jit(solution)/shard_map/ppermute | solution.py:943
  10.9 18.1 %collective-permute-start.4 = (bf16[384,768]{1,0:T(8,128)(2,1)}, bf16[384,768]{1,0:T(8,128)(2,1)S(1)}, u32[]{:S(2)}, u32[]{:S(2)}) collective-permute-start(bf16[384,768]{1,0:T(8,128)(2,1)} %param.25), channel_id=1, source_target_pairs={{0,1},{3,2},{4,5},{7,6},{8,9},{11,10},{12,13},{15,14},{16,17},{19,... | collective-permute-start | bytes 1769480 | tf_op jit(solution)/shard_map/ppermute | solution.py:943
  11.2 34.6 %collective-permute-start.5 = (bf16[1024,768]{1,0:T(8,128)(2,1)}, bf16[1024,768]{1,0:T(8,128)(2,1)}, u32[]{:S(2)}, u32[]{:S(2)}) collective-permute-start(bf16[1024,768]{1,0:T(8,128)(2,1)} %param.33), channel_id=1, source_target_pairs={{0,2},{2,0},{4,6},{6,4},{8,10},{10,8},{12,14},{14,12},{16,18},{18,... | collective-permute-start | bytes 4718600 | tf_op jit(solution)/shard_map/ppermute | solution.py:934
  22.6 22.5 %collective-permute-start.7 = (bf16[768,768]{1,0:T(8,128)(2,1)}, bf16[768,768]{1,0:T(8,128)(2,1)}, u32[]{:S(2)}, u32[]{:S(2)}) collective-permute-start(bf16[768,768]{1,0:T(8,128)(2,1)} %dynamic-slice_bitcast_fusion), channel_id=1, source_target_pairs={{0,1},{3,2},{4,5},{7,6},{8,9},{11,10},{12,13},{15,14},{16,17},{19,... | collective-permute-start | bytes 3538952 | tf_op jit(solution)/shard_map/ppermute | solution.py:943
  31.8 26.0 %all-to-all-start.1 = ((bf16[32,16,768]{2,1,0:T(8,128)(2,1)}), bf16[32,16,768]{2,1,0:T(8,128)(2,1)}, u32[]{:S(2)}, u32[]{:S(2)}) async-start(bf16[32,16,768]{2,1,0:T(8,128)(2,1)} %copy-done.2), calls=%async_computation.1 | async-start | bytes 1572864 | tf_op jit(solution)/shard_map/all_to_all | solution.py:986
  45.1 18.3 %collective-permute-start.8 = (bf16[768,768]{1,0:T(8,128)(2,1)}, bf16[768,768]{1,0:T(8,128)(2,1)S(1)}, u32[]{:S(2)}, u32[]{:S(2)}) collective-permute-start(bf16[768,768]{1,0:T(8,128)(2,1)} %collective-permute-done.7.w_out_one), channel_id=1, source_target_pairs={{1,5},{2,6},{5,1},{6,2},{9,13},{10,14},{13,9},{14,10},{17,21},{18,... | collective-permute-start | bytes 3538952 | tf_op jit(solution)/shard_map/ppermute | solution.py:970
  59.3 27.4 %collective-permute-start.10 = (bf16[768,1536]{1,0:T(8,128)(2,1)}, bf16[768,1536]{1,0:T(8,128)(2,1)}, u32[]{:S(2)}, u32[]{:S(2)}) collective-permute-start(bf16[768,1536]{1,0:T(8,128)(2,1)} %param.29), channel_id=1, source_target_pairs={{0,1},{3,2},{4,5},{7,6},{8,9},{11,10},{12,13},{15,14},{16,17},{19,... | collective-permute-start | bytes 7077896 | tf_op jit(solution)/shard_map/ppermute | solution.py:943
  120.1 35.2 %collective-permute-start.12 = (bf16[384,1536]{1,0:T(8,128)(2,1)}, bf16[384,1536]{1,0:T(8,128)(2,1)}, u32[]{:S(2)}, u32[]{:S(2)}) collective-permute-start(bf16[384,1536]{1,0:T(8,128)(2,1)} %get-tuple-element.88), channel_id=1, source_target_pairs={{0,4},{2,6},{4,0},{6,2},{8,12},{10,14},{12,8},{14,10},{16,20},{18,... | collective-permute-start | bytes 3538952 | tf_op jit(solution)/shard_map/ppermute | solution.py:1015
  121.1 34.3 %collective-permute-start.13 = (bf16[384,1536]{1,0:T(8,128)(2,1)}, bf16[384,1536]{1,0:T(8,128)(2,1)}, u32[]{:S(2)}, u32[]{:S(2)}) collective-permute-start(bf16[384,1536]{1,0:T(8,128)(2,1)} %get-tuple-element.90), channel_id=1, source_target_pairs={{1,0},{2,3},{5,4},{6,7},{9,8},{10,11},{13,12},{14,15},{17,16},{18,... | collective-permute-start | bytes 3538952 | tf_op jit(solution)/shard_map/ppermute | solution.py:1046
  121.2 34.1 %collective-permute-start.14 = (bf16[384,1536]{1,0:T(8,128)(2,1)}, bf16[384,1536]{1,0:T(8,128)(2,1)}, u32[]{:S(2)}, u32[]{:S(2)}) collective-permute-start(bf16[384,1536]{1,0:T(8,128)(2,1)} %get-tuple-element.89), channel_id=1, source_target_pairs={{1,2},{2,1},{5,6},{6,5},{9,10},{10,9},{13,14},{14,13},{17,18},{18,... | collective-permute-start | bytes 3538952 | tf_op jit(solution)/shard_map/ppermute | solution.py:1047
  155.3 9.3 %collective-permute-start.15 = (bf16[1024,768]{1,0:T(8,128)(2,1)}, bf16[1024,768]{1,0:T(8,128)(2,1)}, u32[]{:S(2)}, u32[]{:S(2)}) collective-permute-start(bf16[1024,768]{1,0:T(8,128)(2,1)} %get-tuple-element.91.g_own), channel_id=1, source_target_pairs={{0,2},{2,0},{4,6},{6,4},{8,10},{10,8},{12,14},{14,12},{16,18},{18,... | collective-permute-start | bytes 4718600 | tf_op jit(solution)/shard_map/ppermute | solution.py:934
  162.5 17.6 %collective-permute-start.18 = (bf16[4,1,48,1536]{3,2,1,0:T(8,128)(2,1)}, bf16[4,1,48,1536]{3,2,1,0:T(8,128)(2,1)S(1)}, u32[]{:S(2)}, u32[]{:S(2)}) collective-permute-start(bf16[4,1,48,1536]{3,2,1,0:T(8,128)(2,1)} %get-tuple-element.172), channel_id=1, source_target_pairs={{1,0},{2,3},{5,4},{6,7},{9,8},{10,11},{13,12},{14,15},{17,16},{18,... | collective-permute-start | bytes 1769480 | tf_op jit(solution)/shard_map/ppermute | solution.py:1019
  162.5 17.6 %collective-permute-start.19 = (bf16[4,1,48,1536]{3,2,1,0:T(8,128)(2,1)}, bf16[4,1,48,1536]{3,2,1,0:T(8,128)(2,1)}, u32[]{:S(2)}, u32[]{:S(2)}) collective-permute-start(bf16[4,1,48,1536]{3,2,1,0:T(8,128)(2,1)} %get-tuple-element.171), channel_id=1, source_target_pairs={{1,2},{2,1},{5,6},{6,5},{9,10},{10,9},{13,14},{14,13},{17,18},{18,... | collective-permute-start | bytes 1769480 | tf_op jit(solution)/shard_map/ppermute | solution.py:1020
  164.2 35.7 %collective-permute-start.17 = (bf16[384,1664]{1,0:T(8,128)(2,1)}, bf16[384,1664]{1,0:T(8,128)(2,1)}, u32[]{:S(2)}, u32[]{:S(2)}) collective-permute-start(bf16[384,1664]{1,0:T(8,128)(2,1)} %get-tuple-element.96), channel_id=1, source_target_pairs={{0,4},{2,6},{4,0},{6,2},{8,12},{10,14},{12,8},{14,10},{16,20},{18,... | collective-permute-start | bytes 3833864 | tf_op jit(solution)/shard_map/ppermute | solution.py:1015
  171.5 40.8 %all-to-all-start.2 = ((bf16[32,16,768]{2,1,0:T(8,128)(2,1)}), bf16[32,16,768]{2,1,0:T(8,128)(2,1)S(1)}, u32[]{:S(2)}, u32[]{:S(2)}) async-start(bf16[32,16,768]{2,1,0:T(8,128)(2,1)} %bitcast.122), calls=%async_computation.2 | async-start | bytes 1572864 | tf_op jit(solution)/shard_map/all_to_all | solution.py:1075
  181.5 26.4 %collective-permute-start.22 = (bf16[1,1,48,1536]{3,2,1,0:T(8,128)(2,1)S(1)}, bf16[1,1,48,1536]{3,2,1,0:T(8,128)(2,1)S(1)}, u32[]{:S(2)}, u32[]{:S(2)}) collective-permute-start(bf16[1,1,48,1536]{3,2,1,0:T(8,128)(2,1)S(1)} %get-tuple-element.181), channel_id=1, source_target_pairs={{0,8},{2,10},{4,12},{6,14},{8,0},{10,2},{12,4},{14,6},{16,24},{18,... | collective-permute-start | bytes 442376 | tf_op jit(solution)/shard_map/ppermute | solution.py:1032
  181.8 27.6 %collective-permute-start.23 = (bf16[1,1,48,1536]{3,2,1,0:T(8,128)(2,1)S(1)}, bf16[1,1,48,1536]{3,2,1,0:T(8,128)(2,1)S(1)}, u32[]{:S(2)}, u32[]{:S(2)}) collective-permute-start(bf16[1,1,48,1536]{3,2,1,0:T(8,128)(2,1)S(1)} %get-tuple-element.180), channel_id=1, source_target_pairs={{0,16},{2,18},{4,20},{6,22},{8,24},{10,26},{12,28},{14,30},{16,0},... | collective-permute-start | bytes 442376 | tf_op jit(solution)/shard_map/ppermute | solution.py:1032
  184.5 27.7 %collective-permute-start.24 = (bf16[1,1,48,1536]{3,2,1,0:T(8,128)(2,1)S(1)}, bf16[1,1,48,1536]{3,2,1,0:T(8,128)(2,1)S(1)}, u32[]{:S(2)}, u32[]{:S(2)}) collective-permute-start(bf16[1,1,48,1536]{3,2,1,0:T(8,128)(2,1)S(1)} %get-tuple-element.179), channel_id=1, source_target_pairs={{0,24},{2,26},{4,28},{6,30},{8,16},{10,18},{12,20},{14,22},{16,8},... | collective-permute-start | bytes 442376 | tf_op jit(solution)/shard_map/ppermute | solution.py:1032
  201.0 20.7 %collective-permute-start.26 = (bf16[4,1,48,1536]{3,2,0,1:T(8,128)(2,1)}, bf16[4,1,48,1536]{3,2,0,1:T(8,128)(2,1)}, u32[]{:S(2)}, u32[]{:S(2)}) collective-permute-start(bf16[4,1,48,1536]{3,2,0,1:T(8,128)(2,1)} %get-tuple-element.169), channel_id=1, source_target_pairs={{0,4},{2,6},{4,0},{6,2},{8,12},{10,14},{12,8},{14,10},{16,20},{18,... | collective-permute-start | bytes 1769480 | tf_op jit(solution)/shard_map/ppermute | solution.py:1015
  204.5 19.3 %collective-permute-start.28 = (bf16[4,1,48,1664]{3,2,0,1:T(8,128)(2,1)}, bf16[4,1,48,1664]{3,2,0,1:T(8,128)(2,1)}, u32[]{:S(2)}, u32[]{:S(2)}) collective-permute-start(bf16[4,1,48,1664]{3,2,0,1:T(8,128)(2,1)} %get-tuple-element.165), channel_id=1, source_target_pairs={{1,0},{2,3},{5,4},{6,7},{9,8},{10,11},{13,12},{14,15},{17,16},{18,... | collective-permute-start | bytes 1916936 | tf_op jit(solution)/shard_map/ppermute | solution.py:1019
  207.9 15.9 %collective-permute-start.29 = (bf16[4,1,48,1664]{3,2,0,1:T(8,128)(2,1)}, bf16[4,1,48,1664]{3,2,0,1:T(8,128)(2,1)}, u32[]{:S(2)}, u32[]{:S(2)}) collective-permute-start(bf16[4,1,48,1664]{3,2,0,1:T(8,128)(2,1)} %get-tuple-element.164), channel_id=1, source_target_pairs={{1,2},{2,1},{5,6},{6,5},{9,10},{10,9},{13,14},{14,13},{17,18},{18,... | collective-permute-start | bytes 1916936 | tf_op jit(solution)/shard_map/ppermute | solution.py:1020
  209.4 20.5 %collective-permute-start.16 = (bf16[1024,768]{1,0:T(8,128)(2,1)}, bf16[1024,768]{1,0:T(8,128)(2,1)}, u32[]{:S(2)}, u32[]{:S(2)}) collective-permute-start(bf16[1024,768]{1,0:T(8,128)(2,1)} %get-tuple-element.94), channel_id=1, source_target_pairs={{0,2},{2,0},{4,6},{6,4},{8,10},{10,8},{12,14},{14,12},{16,18},{18,... | collective-permute-start | bytes 4718600 | tf_op jit(solution)/shard_map/ppermute | solution.py:934
  215.5 25.3 %all-to-all-start.3 = ((bf16[16,2,16,768]{3,2,1,0:T(8,128)(2,1)}), bf16[16,2,16,768]{3,2,1,0:T(8,128)(2,1)}, u32[]{:S(2)}, u32[]{:S(2)}) async-start(bf16[16,2,16,768]{3,2,1,0:T(8,128)(2,1)} %bitcast.25), calls=%async_computation.3 | async-start | bytes 1572864 | tf_op jit(solution)/shard_map/all_to_all | solution.py:1095
  221.7 11.0 %collective-permute-start.21 = (bf16[512,768]{1,0:T(8,128)(2,1)}, bf16[512,768]{1,0:T(8,128)(2,1)}, u32[]{:S(2)}, u32[]{:S(2)}) collective-permute-start(bf16[512,768]{1,0:T(8,128)(2,1)} %dynamic-slice_bitcast_fusion.1), channel_id=1, source_target_pairs={{0,1},{3,2},{4,5},{7,6},{8,9},{11,10},{12,13},{15,14},{16,17},{19,... | collective-permute-start | bytes 2359304 | tf_op jit(solution)/shard_map/ppermute | solution.py:943
  226.4 18.8 %collective-permute-start.30 = (bf16[1,1,48,3200]{3,2,1,0:T(8,128)(2,1)}, bf16[1,1,48,3200]{3,2,1,0:T(8,128)(2,1)S(1)}, u32[]{:S(2)}, u32[]{:S(2)}) collective-permute-start(bf16[1,1,48,3200]{3,2,1,0:T(8,128)(2,1)} %get-tuple-element.167), channel_id=1, source_target_pairs={{0,8},{2,10},{4,12},{6,14},{8,0},{10,2},{12,4},{14,6},{16,24},{18,... | collective-permute-start | bytes 921608 | tf_op jit(solution)/shard_map/ppermute | solution.py:1032
  226.6 33.2 %collective-permute-start.31 = (bf16[1,1,48,3200]{3,2,1,0:T(8,128)(2,1)}, bf16[1,1,48,3200]{3,2,1,0:T(8,128)(2,1)}, u32[]{:S(2)}, u32[]{:S(2)}) collective-permute-start(bf16[1,1,48,3200]{3,2,1,0:T(8,128)(2,1)} %get-tuple-element.168), channel_id=1, source_target_pairs={{0,16},{2,18},{4,20},{6,22},{8,24},{10,26},{12,28},{14,30},{16,0},... | collective-permute-start | bytes 921608 | tf_op jit(solution)/shard_map/ppermute | solution.py:1032
  229.3 38.5 %collective-permute-start.32 = (bf16[1,1,48,3200]{3,2,1,0:T(8,128)(2,1)S(1)}, bf16[1,1,48,3200]{3,2,1,0:T(8,128)(2,1)}, u32[]{:S(2)}, u32[]{:S(2)}) collective-permute-start(bf16[1,1,48,3200]{3,2,1,0:T(8,128)(2,1)S(1)} %get-tuple-element.166), channel_id=1, source_target_pairs={{0,24},{2,26},{4,28},{6,30},{8,16},{10,18},{12,20},{14,22},{16,8},... | collective-permute-start | bytes 921608 | tf_op jit(solution)/shard_map/ppermute | solution.py:1032
  232.5 41.6 %collective-permute-start.20 = (bf16[1024,768]{1,0:T(8,128)(2,1)S(1)}, bf16[1024,768]{1,0:T(8,128)(2,1)}, u32[]{:S(2)}, u32[]{:S(2)}) collective-permute-start(bf16[1024,768]{1,0:T(8,128)(2,1)S(1)} %add_convert_fusion), channel_id=1, source_target_pairs={{0,1},{3,2},{4,5},{7,6},{8,9},{11,10},{12,13},{15,14},{16,17},{19,... | collective-permute-start | bytes 4718600 | tf_op jit(solution)/shard_map/ppermute | solution.py:943
  242.8 32.6 %collective-permute-start.25 = (bf16[512,768]{1,0:T(8,128)(2,1)S(1)}, bf16[512,768]{1,0:T(8,128)(2,1)S(1)}, u32[]{:S(2)}, u32[]{:S(2)}) collective-permute-start(bf16[512,768]{1,0:T(8,128)(2,1)S(1)} %fusion), channel_id=1, source_target_pairs={{0,1},{1,0},{2,3},{3,2},{4,5},{5,4},{6,7},{7,6},{8,9},{9,8},{10,11... | collective-permute-start | bytes 2359304 | tf_op jit(solution)/shard_map/ppermute | solution.py:1102
  (31 other events, 171.2 us)

commit v3 on v2

--- a/solution.py
+++ b/solution.py
@@ -1049,9 +1049,10 @@
 
     def send_second(value):
         if not pair_first:
-            return send_pair(value)
+            return send_pair(value) + (value,)
         value = value.reshape(high, 2, mid, part_rows, -1)
-        return taken(value, across, 1), send_across(taken(value, 1 - across, 1))
+        away = taken(value, 1 - across, 1)
+        return taken(value, across, 1), send_across(away), away
 
     in_got = send_across(in_send)
     out_first = send_first(out_keep, out_send)
@@ -1078,8 +1079,8 @@
     sum_in = far(in_value)
     out_oth = swap(after(out_part, leaving))
     out_value = total(*after(out_first, in_value)).astype(BF16)
-    out_terms = send_second(out_value)
-    attn_value = total(*after(attn_first, out_value)).astype(BF16)
+    *out_terms, out_away = send_second(out_value)
+    attn_value = total(*after(attn_first, out_away)).astype(BF16)
     attn_terms = send_pair(attn_value)
     block = hidden + (out_part.astype(F32) + after(out_oth, attn_value).astype(F32)) + out_bias
     block = block.astype(BF16)

time: 279 us -> 278 us (level)
  waiting for transfers between devices: 73 us -> 69.1 us
  starting transfers between devices: 62.9 us -> 65.7 us
where the time goes in v3:
time: 278 us; the launch traced here: 276 us
  Pallas kernels  89.1 us (32%)
  waiting for transfers between devices  69.1 us (25%)
  starting transfers between devices  65.7 us (24%)
  other arithmetic  26 us (9%)
  local copies, waits for them, and re-layouts  24.1 us (9%)
    pallas_call x1, Pallas kernels, attention_back(): pl.pallas_call(functools.partial(attention_back_kernel, lead_rows, part_r...  29.9 us
    pallas_call x1, Pallas kernels, feed(): pl.pallas_call(functools.partial(feed_kernel, in_rows, out_rows), out_sha...  29.5 us
    ppermute x6, waiting for transfers between devices, far(): lax.ppermute(taken(value, spot ^ flip, 2), 'dp', [(d, d ^ flip << shift)...  24 us
    pallas_call x1, Pallas kernels, attention(): pl.pallas_call(attention_kernel, out_shape=(shape((rows, width), F32), ta...  20.7 us
    ppermute x7, waiting for transfers between devices, half_weight(): return lax.ppermute(value, both, weight_move)  16.2 us
    ppermute x3, waiting for transfers between devices, send_across(): return lax.ppermute(value, 'dp', [(d, d ^ 1 << lead) for d in all_dp])  10.1 us
    ppermute x9, starting transfers between devices, swap(): return lax.ppermute(value, 'dp', core_swap)  9.45 us
    all_to_all x1, waiting for transfers between devices, shards(): lax.all_to_all(chosen, both, 0, 0, tiled=True).reshape(rows // 2, width)  8.83 us
  transfers between devices with their start and end apart: 38, of which 13 were waited for; matrix products, arithmetic and copies ran while one was open for 16% of the time, Pallas kernels for 22%

profile of v3, /device:TPU:8, one launch (start us, length us, event | category | flops | bytes accessed | tf_op | source)
XLA Modules:
  0.0 275.8 jit_solution(13014421872321415625)
XLA Ops:
  2.2 2.1 copy_bitcast_fusion
  4.3 6.3 %all-to-all-start = ((bf16[16,2,16,768]{3,2,1,0:T(8,128)(2,1)}), bf16[16,2,16,768]{3,2,1,0:T(8,128)(2,1)S(1)}, u32[]{:S(2)}, u32[]{:S(2)}) async-start(bf16[16,2,16,768]{3,2,1,0:T(8,128)(2,1)} %copy_bitcast_fusion), calls=%async_computation | async-start | bytes 1572864 | tf_op jit(solution)/shard_map/all_to_all | solution.py:976
  11.4 2.4 dynamic-slice_bitcast_fusion
  14.5 8.1 %collective-permute-done = f32[2304]{0:T(1024)S(1)} collective-permute-done((f32[2304]{0:T(1024)S(1)}, f32[2304]{0:T(1024)S(1)}, u32[]{:S(2)}, u32[]{:S(2)}) %collective-permute-start) | collective-permute-done | bytes 9248 | tf_op jit(solution)/shard_map/ppermute | solution.py:943
  22.6 2.5 collective-permute-start.7
  25.1 3.9 %collective-permute-done.4.refs_1_.wp = bf16[384,768]{1,0:T(8,128)(2,1)S(1)} collective-permute-done((bf16[384,768]{1,0:T(8,128)(2,1)}, bf16[384,768]{1,0:T(8,128)(2,1)S(1)}, u32[]{:S(2)}, u32[]{:S(2)}) %collective-permute-start.4) | collective-permute-done | bytes 589856 | tf_op jit(solution)/shard_map/ppermute | solution.py:943
  31.8 6.6 %all-to-all-start.1 = ((bf16[32,16,768]{2,1,0:T(8,128)(2,1)}), bf16[32,16,768]{2,1,0:T(8,128)(2,1)}, u32[]{:S(2)}, u32[]{:S(2)}) async-start(bf16[32,16,768]{2,1,0:T(8,128)(2,1)} %copy-done.2), calls=%async_computation.1 | async-start | bytes 1572864 | tf_op jit(solution)/shard_map/all_to_all | solution.py:986
  41.6 3.5 %collective-permute-done.7.w_out_one = bf16[768,768]{1,0:T(8,128)(2,1)} collective-permute-done((bf16[768,768]{1,0:T(8,128)(2,1)}, bf16[768,768]{1,0:T(8,128)(2,1)}, u32[]{:S(2)}, u32[]{:S(2)}) %collective-permute-start.7) | collective-permute-done | bytes 1179680 | tf_op jit(solution)/shard_map/ppermute | solution.py:943
  48.9 8.8 %all-to-all-done.1 = bf16[32,16,768]{2,1,0:T(8,128)(2,1)} async-done(((bf16[32,16,768]{2,1,0:T(8,128)(2,1)}), bf16[32,16,768]{2,1,0:T(8,128)(2,1)}, u32[]{:S(2)}, u32[]{:S(2)}) %all-to-all-start.1) | async-done | bytes 786464 | tf_op jit(solution)/shard_map/all_to_all | solution.py:986
  64.4 20.7 %attention.1 = (f32[1024,768]{1,0:T(8,128)}, bf16[1024,768]{1,0:T(8,128)(2,1)}, bf16[1024,768]{1,0:T(8,128)(2,1)}, f32[1024,128]{1,0:T(8,128)}, bf16[1024,384]{1...) custom-call(f32[1]{0:T(128)} %slice.93.blend, ...), custom_call_target="tpu_custom_call" | custom-call | flops 1048576 | bytes 1048576 | tf_op jit(solution)/shard_map/attention/pallas_call | solution.py:290
  86.8 2.6 collective-permute-done.9.p_oth
  90.5 29.5 %feed.1 = (f32[1024,768]{1,0:T(8,128)}, bf16[1024,768]{1,0:T(8,128)(2,1)}, bf16[1024,768]{1,0:T(8,128)(2,1)}, bf16[384,1536]{1,0:T(8,128)(2,1)}, bf16[384,1536]{...) custom-call(s32[3]{0:T(128)} %pad_add_fusion.flags, ...), custom_call_target="tpu_custom_call" | custom-call | flops 1048576 | bytes 1048576 | tf_op jit(solution)/shard_map/feed/pallas_call | solution.py:496
  121.2 1.7 collective-permute-start.14
  125.4 29.9 %attention_back.1 = (f32[1024,768]{1,0:T(8,128)}, bf16[1024,768]{1,0:T(8,128)(2,1)}, bf16[384,1664]{1,0:T(8,128)(2,1)}, bf16[384,1664]{1,0:T(8,128)(2,1)}, f32[9,768]{1,0:T(8,128)}) custom-call(s32[3]{0:T(128)} %pad_add_fusion.flags, f32[5,768]{1,0:T(8,128)} %stack.46.vecs, f32[1,1024]{1,0:T(1,128)} %bitcast.128, f32[6,1024]{1,0:T(8,128)} %get-tuple-element.74.lse, ...), custom_call_target="tpu_custom_call" | custom-call | flops 1048576 | bytes 1048576 | tf_op jit(solution)/shard_map/attention_back/pallas_call | solution.py:776
  155.3 4.1 %collective-permute-start.15 = (bf16[1024,768]{1,0:T(8,128)(2,1)}, bf16[1024,768]{1,0:T(8,128)(2,1)}, u32[]{:S(2)}, u32[]{:S(2)}) collective-permute-start(bf16[1024,768]{1,0:T(8,128)(2,1)} %get-tuple-element.91.g_own), channel_id=1, source_target_pairs={{0,2},{2,0},{4,6},{6,4},{8,10},{10,8},{12,14},{14,12},{16,18},{18,... | collective-permute-start | bytes 4718600 | tf_op jit(solution)/shard_map/ppermute | solution.py:934
  159.5 1.9 add_convert_fusion.3
  164.6 6.9 %mixed_back.1 = (bf16[16,2,16,768]{3,2,1,0:T(8,128)(2,1)}, bf16[1024,768]{1,0:T(8,128)(2,1)}) custom-call(f32[1]{0:T(128)} %slice.93.blend, s32[3]{0:T(128)} %pad_add_fusion.flags, f32[5,768]{1,0:T(8,128)} %stack.46.vecs, f32[1024,768]{1,0:T(8,128)} %get-tuple-element.86.gh, bf16[1024,768]{1,0:T(8,128)(2,1)} %get-tuple-element.91.g_own, ...), custom_call_target="tpu_custom_call" | custom-call | flops 1048576 | bytes 1048576 | tf_op jit(solution)/shard_map/mixed_back/pallas_call | solution.py:874
  171.5 8.6 %all-to-all-start.2 = ((bf16[32,16,768]{2,1,0:T(8,128)(2,1)}), bf16[32,16,768]{2,1,0:T(8,128)(2,1)S(1)}, u32[]{:S(2)}, u32[]{:S(2)}) async-start(bf16[32,16,768]{2,1,0:T(8,128)(2,1)} %bitcast.122), calls=%async_computation.2 | async-start | bytes 1572864 | tf_op jit(solution)/shard_map/all_to_all | solution.py:1076
  181.8 2.7 collective-permute-start.23
  185.0 2.2 add_convert_fusion.2
  189.8 10.1 %collective-permute-done.17 = bf16[384,1664]{1,0:T(8,128)(2,1)} collective-permute-done((bf16[384,1664]{1,0:T(8,128)(2,1)}, bf16[384,1664]{1,0:T(8,128)(2,1)}, u32[]{:S(2)}, u32[]{:S(2)}) %collective-permute-start.17) | collective-permute-done | bytes 1277984 | tf_op jit(solution)/shard_map/ppermute | solution.py:1015
  199.9 1.6 add_convert_fusion.1.refs_0_
  202.8 3.7 %collective-permute-start.28 = (bf16[4,1,48,1664]{3,2,0,1:T(8,128)(2,1)}, bf16[4,1,48,1664]{3,2,0,1:T(8,128)(2,1)}, u32[]{:S(2)}, u32[]{:S(2)}) collective-permute-start(bf16[4,1,48,1664]{3,2,0,1:T(8,128)(2,1)} %get-tuple-element.165), channel_id=1, source_target_pairs={{1,0},{2,3},{5,4},{6,7},{9,8},{10,11},{13,12},{14,15},{17,16},{18,... | collective-permute-start | bytes 1916936 | tf_op jit(solution)/shard_map/ppermute | solution.py:1019
  209.0 2.1 collective-permute-start.16
  215.5 5.1 %all-to-all-start.3 = ((bf16[16,2,16,768]{3,2,1,0:T(8,128)(2,1)}), bf16[16,2,16,768]{3,2,1,0:T(8,128)(2,1)}, u32[]{:S(2)}, u32[]{:S(2)}) async-start(bf16[16,2,16,768]{3,2,1,0:T(8,128)(2,1)} %bitcast.27), calls=%async_computation.3 | async-start | bytes 1572864 | tf_op jit(solution)/shard_map/all_to_all | solution.py:1096
  222.8 1.7 fusion.1
  225.5 2.8 %collective-permute-start.31 = (bf16[1,1,48,3200]{3,2,1,0:T(8,128)(2,1)}, bf16[1,1,48,3200]{3,2,1,0:T(8,128)(2,1)}, u32[]{:S(2)}, u32[]{:S(2)}) collective-permute-start(bf16[1,1,48,3200]{3,2,1,0:T(8,128)(2,1)} %get-tuple-element.168), channel_id=1, source_target_pairs={{0,16},{2,18},{4,20},{6,22},{8,24},{10,26},{12,28},{14,30},{16,0},... | collective-permute-start | bytes 921608 | tf_op jit(solution)/shard_map/ppermute | solution.py:1032
  228.9 2.6 add_convert_fusion
  232.8 6.8 %all-to-all-done.3 = bf16[16,2,16,768]{3,2,1,0:T(8,128)(2,1)} async-done(((bf16[16,2,16,768]{3,2,1,0:T(8,128)(2,1)}), bf16[16,2,16,768]{3,2,1,0:T(8,128)(2,1)}, u32[]{:S(2)}, u32[]{:S(2)}) %all-to-all-start.3) | async-done | bytes 786464 | tf_op jit(solution)/shard_map/all_to_all | solution.py:1096
  241.7 2.1 collective-permute-start.25
  244.0 14.6 %collective-permute-done.31 = bf16[1,1,48,3200]{3,2,1,0:T(8,128)(2,1)} collective-permute-done((bf16[1,1,48,3200]{3,2,1,0:T(8,128)(2,1)}, bf16[1,1,48,3200]{3,2,1,0:T(8,128)(2,1)}, u32[]{:S(2)}, u32[]{:S(2)}) %collective-permute-start.31) | collective-permute-done | bytes 307232 | tf_op jit(solution)/shard_map/ppermute | solution.py:1032
  258.6 8.0 %collective-permute-done.32 = bf16[1,1,48,3200]{3,2,1,0:T(8,128)(2,1)} collective-permute-done((bf16[1,1,48,3200]{3,2,1,0:T(8,128)(2,1)S(1)}, bf16[1,1,48,3200]{3,2,1,0:T(8,128)(2,1)}, u32[]{:S(2)}, u32[]{:S(2)}) %collective-permute-start.32) | collective-permute-done | bytes 307232 | tf_op jit(solution)/shard_map/ppermute | solution.py:1032
  (169 shorter events, 57.8 us)
Async XLA Ops:
  0.6 28.9 %collective-permute-start.3 = (bf16[3,768,384]{2,1,0:T(8,128)(2,1)}, bf16[3,768,384]{2,1,0:T(8,128)(2,1)S(1)}, u32[]{:S(2)}, u32[]{:S(2)}) collective-permute-start(bf16[3,768,384]{2,1,0:T(8,128)(2,1)} %bitcast.130), channel_id=1, source_target_pairs={{0,1},{3,2},{4,5},{7,6},{8,9},{11,10},{12,13},{15,14},{16,17},{19,... | collective-permute-start | bytes 5308424 | tf_op jit(solution)/shard_map/ppermute | solution.py:943
  4.3 25.2 %all-to-all-start = ((bf16[16,2,16,768]{3,2,1,0:T(8,128)(2,1)}), bf16[16,2,16,768]{3,2,1,0:T(8,128)(2,1)S(1)}, u32[]{:S(2)}, u32[]{:S(2)}) async-start(bf16[16,2,16,768]{3,2,1,0:T(8,128)(2,1)} %copy_bitcast_fusion), calls=%async_computation | async-start | bytes 1572864 | tf_op jit(solution)/shard_map/all_to_all | solution.py:976
  10.6 36.8 %collective-permute-start.2 = (bf16[1024,768]{1,0:T(8,128)(2,1)}, bf16[1024,768]{1,0:T(8,128)(2,1)}, u32[]{:S(2)}, u32[]{:S(2)}) collective-permute-start(bf16[1024,768]{1,0:T(8,128)(2,1)} %param.17), channel_id=1, source_target_pairs={{0,2},{2,0},{4,6},{6,4},{8,10},{10,8},{12,14},{14,12},{16,18},{18,... | collective-permute-start | bytes 4718600 | tf_op jit(solution)/shard_map/ppermute | solution.py:934
  10.8 11.7 %collective-permute-start = (f32[2304]{0:T(1024)S(1)}, f32[2304]{0:T(1024)S(1)}, u32[]{:S(2)}, u32[]{:S(2)}) collective-permute-start(f32[2304]{0:T(1024)S(1)} %constant_dynamic-update-slice_fusion), channel_id=1, source_target_pairs={{0,1},{3,2},{4,5},{7,6},{8,9},{11,10},{12,13},{15,14},{16,17},{19,... | collective-permute-start | bytes 27656 | tf_op jit(solution)/shard_map/ppermute | solution.py:943
  10.9 18.1 %collective-permute-start.4 = (bf16[384,768]{1,0:T(8,128)(2,1)}, bf16[384,768]{1,0:T(8,128)(2,1)S(1)}, u32[]{:S(2)}, u32[]{:S(2)}) collective-permute-start(bf16[384,768]{1,0:T(8,128)(2,1)} %param.25), channel_id=1, source_target_pairs={{0,1},{3,2},{4,5},{7,6},{8,9},{11,10},{12,13},{15,14},{16,17},{19,... | collective-permute-start | bytes 1769480 | tf_op jit(solution)/shard_map/ppermute | solution.py:943
  11.2 34.6 %collective-permute-start.5 = (bf16[1024,768]{1,0:T(8,128)(2,1)}, bf16[1024,768]{1,0:T(8,128)(2,1)}, u32[]{:S(2)}, u32[]{:S(2)}) collective-permute-start(bf16[1024,768]{1,0:T(8,128)(2,1)} %param.33), channel_id=1, source_target_pairs={{0,2},{2,0},{4,6},{6,4},{8,10},{10,8},{12,14},{14,12},{16,18},{18,... | collective-permute-start | bytes 4718600 | tf_op jit(solution)/shard_map/ppermute | solution.py:934
  22.6 22.5 %collective-permute-start.7 = (bf16[768,768]{1,0:T(8,128)(2,1)}, bf16[768,768]{1,0:T(8,128)(2,1)}, u32[]{:S(2)}, u32[]{:S(2)}) collective-permute-start(bf16[768,768]{1,0:T(8,128)(2,1)} %dynamic-slice_bitcast_fusion), channel_id=1, source_target_pairs={{0,1},{3,2},{4,5},{7,6},{8,9},{11,10},{12,13},{15,14},{16,17},{19,... | collective-permute-start | bytes 3538952 | tf_op jit(solution)/shard_map/ppermute | solution.py:943
  31.8 26.0 %all-to-all-start.1 = ((bf16[32,16,768]{2,1,0:T(8,128)(2,1)}), bf16[32,16,768]{2,1,0:T(8,128)(2,1)}, u32[]{:S(2)}, u32[]{:S(2)}) async-start(bf16[32,16,768]{2,1,0:T(8,128)(2,1)} %copy-done.2), calls=%async_computation.1 | async-start | bytes 1572864 | tf_op jit(solution)/shard_map/all_to_all | solution.py:986
  45.1 18.3 %collective-permute-start.8 = (bf16[768,768]{1,0:T(8,128)(2,1)}, bf16[768,768]{1,0:T(8,128)(2,1)S(1)}, u32[]{:S(2)}, u32[]{:S(2)}) collective-permute-start(bf16[768,768]{1,0:T(8,128)(2,1)} %collective-permute-done.7.w_out_one), channel_id=1, source_target_pairs={{1,5},{2,6},{5,1},{6,2},{9,13},{10,14},{13,9},{14,10},{17,21},{18,... | collective-permute-start | bytes 3538952 | tf_op jit(solution)/shard_map/ppermute | solution.py:970
  59.3 27.4 %collective-permute-start.10 = (bf16[768,1536]{1,0:T(8,128)(2,1)}, bf16[768,1536]{1,0:T(8,128)(2,1)}, u32[]{:S(2)}, u32[]{:S(2)}) collective-permute-start(bf16[768,1536]{1,0:T(8,128)(2,1)} %param.29), channel_id=1, source_target_pairs={{0,1},{3,2},{4,5},{7,6},{8,9},{11,10},{12,13},{15,14},{16,17},{19,... | collective-permute-start | bytes 7077896 | tf_op jit(solution)/shard_map/ppermute | solution.py:943
  120.1 35.2 %collective-permute-start.12 = (bf16[384,1536]{1,0:T(8,128)(2,1)}, bf16[384,1536]{1,0:T(8,128)(2,1)}, u32[]{:S(2)}, u32[]{:S(2)}) collective-permute-start(bf16[384,1536]{1,0:T(8,128)(2,1)} %get-tuple-element.88), channel_id=1, source_target_pairs={{0,4},{2,6},{4,0},{6,2},{8,12},{10,14},{12,8},{14,10},{16,20},{18,... | collective-permute-start | bytes 3538952 | tf_op jit(solution)/shard_map/ppermute | solution.py:1015
  121.1 34.3 %collective-permute-start.13 = (bf16[384,1536]{1,0:T(8,128)(2,1)}, bf16[384,1536]{1,0:T(8,128)(2,1)}, u32[]{:S(2)}, u32[]{:S(2)}) collective-permute-start(bf16[384,1536]{1,0:T(8,128)(2,1)} %get-tuple-element.90), channel_id=1, source_target_pairs={{1,0},{2,3},{5,4},{6,7},{9,8},{10,11},{13,12},{14,15},{17,16},{18,... | collective-permute-start | bytes 3538952 | tf_op jit(solution)/shard_map/ppermute | solution.py:1046
  121.2 34.1 %collective-permute-start.14 = (bf16[384,1536]{1,0:T(8,128)(2,1)}, bf16[384,1536]{1,0:T(8,128)(2,1)}, u32[]{:S(2)}, u32[]{:S(2)}) collective-permute-start(bf16[384,1536]{1,0:T(8,128)(2,1)} %get-tuple-element.89), channel_id=1, source_target_pairs={{1,2},{2,1},{5,6},{6,5},{9,10},{10,9},{13,14},{14,13},{17,18},{18,... | collective-permute-start | bytes 3538952 | tf_op jit(solution)/shard_map/ppermute | solution.py:1047
  155.3 9.2 %collective-permute-start.15 = (bf16[1024,768]{1,0:T(8,128)(2,1)}, bf16[1024,768]{1,0:T(8,128)(2,1)}, u32[]{:S(2)}, u32[]{:S(2)}) collective-permute-start(bf16[1024,768]{1,0:T(8,128)(2,1)} %get-tuple-element.91.g_own), channel_id=1, source_target_pairs={{0,2},{2,0},{4,6},{6,4},{8,10},{10,8},{12,14},{14,12},{16,18},{18,... | collective-permute-start | bytes 4718600 | tf_op jit(solution)/shard_map/ppermute | solution.py:934
  162.5 17.6 %collective-permute-start.18 = (bf16[4,1,48,1536]{3,2,1,0:T(8,128)(2,1)}, bf16[4,1,48,1536]{3,2,1,0:T(8,128)(2,1)S(1)}, u32[]{:S(2)}, u32[]{:S(2)}) collective-permute-start(bf16[4,1,48,1536]{3,2,1,0:T(8,128)(2,1)} %get-tuple-element.172), channel_id=1, source_target_pairs={{1,0},{2,3},{5,4},{6,7},{9,8},{10,11},{13,12},{14,15},{17,16},{18,... | collective-permute-start | bytes 1769480 | tf_op jit(solution)/shard_map/ppermute | solution.py:1019
  162.5 17.6 %collective-permute-start.19 = (bf16[4,1,48,1536]{3,2,1,0:T(8,128)(2,1)}, bf16[4,1,48,1536]{3,2,1,0:T(8,128)(2,1)}, u32[]{:S(2)}, u32[]{:S(2)}) collective-permute-start(bf16[4,1,48,1536]{3,2,1,0:T(8,128)(2,1)} %get-tuple-element.171), channel_id=1, source_target_pairs={{1,2},{2,1},{5,6},{6,5},{9,10},{10,9},{13,14},{14,13},{17,18},{18,... | collective-permute-start | bytes 1769480 | tf_op jit(solution)/shard_map/ppermute | solution.py:1020
  164.2 35.7 %collective-permute-start.17 = (bf16[384,1664]{1,0:T(8,128)(2,1)}, bf16[384,1664]{1,0:T(8,128)(2,1)}, u32[]{:S(2)}, u32[]{:S(2)}) collective-permute-start(bf16[384,1664]{1,0:T(8,128)(2,1)} %get-tuple-element.96), channel_id=1, source_target_pairs={{0,4},{2,6},{4,0},{6,2},{8,12},{10,14},{12,8},{14,10},{16,20},{18,... | collective-permute-start | bytes 3833864 | tf_op jit(solution)/shard_map/ppermute | solution.py:1015
  171.5 40.8 %all-to-all-start.2 = ((bf16[32,16,768]{2,1,0:T(8,128)(2,1)}), bf16[32,16,768]{2,1,0:T(8,128)(2,1)S(1)}, u32[]{:S(2)}, u32[]{:S(2)}) async-start(bf16[32,16,768]{2,1,0:T(8,128)(2,1)} %bitcast.122), calls=%async_computation.2 | async-start | bytes 1572864 | tf_op jit(solution)/shard_map/all_to_all | solution.py:1076
  181.5 25.9 %collective-permute-start.22 = (bf16[1,1,48,1536]{3,2,1,0:T(8,128)(2,1)S(1)}, bf16[1,1,48,1536]{3,2,1,0:T(8,128)(2,1)S(1)}, u32[]{:S(2)}, u32[]{:S(2)}) collective-permute-start(bf16[1,1,48,1536]{3,2,1,0:T(8,128)(2,1)S(1)} %get-tuple-element.181), channel_id=1, source_target_pairs={{0,8},{2,10},{4,12},{6,14},{8,0},{10,2},{12,4},{14,6},{16,24},{18,... | collective-permute-start | bytes 442376 | tf_op jit(solution)/shard_map/ppermute | solution.py:1032
  181.8 27.1 %collective-permute-start.23 = (bf16[1,1,48,1536]{3,2,1,0:T(8,128)(2,1)S(1)}, bf16[1,1,48,1536]{3,2,1,0:T(8,128)(2,1)S(1)}, u32[]{:S(2)}, u32[]{:S(2)}) collective-permute-start(bf16[1,1,48,1536]{3,2,1,0:T(8,128)(2,1)S(1)} %get-tuple-element.180), channel_id=1, source_target_pairs={{0,16},{2,18},{4,20},{6,22},{8,24},{10,26},{12,28},{14,30},{16,0},... | collective-permute-start | bytes 442376 | tf_op jit(solution)/shard_map/ppermute | solution.py:1032
  184.5 27.7 %collective-permute-start.24 = (bf16[1,1,48,1536]{3,2,1,0:T(8,128)(2,1)S(1)}, bf16[1,1,48,1536]{3,2,1,0:T(8,128)(2,1)S(1)}, u32[]{:S(2)}, u32[]{:S(2)}) collective-permute-start(bf16[1,1,48,1536]{3,2,1,0:T(8,128)(2,1)S(1)} %get-tuple-element.179), channel_id=1, source_target_pairs={{0,24},{2,26},{4,28},{6,30},{8,16},{10,18},{12,20},{14,22},{16,8},... | collective-permute-start | bytes 442376 | tf_op jit(solution)/shard_map/ppermute | solution.py:1032
  188.3 32.2 %collective-permute-start.26 = (bf16[4,1,48,1536]{3,2,0,1:T(8,128)(2,1)}, bf16[4,1,48,1536]{3,2,0,1:T(8,128)(2,1)}, u32[]{:S(2)}, u32[]{:S(2)}) collective-permute-start(bf16[4,1,48,1536]{3,2,0,1:T(8,128)(2,1)} %get-tuple-element.170), channel_id=1, source_target_pairs={{0,4},{2,6},{4,0},{6,2},{8,12},{10,14},{12,8},{14,10},{16,20},{18,... | collective-permute-start | bytes 1769480 | tf_op jit(solution)/shard_map/ppermute | solution.py:1015
  202.8 20.0 %collective-permute-start.28 = (bf16[4,1,48,1664]{3,2,0,1:T(8,128)(2,1)}, bf16[4,1,48,1664]{3,2,0,1:T(8,128)(2,1)}, u32[]{:S(2)}, u32[]{:S(2)}) collective-permute-start(bf16[4,1,48,1664]{3,2,0,1:T(8,128)(2,1)} %get-tuple-element.165), channel_id=1, source_target_pairs={{1,0},{2,3},{5,4},{6,7},{9,8},{10,11},{13,12},{14,15},{17,16},{18,... | collective-permute-start | bytes 1916936 | tf_op jit(solution)/shard_map/ppermute | solution.py:1019
  207.4 15.4 %collective-permute-start.29 = (bf16[4,1,48,1664]{3,2,0,1:T(8,128)(2,1)}, bf16[4,1,48,1664]{3,2,0,1:T(8,128)(2,1)}, u32[]{:S(2)}, u32[]{:S(2)}) collective-permute-start(bf16[4,1,48,1664]{3,2,0,1:T(8,128)(2,1)} %get-tuple-element.164), channel_id=1, source_target_pairs={{1,2},{2,1},{5,6},{6,5},{9,10},{10,9},{13,14},{14,13},{17,18},{18,... | collective-permute-start | bytes 1916936 | tf_op jit(solution)/shard_map/ppermute | solution.py:1020
  209.0 20.0 %collective-permute-start.16 = (bf16[1024,768]{1,0:T(8,128)(2,1)}, bf16[1024,768]{1,0:T(8,128)(2,1)}, u32[]{:S(2)}, u32[]{:S(2)}) collective-permute-start(bf16[1024,768]{1,0:T(8,128)(2,1)} %get-tuple-element.94), channel_id=1, source_target_pairs={{0,2},{2,0},{4,6},{6,4},{8,10},{10,8},{12,14},{14,12},{16,18},{18,... | collective-permute-start | bytes 4718600 | tf_op jit(solution)/shard_map/ppermute | solution.py:934
  215.5 24.2 %all-to-all-start.3 = ((bf16[16,2,16,768]{3,2,1,0:T(8,128)(2,1)}), bf16[16,2,16,768]{3,2,1,0:T(8,128)(2,1)}, u32[]{:S(2)}, u32[]{:S(2)}) async-start(bf16[16,2,16,768]{3,2,1,0:T(8,128)(2,1)} %bitcast.27), calls=%async_computation.3 | async-start | bytes 1572864 | tf_op jit(solution)/shard_map/all_to_all | solution.py:1096
  220.6 12.3 %collective-permute-start.21 = (bf16[512,768]{1,0:T(8,128)(2,1)}, bf16[512,768]{1,0:T(8,128)(2,1)}, u32[]{:S(2)}, u32[]{:S(2)}) collective-permute-start(bf16[512,768]{1,0:T(8,128)(2,1)} %dynamic-slice_bitcast_fusion.1), channel_id=1, source_target_pairs={{0,1},{3,2},{4,5},{7,6},{8,9},{11,10},{12,13},{15,14},{16,17},{19,... | collective-permute-start | bytes 2359304 | tf_op jit(solution)/shard_map/ppermute | solution.py:943
  225.4 18.6 %collective-permute-start.30 = (bf16[1,1,48,3200]{3,2,1,0:T(8,128)(2,1)}, bf16[1,1,48,3200]{3,2,1,0:T(8,128)(2,1)S(1)}, u32[]{:S(2)}, u32[]{:S(2)}) collective-permute-start(bf16[1,1,48,3200]{3,2,1,0:T(8,128)(2,1)} %get-tuple-element.167), channel_id=1, source_target_pairs={{0,8},{2,10},{4,12},{6,14},{8,0},{10,2},{12,4},{14,6},{16,24},{18,... | collective-permute-start | bytes 921608 | tf_op jit(solution)/shard_map/ppermute | solution.py:1032
  225.5 33.1 %collective-permute-start.31 = (bf16[1,1,48,3200]{3,2,1,0:T(8,128)(2,1)}, bf16[1,1,48,3200]{3,2,1,0:T(8,128)(2,1)}, u32[]{:S(2)}, u32[]{:S(2)}) collective-permute-start(bf16[1,1,48,3200]{3,2,1,0:T(8,128)(2,1)} %get-tuple-element.168), channel_id=1, source_target_pairs={{0,16},{2,18},{4,20},{6,22},{8,24},{10,26},{12,28},{14,30},{16,0},... | collective-permute-start | bytes 921608 | tf_op jit(solution)/shard_map/ppermute | solution.py:1032
  228.3 38.4 %collective-permute-start.32 = (bf16[1,1,48,3200]{3,2,1,0:T(8,128)(2,1)S(1)}, bf16[1,1,48,3200]{3,2,1,0:T(8,128)(2,1)}, u32[]{:S(2)}, u32[]{:S(2)}) collective-permute-start(bf16[1,1,48,3200]{3,2,1,0:T(8,128)(2,1)S(1)} %get-tuple-element.166), channel_id=1, source_target_pairs={{0,24},{2,26},{4,28},{6,30},{8,16},{10,18},{12,20},{14,22},{16,8},... | collective-permute-start | bytes 921608 | tf_op jit(solution)/shard_map/ppermute | solution.py:1032
  231.5 41.5 %collective-permute-start.20 = (bf16[1024,768]{1,0:T(8,128)(2,1)S(1)}, bf16[1024,768]{1,0:T(8,128)(2,1)}, u32[]{:S(2)}, u32[]{:S(2)}) collective-permute-start(bf16[1024,768]{1,0:T(8,128)(2,1)S(1)} %add_convert_fusion), channel_id=1, source_target_pairs={{0,1},{3,2},{4,5},{7,6},{8,9},{11,10},{12,13},{15,14},{16,17},{19,... | collective-permute-start | bytes 4718600 | tf_op jit(solution)/shard_map/ppermute | solution.py:943
  241.7 32.7 %collective-permute-start.25 = (bf16[512,768]{1,0:T(8,128)(2,1)S(1)}, bf16[512,768]{1,0:T(8,128)(2,1)S(1)}, u32[]{:S(2)}, u32[]{:S(2)}) collective-permute-start(bf16[512,768]{1,0:T(8,128)(2,1)S(1)} %fusion), channel_id=1, source_target_pairs={{0,1},{1,0},{2,3},{3,2},{4,5},{5,4},{6,7},{7,6},{8,9},{9,8},{10,11... | collective-permute-start | bytes 2359304 | tf_op jit(solution)/shard_map/ppermute | solution.py:1103
  (31 other events, 166.7 us)

commit v4 on v3

--- a/solution.py
+++ b/solution.py
@@ -1109,7 +1109,7 @@
     marker = swap(returning[0, :, :LANES])
     summed = far(
         side_by_side(*(after(terms, marker) for terms in (out_terms, attn_terms))),
-        mine,
+        block_out,
     )
     sum_out, sum_attn = after(summed[:, :units], other), summed[:, units:]
     sum_qkv = sum_attn[:, : 3 * local].reshape(-1, 3, local)

time: 278 us -> 277 us (level)
    ppermute x7, waiting for transfers between devices: 16.2 us -> 24.7 us  [half_weight(): return lax.ppermute(value, both, weight_move)]
    ppermute x6, waiting for transfers between devices: 24 us -> 17.1 us  [far(): lax.ppermute(taken(value, spot ^ flip, 2), 'dp', [(d, d ^ flip << shift)...]
    all_to_all x1, waiting for transfers between devices: 6.83 us -> 3.05 us  [shards(): lax.all_to_all(returning.reshape(dp_count, 2, piece, width), 'dp', 0, 0,...]
    ppermute x2, starting transfers between devices: 3.73 us -> 0.04 us  [send_pair(): lax.ppermute(taken(value, jnp.where(home, 1 - core, core), 2), both, pair...]
  transfers between devices with their start and end apart: 38 -> 38, of which waited for: 13 -> 14; matrix products, arithmetic and copies ran while one was open for 16% -> 16% of each run, Pallas kernels for 22% -> 22%
where the time goes in v4:
time: 277 us; the launch traced here: 276 us
  Pallas kernels  89.1 us (32%)
  waiting for transfers between devices  67.7 us (24%)
  starting transfers between devices  66.3 us (24%)
  other arithmetic  26.8 us (10%)
  local copies, waits for them, and re-layouts  23.9 us (9%)
    pallas_call x1, Pallas kernels, attention_back(): pl.pallas_call(functools.partial(attention_back_kernel, lead_rows, part_r...  29.9 us
    pallas_call x1, Pallas kernels, feed(): pl.pallas_call(functools.partial(feed_kernel, in_rows, out_rows), out_sha...  29.5 us
    ppermute x7, waiting for transfers between devices, half_weight(): return lax.ppermute(value, both, weight_move)  24.7 us
    pallas_call x1, Pallas kernels, attention(): pl.pallas_call(attention_kernel, out_shape=(shape((rows, width), F32), ta...  20.7 us
    ppermute x6, waiting for transfers between devices, far(): lax.ppermute(taken(value, spot ^ flip, 2), 'dp', [(d, d ^ flip << shift)...  17.1 us
    ppermute x9, starting transfers between devices, swap(): return lax.ppermute(value, 'dp', core_swap)  11 us
    ppermute x3, waiting for transfers between devices, send_across(): return lax.ppermute(value, 'dp', [(d, d ^ 1 << lead) for d in all_dp])  10.1 us
    ppermute x7, starting transfers between devices, half_weight(): return lax.ppermute(value, both, weight_move)  9.43 us
  transfers between devices with their start and end apart: 38, of which 14 were waited for; matrix products, arithmetic and copies ran while one was open for 16% of the time, Pallas kernels for 22%

profile of v4, /device:TPU:8, one launch (start us, length us, event | category | flops | bytes accessed | tf_op | source)
XLA Modules:
  0.0 275.8 jit_solution(7605634587187137991)
XLA Ops:
  2.2 2.1 copy_bitcast_fusion
  4.3 6.3 %all-to-all-start = ((bf16[16,2,16,768]{3,2,1,0:T(8,128)(2,1)}), bf16[16,2,16,768]{3,2,1,0:T(8,128)(2,1)S(1)}, u32[]{:S(2)}, u32[]{:S(2)}) async-start(bf16[16,2,16,768]{3,2,1,0:T(8,128)(2,1)} %copy_bitcast_fusion), calls=%async_computation | async-start | bytes 1572864 | tf_op jit(solution)/shard_map/all_to_all | solution.py:976
  11.4 2.4 dynamic-slice_bitcast_fusion
  14.5 8.1 %collective-permute-done = f32[2304]{0:T(1024)S(1)} collective-permute-done((f32[2304]{0:T(1024)S(1)}, f32[2304]{0:T(1024)S(1)}, u32[]{:S(2)}, u32[]{:S(2)}) %collective-permute-start) | collective-permute-done | bytes 9248 | tf_op jit(solution)/shard_map/ppermute | solution.py:943
  22.6 2.5 collective-permute-start.7
  25.1 3.9 %collective-permute-done.4.refs_1_.wp = bf16[384,768]{1,0:T(8,128)(2,1)S(1)} collective-permute-done((bf16[384,768]{1,0:T(8,128)(2,1)}, bf16[384,768]{1,0:T(8,128)(2,1)S(1)}, u32[]{:S(2)}, u32[]{:S(2)}) %collective-permute-start.4) | collective-permute-done | bytes 589856 | tf_op jit(solution)/shard_map/ppermute | solution.py:943
  31.7 6.6 %all-to-all-start.1 = ((bf16[32,16,768]{2,1,0:T(8,128)(2,1)}), bf16[32,16,768]{2,1,0:T(8,128)(2,1)}, u32[]{:S(2)}, u32[]{:S(2)}) async-start(bf16[32,16,768]{2,1,0:T(8,128)(2,1)} %copy-done.2), calls=%async_computation.1 | async-start | bytes 1572864 | tf_op jit(solution)/shard_map/all_to_all | solution.py:986
  41.6 3.5 %collective-permute-done.7.w_out_one = bf16[768,768]{1,0:T(8,128)(2,1)} collective-permute-done((bf16[768,768]{1,0:T(8,128)(2,1)}, bf16[768,768]{1,0:T(8,128)(2,1)}, u32[]{:S(2)}, u32[]{:S(2)}) %collective-permute-start.7) | collective-permute-done | bytes 1179680 | tf_op jit(solution)/shard_map/ppermute | solution.py:943
  48.9 8.8 %all-to-all-done.1 = bf16[32,16,768]{2,1,0:T(8,128)(2,1)} async-done(((bf16[32,16,768]{2,1,0:T(8,128)(2,1)}), bf16[32,16,768]{2,1,0:T(8,128)(2,1)}, u32[]{:S(2)}, u32[]{:S(2)}) %all-to-all-start.1) | async-done | bytes 786464 | tf_op jit(solution)/shard_map/all_to_all | solution.py:986
  64.4 20.7 %attention.1 = (f32[1024,768]{1,0:T(8,128)}, bf16[1024,768]{1,0:T(8,128)(2,1)}, bf16[1024,768]{1,0:T(8,128)(2,1)}, f32[1024,128]{1,0:T(8,128)}, bf16[1024,384]{1...) custom-call(f32[1]{0:T(128)} %slice.93.blend, ...), custom_call_target="tpu_custom_call" | custom-call | flops 1048576 | bytes 1048576 | tf_op jit(solution)/shard_map/attention/pallas_call | solution.py:290
  86.8 2.6 collective-permute-done.9.p_oth
  90.5 29.5 %feed.1 = (f32[1024,768]{1,0:T(8,128)}, bf16[1024,768]{1,0:T(8,128)(2,1)}, bf16[1024,768]{1,0:T(8,128)(2,1)}, bf16[384,1536]{1,0:T(8,128)(2,1)}, bf16[384,1536]{...) custom-call(s32[3]{0:T(128)} %pad_add_fusion.flags, ...), custom_call_target="tpu_custom_call" | custom-call | flops 1048576 | bytes 1048576 | tf_op jit(solution)/shard_map/feed/pallas_call | solution.py:496
  121.2 1.7 collective-permute-start.14
  125.4 29.9 %attention_back.1 = (f32[1024,768]{1,0:T(8,128)}, bf16[1024,768]{1,0:T(8,128)(2,1)}, bf16[384,1664]{1,0:T(8,128)(2,1)}, bf16[384,1664]{1,0:T(8,128)(2,1)}, f32[9,768]{1,0:T(8,128)}) custom-call(s32[3]{0:T(128)} %pad_add_fusion.flags, f32[5,768]{1,0:T(8,128)} %stack.46.vecs, f32[1,1024]{1,0:T(1,128)} %bitcast.128, f32[6,1024]{1,0:T(8,128)} %get-tuple-element.74.lse, ...), custom_call_target="tpu_custom_call" | custom-call | flops 1048576 | bytes 1048576 | tf_op jit(solution)/shard_map/attention_back/pallas_call | solution.py:776
  155.4 4.1 %collective-permute-start.15 = (bf16[1024,768]{1,0:T(8,128)(2,1)}, bf16[1024,768]{1,0:T(8,128)(2,1)}, u32[]{:S(2)}, u32[]{:S(2)}) collective-permute-start(bf16[1024,768]{1,0:T(8,128)(2,1)} %get-tuple-element.91.g_own), channel_id=1, source_target_pairs={{0,2},{2,0},{4,6},{6,4},{8,10},{10,8},{12,14},{14,12},{16,18},{18,... | collective-permute-start | bytes 4718600 | tf_op jit(solution)/shard_map/ppermute | solution.py:934
  159.5 1.9 add_convert_fusion.3
  164.6 6.9 %mixed_back.1 = (bf16[16,2,16,768]{3,2,1,0:T(8,128)(2,1)}, bf16[1024,768]{1,0:T(8,128)(2,1)}) custom-call(f32[1]{0:T(128)} %slice.93.blend, s32[3]{0:T(128)} %pad_add_fusion.flags, f32[5,768]{1,0:T(8,128)} %stack.46.vecs, f32[1024,768]{1,0:T(8,128)} %get-tuple-element.86.gh, bf16[1024,768]{1,0:T(8,128)(2,1)} %get-tuple-element.91.g_own, ...), custom_call_target="tpu_custom_call" | custom-call | flops 1048576 | bytes 1048576 | tf_op jit(solution)/shard_map/mixed_back/pallas_call | solution.py:874
  171.5 8.6 %all-to-all-start.2 = ((bf16[32,16,768]{2,1,0:T(8,128)(2,1)}), bf16[32,16,768]{2,1,0:T(8,128)(2,1)S(1)}, u32[]{:S(2)}, u32[]{:S(2)}) async-start(bf16[32,16,768]{2,1,0:T(8,128)(2,1)} %bitcast.122), calls=%async_computation.2 | async-start | bytes 1572864 | tf_op jit(solution)/shard_map/all_to_all | solution.py:1076
  181.8 2.7 collective-permute-start.23
  185.1 2.2 add_convert_fusion.2
  189.8 10.1 %collective-permute-done.17 = bf16[384,1664]{1,0:T(8,128)(2,1)} collective-permute-done((bf16[384,1664]{1,0:T(8,128)(2,1)}, bf16[384,1664]{1,0:T(8,128)(2,1)}, u32[]{:S(2)}, u32[]{:S(2)}) %collective-permute-start.17) | collective-permute-done | bytes 1277984 | tf_op jit(solution)/shard_map/ppermute | solution.py:1015
  199.9 3.7 %collective-permute-start.16 = (bf16[1024,768]{1,0:T(8,128)(2,1)}, bf16[1024,768]{1,0:T(8,128)(2,1)}, u32[]{:S(2)}, u32[]{:S(2)}) collective-permute-start(bf16[1024,768]{1,0:T(8,128)(2,1)} %get-tuple-element.94), channel_id=1, source_target_pairs={{0,2},{2,0},{4,6},{6,4},{8,10},{10,8},{12,14},{14,12},{16,18},{18,... | collective-permute-start | bytes 4718600 | tf_op jit(solution)/shard_map/ppermute | solution.py:934
  203.6 1.6 add_convert_fusion.1.refs_0_
  208.8 3.3 %collective-permute-done.24 = bf16[1,1,48,1536]{3,2,1,0:T(8,128)(2,1)S(1)} collective-permute-done((bf16[1,1,48,1536]{3,2,1,0:T(8,128)(2,1)S(1)}, bf16[1,1,48,1536]{3,2,1,0:T(8,128)(2,1)S(1)}, u32[]{:S(2)}, u32[]{:S(2)}) %collective-permute-start.24) | collective-permute-done | bytes 147488 | tf_op jit(solution)/shard_map/ppermute | solution.py:1032
  215.4 6.3 %all-to-all-start.3 = ((bf16[16,2,16,768]{3,2,1,0:T(8,128)(2,1)}), bf16[16,2,16,768]{3,2,1,0:T(8,128)(2,1)}, u32[]{:S(2)}, u32[]{:S(2)}) async-start(bf16[16,2,16,768]{3,2,1,0:T(8,128)(2,1)} %bitcast.27), calls=%async_computation.3 | async-start | bytes 1572864 | tf_op jit(solution)/shard_map/all_to_all | solution.py:1096
  223.6 3.5 %add_convert_fusion = bf16[1024,768]{1,0:T(8,128)(2,1)S(1)} fusion(f32[1024,768]{1,0:T(8,128)} %get-tuple-element.72, bf16[1024,768]{1,0:T(8,128)(2,1)} %collective-permute-done.16, bf16[1024,768]{1,0:T(8,128)(2,1)} %get-tuple-element.94, f32[768]{0:T(1024)S(1)} %copy-done.16), kind=kLoop, calls=%fused_computation.2 | loop fusion | flops 4718592 | bytes 7867392 | tf_op jit(solution)/shard_map/convert_element_type | solution.py:1086
  227.1 4.0 %collective-permute-start.20 = (bf16[1024,768]{1,0:T(8,128)(2,1)S(1)}, bf16[1024,768]{1,0:T(8,128)(2,1)}, u32[]{:S(2)}, u32[]{:S(2)}) collective-permute-start(bf16[1024,768]{1,0:T(8,128)(2,1)S(1)} %add_convert_fusion), channel_id=1, source_target_pairs={{0,1},{3,2},{4,5},{7,6},{8,9},{11,10},{12,13},{15,14},{16,17},{19,... | collective-permute-start | bytes 4718600 | tf_op jit(solution)/shard_map/ppermute | solution.py:943
  234.4 2.9 %collective-permute-start.31 = (bf16[1,1,48,3200]{3,2,1,0:T(8,128)(2,1)}, bf16[1,1,48,3200]{3,2,1,0:T(8,128)(2,1)}, u32[]{:S(2)}, u32[]{:S(2)}) collective-permute-start(bf16[1,1,48,3200]{3,2,1,0:T(8,128)(2,1)} %get-tuple-element.168), channel_id=1, source_target_pairs={{0,16},{2,18},{4,20},{6,22},{8,24},{10,26},{12,28},{14,30},{16,0},... | collective-permute-start | bytes 921608 | tf_op jit(solution)/shard_map/ppermute | solution.py:1032
  237.8 3.0 %all-to-all-done.3 = bf16[16,2,16,768]{3,2,1,0:T(8,128)(2,1)} async-done(((bf16[16,2,16,768]{3,2,1,0:T(8,128)(2,1)}), bf16[16,2,16,768]{3,2,1,0:T(8,128)(2,1)}, u32[]{:S(2)}, u32[]{:S(2)}) %all-to-all-start.3) | async-done | bytes 786464 | tf_op jit(solution)/shard_map/all_to_all | solution.py:1096
  244.3 8.5 %collective-permute-done.20 = bf16[1024,768]{1,0:T(8,128)(2,1)} collective-permute-done((bf16[1024,768]{1,0:T(8,128)(2,1)S(1)}, bf16[1024,768]{1,0:T(8,128)(2,1)}, u32[]{:S(2)}, u32[]{:S(2)}) %collective-permute-start.20) | collective-permute-done | bytes 1572896 | tf_op jit(solution)/shard_map/ppermute | solution.py:943
  254.1 5.7 %collective-permute-done.31 = bf16[1,1,48,3200]{3,2,1,0:T(8,128)(2,1)} collective-permute-done((bf16[1,1,48,3200]{3,2,1,0:T(8,128)(2,1)}, bf16[1,1,48,3200]{3,2,1,0:T(8,128)(2,1)}, u32[]{:S(2)}, u32[]{:S(2)}) %collective-permute-start.31) | collective-permute-done | bytes 307232 | tf_op jit(solution)/shard_map/ppermute | solution.py:1032
  259.8 8.1 %collective-permute-done.32 = bf16[1,1,48,3200]{3,2,1,0:T(8,128)(2,1)} collective-permute-done((bf16[1,1,48,3200]{3,2,1,0:T(8,128)(2,1)S(1)}, bf16[1,1,48,3200]{3,2,1,0:T(8,128)(2,1)}, u32[]{:S(2)}, u32[]{:S(2)}) %collective-permute-start.32) | collective-permute-done | bytes 307232 | tf_op jit(solution)/shard_map/ppermute | solution.py:1032
  (167 shorter events, 58.4 us)
Async XLA Ops:
  0.6 28.9 %collective-permute-start.3 = (bf16[3,768,384]{2,1,0:T(8,128)(2,1)}, bf16[3,768,384]{2,1,0:T(8,128)(2,1)S(1)}, u32[]{:S(2)}, u32[]{:S(2)}) collective-permute-start(bf16[3,768,384]{2,1,0:T(8,128)(2,1)} %bitcast.130), channel_id=1, source_target_pairs={{0,1},{3,2},{4,5},{7,6},{8,9},{11,10},{12,13},{15,14},{16,17},{19,... | collective-permute-start | bytes 5308424 | tf_op jit(solution)/shard_map/ppermute | solution.py:943
  4.3 25.2 %all-to-all-start = ((bf16[16,2,16,768]{3,2,1,0:T(8,128)(2,1)}), bf16[16,2,16,768]{3,2,1,0:T(8,128)(2,1)S(1)}, u32[]{:S(2)}, u32[]{:S(2)}) async-start(bf16[16,2,16,768]{3,2,1,0:T(8,128)(2,1)} %copy_bitcast_fusion), calls=%async_computation | async-start | bytes 1572864 | tf_op jit(solution)/shard_map/all_to_all | solution.py:976
  10.6 36.8 %collective-permute-start.2 = (bf16[1024,768]{1,0:T(8,128)(2,1)}, bf16[1024,768]{1,0:T(8,128)(2,1)}, u32[]{:S(2)}, u32[]{:S(2)}) collective-permute-start(bf16[1024,768]{1,0:T(8,128)(2,1)} %param.17), channel_id=1, source_target_pairs={{0,2},{2,0},{4,6},{6,4},{8,10},{10,8},{12,14},{14,12},{16,18},{18,... | collective-permute-start | bytes 4718600 | tf_op jit(solution)/shard_map/ppermute | solution.py:934
  10.8 11.7 %collective-permute-start = (f32[2304]{0:T(1024)S(1)}, f32[2304]{0:T(1024)S(1)}, u32[]{:S(2)}, u32[]{:S(2)}) collective-permute-start(f32[2304]{0:T(1024)S(1)} %constant_dynamic-update-slice_fusion), channel_id=1, source_target_pairs={{0,1},{3,2},{4,5},{7,6},{8,9},{11,10},{12,13},{15,14},{16,17},{19,... | collective-permute-start | bytes 27656 | tf_op jit(solution)/shard_map/ppermute | solution.py:943
  10.9 18.1 %collective-permute-start.4 = (bf16[384,768]{1,0:T(8,128)(2,1)}, bf16[384,768]{1,0:T(8,128)(2,1)S(1)}, u32[]{:S(2)}, u32[]{:S(2)}) collective-permute-start(bf16[384,768]{1,0:T(8,128)(2,1)} %param.25), channel_id=1, source_target_pairs={{0,1},{3,2},{4,5},{7,6},{8,9},{11,10},{12,13},{15,14},{16,17},{19,... | collective-permute-start | bytes 1769480 | tf_op jit(solution)/shard_map/ppermute | solution.py:943
  11.2 34.6 %collective-permute-start.5 = (bf16[1024,768]{1,0:T(8,128)(2,1)}, bf16[1024,768]{1,0:T(8,128)(2,1)}, u32[]{:S(2)}, u32[]{:S(2)}) collective-permute-start(bf16[1024,768]{1,0:T(8,128)(2,1)} %param.33), channel_id=1, source_target_pairs={{0,2},{2,0},{4,6},{6,4},{8,10},{10,8},{12,14},{14,12},{16,18},{18,... | collective-permute-start | bytes 4718600 | tf_op jit(solution)/shard_map/ppermute | solution.py:934
  22.6 22.5 %collective-permute-start.7 = (bf16[768,768]{1,0:T(8,128)(2,1)}, bf16[768,768]{1,0:T(8,128)(2,1)}, u32[]{:S(2)}, u32[]{:S(2)}) collective-permute-start(bf16[768,768]{1,0:T(8,128)(2,1)} %dynamic-slice_bitcast_fusion), channel_id=1, source_target_pairs={{0,1},{3,2},{4,5},{7,6},{8,9},{11,10},{12,13},{15,14},{16,17},{19,... | collective-permute-start | bytes 3538952 | tf_op jit(solution)/shard_map/ppermute | solution.py:943
  31.7 26.0 %all-to-all-start.1 = ((bf16[32,16,768]{2,1,0:T(8,128)(2,1)}), bf16[32,16,768]{2,1,0:T(8,128)(2,1)}, u32[]{:S(2)}, u32[]{:S(2)}) async-start(bf16[32,16,768]{2,1,0:T(8,128)(2,1)} %copy-done.2), calls=%async_computation.1 | async-start | bytes 1572864 | tf_op jit(solution)/shard_map/all_to_all | solution.py:986
  45.1 18.3 %collective-permute-start.8 = (bf16[768,768]{1,0:T(8,128)(2,1)}, bf16[768,768]{1,0:T(8,128)(2,1)S(1)}, u32[]{:S(2)}, u32[]{:S(2)}) collective-permute-start(bf16[768,768]{1,0:T(8,128)(2,1)} %collective-permute-done.7.w_out_one), channel_id=1, source_target_pairs={{1,5},{2,6},{5,1},{6,2},{9,13},{10,14},{13,9},{14,10},{17,21},{18,... | collective-permute-start | bytes 3538952 | tf_op jit(solution)/shard_map/ppermute | solution.py:970
  59.3 27.4 %collective-permute-start.10 = (bf16[768,1536]{1,0:T(8,128)(2,1)}, bf16[768,1536]{1,0:T(8,128)(2,1)}, u32[]{:S(2)}, u32[]{:S(2)}) collective-permute-start(bf16[768,1536]{1,0:T(8,128)(2,1)} %param.29), channel_id=1, source_target_pairs={{0,1},{3,2},{4,5},{7,6},{8,9},{11,10},{12,13},{15,14},{16,17},{19,... | collective-permute-start | bytes 7077896 | tf_op jit(solution)/shard_map/ppermute | solution.py:943
  120.0 35.3 %collective-permute-start.12 = (bf16[384,1536]{1,0:T(8,128)(2,1)}, bf16[384,1536]{1,0:T(8,128)(2,1)}, u32[]{:S(2)}, u32[]{:S(2)}) collective-permute-start(bf16[384,1536]{1,0:T(8,128)(2,1)} %get-tuple-element.88), channel_id=1, source_target_pairs={{0,4},{2,6},{4,0},{6,2},{8,12},{10,14},{12,8},{14,10},{16,20},{18,... | collective-permute-start | bytes 3538952 | tf_op jit(solution)/shard_map/ppermute | solution.py:1015
  121.0 34.3 %collective-permute-start.13 = (bf16[384,1536]{1,0:T(8,128)(2,1)}, bf16[384,1536]{1,0:T(8,128)(2,1)}, u32[]{:S(2)}, u32[]{:S(2)}) collective-permute-start(bf16[384,1536]{1,0:T(8,128)(2,1)} %get-tuple-element.90), channel_id=1, source_target_pairs={{1,0},{2,3},{5,4},{6,7},{9,8},{10,11},{13,12},{14,15},{17,16},{18,... | collective-permute-start | bytes 3538952 | tf_op jit(solution)/shard_map/ppermute | solution.py:1046
  121.2 34.2 %collective-permute-start.14 = (bf16[384,1536]{1,0:T(8,128)(2,1)}, bf16[384,1536]{1,0:T(8,128)(2,1)}, u32[]{:S(2)}, u32[]{:S(2)}) collective-permute-start(bf16[384,1536]{1,0:T(8,128)(2,1)} %get-tuple-element.89), channel_id=1, source_target_pairs={{1,2},{2,1},{5,6},{6,5},{9,10},{10,9},{13,14},{14,13},{17,18},{18,... | collective-permute-start | bytes 3538952 | tf_op jit(solution)/shard_map/ppermute | solution.py:1047
  155.4 9.2 %collective-permute-start.15 = (bf16[1024,768]{1,0:T(8,128)(2,1)}, bf16[1024,768]{1,0:T(8,128)(2,1)}, u32[]{:S(2)}, u32[]{:S(2)}) collective-permute-start(bf16[1024,768]{1,0:T(8,128)(2,1)} %get-tuple-element.91.g_own), channel_id=1, source_target_pairs={{0,2},{2,0},{4,6},{6,4},{8,10},{10,8},{12,14},{14,12},{16,18},{18,... | collective-permute-start | bytes 4718600 | tf_op jit(solution)/shard_map/ppermute | solution.py:934
  162.5 17.6 %collective-permute-start.18 = (bf16[4,1,48,1536]{3,2,1,0:T(8,128)(2,1)}, bf16[4,1,48,1536]{3,2,1,0:T(8,128)(2,1)S(1)}, u32[]{:S(2)}, u32[]{:S(2)}) collective-permute-start(bf16[4,1,48,1536]{3,2,1,0:T(8,128)(2,1)} %get-tuple-element.172), channel_id=1, source_target_pairs={{1,0},{2,3},{5,4},{6,7},{9,8},{10,11},{13,12},{14,15},{17,16},{18,... | collective-permute-start | bytes 1769480 | tf_op jit(solution)/shard_map/ppermute | solution.py:1019
  162.5 17.6 %collective-permute-start.19 = (bf16[4,1,48,1536]{3,2,1,0:T(8,128)(2,1)}, bf16[4,1,48,1536]{3,2,1,0:T(8,128)(2,1)}, u32[]{:S(2)}, u32[]{:S(2)}) collective-permute-start(bf16[4,1,48,1536]{3,2,1,0:T(8,128)(2,1)} %get-tuple-element.171), channel_id=1, source_target_pairs={{1,2},{2,1},{5,6},{6,5},{9,10},{10,9},{13,14},{14,13},{17,18},{18,... | collective-permute-start | bytes 1769480 | tf_op jit(solution)/shard_map/ppermute | solution.py:1020
  164.2 35.7 %collective-permute-start.17 = (bf16[384,1664]{1,0:T(8,128)(2,1)}, bf16[384,1664]{1,0:T(8,128)(2,1)}, u32[]{:S(2)}, u32[]{:S(2)}) collective-permute-start(bf16[384,1664]{1,0:T(8,128)(2,1)} %get-tuple-element.96), channel_id=1, source_target_pairs={{0,4},{2,6},{4,0},{6,2},{8,12},{10,14},{12,8},{14,10},{16,20},{18,... | collective-permute-start | bytes 3833864 | tf_op jit(solution)/shard_map/ppermute | solution.py:1015
  171.5 40.8 %all-to-all-start.2 = ((bf16[32,16,768]{2,1,0:T(8,128)(2,1)}), bf16[32,16,768]{2,1,0:T(8,128)(2,1)S(1)}, u32[]{:S(2)}, u32[]{:S(2)}) async-start(bf16[32,16,768]{2,1,0:T(8,128)(2,1)} %bitcast.122), calls=%async_computation.2 | async-start | bytes 1572864 | tf_op jit(solution)/shard_map/all_to_all | solution.py:1076
  181.5 25.8 %collective-permute-start.22 = (bf16[1,1,48,1536]{3,2,1,0:T(8,128)(2,1)S(1)}, bf16[1,1,48,1536]{3,2,1,0:T(8,128)(2,1)S(1)}, u32[]{:S(2)}, u32[]{:S(2)}) collective-permute-start(bf16[1,1,48,1536]{3,2,1,0:T(8,128)(2,1)S(1)} %get-tuple-element.181), channel_id=1, source_target_pairs={{0,8},{2,10},{4,12},{6,14},{8,0},{10,2},{12,4},{14,6},{16,24},{18,... | collective-permute-start | bytes 442376 | tf_op jit(solution)/shard_map/ppermute | solution.py:1032
  181.8 25.5 %collective-permute-start.23 = (bf16[1,1,48,1536]{3,2,1,0:T(8,128)(2,1)S(1)}, bf16[1,1,48,1536]{3,2,1,0:T(8,128)(2,1)S(1)}, u32[]{:S(2)}, u32[]{:S(2)}) collective-permute-start(bf16[1,1,48,1536]{3,2,1,0:T(8,128)(2,1)S(1)} %get-tuple-element.180), channel_id=1, source_target_pairs={{0,16},{2,18},{4,20},{6,22},{8,24},{10,26},{12,28},{14,30},{16,0},... | collective-permute-start | bytes 442376 | tf_op jit(solution)/shard_map/ppermute | solution.py:1032
  184.5 27.7 %collective-permute-start.24 = (bf16[1,1,48,1536]{3,2,1,0:T(8,128)(2,1)S(1)}, bf16[1,1,48,1536]{3,2,1,0:T(8,128)(2,1)S(1)}, u32[]{:S(2)}, u32[]{:S(2)}) collective-permute-start(bf16[1,1,48,1536]{3,2,1,0:T(8,128)(2,1)S(1)} %get-tuple-element.179), channel_id=1, source_target_pairs={{0,24},{2,26},{4,28},{6,30},{8,16},{10,18},{12,20},{14,22},{16,8},... | collective-permute-start | bytes 442376 | tf_op jit(solution)/shard_map/ppermute | solution.py:1032
  188.4 35.2 %collective-permute-start.26 = (bf16[4,1,48,1536]{3,2,0,1:T(8,128)(2,1)}, bf16[4,1,48,1536]{3,2,0,1:T(8,128)(2,1)}, u32[]{:S(2)}, u32[]{:S(2)}) collective-permute-start(bf16[4,1,48,1536]{3,2,0,1:T(8,128)(2,1)} %get-tuple-element.170), channel_id=1, source_target_pairs={{0,4},{2,6},{4,0},{6,2},{8,12},{10,14},{12,8},{14,10},{16,20},{18,... | collective-permute-start | bytes 1769480 | tf_op jit(solution)/shard_map/ppermute | solution.py:1015
  199.9 23.7 %collective-permute-start.16 = (bf16[1024,768]{1,0:T(8,128)(2,1)}, bf16[1024,768]{1,0:T(8,128)(2,1)}, u32[]{:S(2)}, u32[]{:S(2)}) collective-permute-start(bf16[1024,768]{1,0:T(8,128)(2,1)} %get-tuple-element.94), channel_id=1, source_target_pairs={{0,2},{2,0},{4,6},{6,4},{8,10},{10,8},{12,14},{14,12},{16,18},{18,... | collective-permute-start | bytes 4718600 | tf_op jit(solution)/shard_map/ppermute | solution.py:934
  207.3 14.5 %collective-permute-start.28 = (bf16[4,1,48,1664]{3,2,0,1:T(8,128)(2,1)}, bf16[4,1,48,1664]{3,2,0,1:T(8,128)(2,1)}, u32[]{:S(2)}, u32[]{:S(2)}) collective-permute-start(bf16[4,1,48,1664]{3,2,0,1:T(8,128)(2,1)} %get-tuple-element.165), channel_id=1, source_target_pairs={{1,0},{2,3},{5,4},{6,7},{9,8},{10,11},{13,12},{14,15},{17,16},{18,... | collective-permute-start | bytes 1916936 | tf_op jit(solution)/shard_map/ppermute | solution.py:1019
  207.3 14.7 %collective-permute-start.29 = (bf16[4,1,48,1664]{3,2,0,1:T(8,128)(2,1)}, bf16[4,1,48,1664]{3,2,0,1:T(8,128)(2,1)}, u32[]{:S(2)}, u32[]{:S(2)}) collective-permute-start(bf16[4,1,48,1664]{3,2,0,1:T(8,128)(2,1)} %get-tuple-element.164), channel_id=1, source_target_pairs={{1,2},{2,1},{5,6},{6,5},{9,10},{10,9},{13,14},{14,13},{17,18},{18,... | collective-permute-start | bytes 1916936 | tf_op jit(solution)/shard_map/ppermute | solution.py:1020
  215.4 25.4 %all-to-all-start.3 = ((bf16[16,2,16,768]{3,2,1,0:T(8,128)(2,1)}), bf16[16,2,16,768]{3,2,1,0:T(8,128)(2,1)}, u32[]{:S(2)}, u32[]{:S(2)}) async-start(bf16[16,2,16,768]{3,2,1,0:T(8,128)(2,1)} %bitcast.27), calls=%async_computation.3 | async-start | bytes 1572864 | tf_op jit(solution)/shard_map/all_to_all | solution.py:1096
  221.8 16.1 %collective-permute-start.21 = (bf16[512,768]{1,0:T(8,128)(2,1)}, bf16[512,768]{1,0:T(8,128)(2,1)}, u32[]{:S(2)}, u32[]{:S(2)}) collective-permute-start(bf16[512,768]{1,0:T(8,128)(2,1)} %dynamic-slice_bitcast_fusion.1), channel_id=1, source_target_pairs={{0,1},{3,2},{4,5},{7,6},{8,9},{11,10},{12,13},{15,14},{16,17},{19,... | collective-permute-start | bytes 2359304 | tf_op jit(solution)/shard_map/ppermute | solution.py:943
  227.1 25.7 %collective-permute-start.20 = (bf16[1024,768]{1,0:T(8,128)(2,1)S(1)}, bf16[1024,768]{1,0:T(8,128)(2,1)}, u32[]{:S(2)}, u32[]{:S(2)}) collective-permute-start(bf16[1024,768]{1,0:T(8,128)(2,1)S(1)} %add_convert_fusion), channel_id=1, source_target_pairs={{0,1},{3,2},{4,5},{7,6},{8,9},{11,10},{12,13},{15,14},{16,17},{19,... | collective-permute-start | bytes 4718600 | tf_op jit(solution)/shard_map/ppermute | solution.py:943
  233.3 20.8 %collective-permute-start.30 = (bf16[1,1,48,3200]{3,2,1,0:T(8,128)(2,1)}, bf16[1,1,48,3200]{3,2,1,0:T(8,128)(2,1)S(1)}, u32[]{:S(2)}, u32[]{:S(2)}) collective-permute-start(bf16[1,1,48,3200]{3,2,1,0:T(8,128)(2,1)} %get-tuple-element.167), channel_id=1, source_target_pairs={{0,8},{2,10},{4,12},{6,14},{8,0},{10,2},{12,4},{14,6},{16,24},{18,... | collective-permute-start | bytes 921608 | tf_op jit(solution)/shard_map/ppermute | solution.py:1032
  234.4 25.4 %collective-permute-start.31 = (bf16[1,1,48,3200]{3,2,1,0:T(8,128)(2,1)}, bf16[1,1,48,3200]{3,2,1,0:T(8,128)(2,1)}, u32[]{:S(2)}, u32[]{:S(2)}) collective-permute-start(bf16[1,1,48,3200]{3,2,1,0:T(8,128)(2,1)} %get-tuple-element.168), channel_id=1, source_target_pairs={{0,16},{2,18},{4,20},{6,22},{8,24},{10,26},{12,28},{14,30},{16,0},... | collective-permute-start | bytes 921608 | tf_op jit(solution)/shard_map/ppermute | solution.py:1032
  237.3 30.6 %collective-permute-start.32 = (bf16[1,1,48,3200]{3,2,1,0:T(8,128)(2,1)S(1)}, bf16[1,1,48,3200]{3,2,1,0:T(8,128)(2,1)}, u32[]{:S(2)}, u32[]{:S(2)}) collective-permute-start(bf16[1,1,48,3200]{3,2,1,0:T(8,128)(2,1)S(1)} %get-tuple-element.166), channel_id=1, source_target_pairs={{0,24},{2,26},{4,28},{6,30},{8,16},{10,18},{12,20},{14,22},{16,8},... | collective-permute-start | bytes 921608 | tf_op jit(solution)/shard_map/ppermute | solution.py:1032
  242.9 31.5 %collective-permute-start.25 = (bf16[512,768]{1,0:T(8,128)(2,1)S(1)}, bf16[512,768]{1,0:T(8,128)(2,1)S(1)}, u32[]{:S(2)}, u32[]{:S(2)}) collective-permute-start(bf16[512,768]{1,0:T(8,128)(2,1)S(1)} %fusion), channel_id=1, source_target_pairs={{0,1},{1,0},{2,3},{3,2},{4,5},{5,4},{6,7},{7,6},{8,9},{9,8},{10,11... | collective-permute-start | bytes 2359304 | tf_op jit(solution)/shard_map/ppermute | solution.py:1103
  (30 other events, 161.9 us)

commit v5 on v4

--- a/solution.py
+++ b/solution.py
@@ -718,7 +718,7 @@
         move(part_v.at[here, :], part.at[here, :], last_sems.at[i]).start()
         return carry
 
-    lax.fori_loop(0, rows // big, finish, 0)
+    lax.fori_loop(0, rows // big, finish, 0, unroll=2)
     for i in range(rows // big):
         here = pl.ds(i * big, big)
         stores.append(move(part_v.at[here, :], part.at[here, :], last_sems.at[i]))

time: 277 us -> 277 us (level)
  no operation moved by 1% of the time
where the time goes in v5:
time: 277 us; the launch traced here: 275 us
  Pallas kernels  88.8 us (32%)
  waiting for transfers between devices  67.7 us (24%)
  starting transfers between devices  66.3 us (24%)
  other arithmetic  26.8 us (10%)
  local copies, waits for them, and re-layouts  23.9 us (9%)
    pallas_call x1, Pallas kernels, attention_back(): pl.pallas_call(functools.partial(attention_back_kernel, lead_rows, part_r...  29.6 us
    pallas_call x1, Pallas kernels, feed(): pl.pallas_call(functools.partial(feed_kernel, in_rows, out_rows), out_sha...  29.5 us
    ppermute x7, waiting for transfers between devices, half_weight(): return lax.ppermute(value, both, weight_move)  24.7 us
    pallas_call x1, Pallas kernels, attention(): pl.pallas_call(attention_kernel, out_shape=(shape((rows, width), F32), ta...  20.7 us
    ppermute x6, waiting for transfers between devices, far(): lax.ppermute(taken(value, spot ^ flip, 2), 'dp', [(d, d ^ flip << shift)...  17.1 us
    ppermute x9, starting transfers between devices, swap(): return lax.ppermute(value, 'dp', core_swap)  11 us
    ppermute x3, waiting for transfers between devices, send_across(): return lax.ppermute(value, 'dp', [(d, d ^ 1 << lead) for d in all_dp])  10.1 us
    ppermute x7, starting transfers between devices, half_weight(): return lax.ppermute(value, both, weight_move)  9.43 us
  transfers between devices with their start and end apart: 38, of which 14 were waited for; matrix products, arithmetic and copies ran while one was open for 16% of the time, Pallas kernels for 22%

profile of v5, /device:TPU:8, one launch (start us, length us, event | category | flops | bytes accessed | tf_op | source)
XLA Modules:
  0.0 275.5 jit_solution(11366009383634067586)
XLA Ops:
  2.2 2.1 copy_bitcast_fusion
  4.3 6.3 %all-to-all-start = ((bf16[16,2,16,768]{3,2,1,0:T(8,128)(2,1)}), bf16[16,2,16,768]{3,2,1,0:T(8,128)(2,1)S(1)}, u32[]{:S(2)}, u32[]{:S(2)}) async-start(bf16[16,2,16,768]{3,2,1,0:T(8,128)(2,1)} %copy_bitcast_fusion), calls=%async_computation | async-start | bytes 1572864 | tf_op jit(solution)/shard_map/all_to_all | solution.py:976
  11.4 2.4 dynamic-slice_bitcast_fusion
  14.5 8.1 %collective-permute-done = f32[2304]{0:T(1024)S(1)} collective-permute-done((f32[2304]{0:T(1024)S(1)}, f32[2304]{0:T(1024)S(1)}, u32[]{:S(2)}, u32[]{:S(2)}) %collective-permute-start) | collective-permute-done | bytes 9248 | tf_op jit(solution)/shard_map/ppermute | solution.py:943
  22.6 2.5 collective-permute-start.7
  25.1 3.9 %collective-permute-done.4.refs_1_.wp = bf16[384,768]{1,0:T(8,128)(2,1)S(1)} collective-permute-done((bf16[384,768]{1,0:T(8,128)(2,1)}, bf16[384,768]{1,0:T(8,128)(2,1)S(1)}, u32[]{:S(2)}, u32[]{:S(2)}) %collective-permute-start.4) | collective-permute-done | bytes 589856 | tf_op jit(solution)/shard_map/ppermute | solution.py:943
  31.7 6.6 %all-to-all-start.1 = ((bf16[32,16,768]{2,1,0:T(8,128)(2,1)}), bf16[32,16,768]{2,1,0:T(8,128)(2,1)}, u32[]{:S(2)}, u32[]{:S(2)}) async-start(bf16[32,16,768]{2,1,0:T(8,128)(2,1)} %copy-done.2), calls=%async_computation.1 | async-start | bytes 1572864 | tf_op jit(solution)/shard_map/all_to_all | solution.py:986
  41.6 3.5 %collective-permute-done.7.w_out_one = bf16[768,768]{1,0:T(8,128)(2,1)} collective-permute-done((bf16[768,768]{1,0:T(8,128)(2,1)}, bf16[768,768]{1,0:T(8,128)(2,1)}, u32[]{:S(2)}, u32[]{:S(2)}) %collective-permute-start.7) | collective-permute-done | bytes 1179680 | tf_op jit(solution)/shard_map/ppermute | solution.py:943
  48.9 8.8 %all-to-all-done.1 = bf16[32,16,768]{2,1,0:T(8,128)(2,1)} async-done(((bf16[32,16,768]{2,1,0:T(8,128)(2,1)}), bf16[32,16,768]{2,1,0:T(8,128)(2,1)}, u32[]{:S(2)}, u32[]{:S(2)}) %all-to-all-start.1) | async-done | bytes 786464 | tf_op jit(solution)/shard_map/all_to_all | solution.py:986
  64.4 20.7 %attention.1 = (f32[1024,768]{1,0:T(8,128)}, bf16[1024,768]{1,0:T(8,128)(2,1)}, bf16[1024,768]{1,0:T(8,128)(2,1)}, f32[1024,128]{1,0:T(8,128)}, bf16[1024,384]{1...) custom-call(f32[1]{0:T(128)} %slice.93.blend, ...), custom_call_target="tpu_custom_call" | custom-call | flops 1048576 | bytes 1048576 | tf_op jit(solution)/shard_map/attention/pallas_call | solution.py:290
  86.8 2.6 collective-permute-done.9.p_oth
  90.5 29.5 %feed.1 = (f32[1024,768]{1,0:T(8,128)}, bf16[1024,768]{1,0:T(8,128)(2,1)}, bf16[1024,768]{1,0:T(8,128)(2,1)}, bf16[384,1536]{1,0:T(8,128)(2,1)}, bf16[384,1536]{...) custom-call(s32[3]{0:T(128)} %pad_add_fusion.flags, ...), custom_call_target="tpu_custom_call" | custom-call | flops 1048576 | bytes 1048576 | tf_op jit(solution)/shard_map/feed/pallas_call | solution.py:496
  121.2 1.7 collective-permute-start.14
  125.4 29.6 %attention_back.1 = (f32[1024,768]{1,0:T(8,128)}, bf16[1024,768]{1,0:T(8,128)(2,1)}, bf16[384,1664]{1,0:T(8,128)(2,1)}, bf16[384,1664]{1,0:T(8,128)(2,1)}, f32[9,768]{1,0:T(8,128)}) custom-call(s32[3]{0:T(128)} %pad_add_fusion.flags, f32[5,768]{1,0:T(8,128)} %stack.46.vecs, f32[1,1024]{1,0:T(1,128)} %bitcast.128, f32[6,1024]{1,0:T(8,128)} %get-tuple-element.74.lse, ...), custom_call_target="tpu_custom_call" | custom-call | flops 1048576 | bytes 1048576 | tf_op jit(solution)/shard_map/attention_back/pallas_call | solution.py:776
  155.0 4.1 %collective-permute-start.15 = (bf16[1024,768]{1,0:T(8,128)(2,1)}, bf16[1024,768]{1,0:T(8,128)(2,1)}, u32[]{:S(2)}, u32[]{:S(2)}) collective-permute-start(bf16[1024,768]{1,0:T(8,128)(2,1)} %get-tuple-element.91.g_own), channel_id=1, source_target_pairs={{0,2},{2,0},{4,6},{6,4},{8,10},{10,8},{12,14},{14,12},{16,18},{18,... | collective-permute-start | bytes 4718600 | tf_op jit(solution)/shard_map/ppermute | solution.py:934
  159.1 1.9 add_convert_fusion.3
  164.3 6.9 %mixed_back.1 = (bf16[16,2,16,768]{3,2,1,0:T(8,128)(2,1)}, bf16[1024,768]{1,0:T(8,128)(2,1)}) custom-call(f32[1]{0:T(128)} %slice.93.blend, s32[3]{0:T(128)} %pad_add_fusion.flags, f32[5,768]{1,0:T(8,128)} %stack.46.vecs, f32[1024,768]{1,0:T(8,128)} %get-tuple-element.86.gh, bf16[1024,768]{1,0:T(8,128)(2,1)} %get-tuple-element.91.g_own, ...), custom_call_target="tpu_custom_call" | custom-call | flops 1048576 | bytes 1048576 | tf_op jit(solution)/shard_map/mixed_back/pallas_call | solution.py:874
  171.2 8.6 %all-to-all-start.2 = ((bf16[32,16,768]{2,1,0:T(8,128)(2,1)}), bf16[32,16,768]{2,1,0:T(8,128)(2,1)S(1)}, u32[]{:S(2)}, u32[]{:S(2)}) async-start(bf16[32,16,768]{2,1,0:T(8,128)(2,1)} %bitcast.122), calls=%async_computation.2 | async-start | bytes 1572864 | tf_op jit(solution)/shard_map/all_to_all | solution.py:1076
  181.5 2.7 collective-permute-start.23
  184.7 2.2 add_convert_fusion.2
  189.5 10.1 %collective-permute-done.17 = bf16[384,1664]{1,0:T(8,128)(2,1)} collective-permute-done((bf16[384,1664]{1,0:T(8,128)(2,1)}, bf16[384,1664]{1,0:T(8,128)(2,1)}, u32[]{:S(2)}, u32[]{:S(2)}) %collective-permute-start.17) | collective-permute-done | bytes 1277984 | tf_op jit(solution)/shard_map/ppermute | solution.py:1015
  199.6 3.7 %collective-permute-start.16 = (bf16[1024,768]{1,0:T(8,128)(2,1)}, bf16[1024,768]{1,0:T(8,128)(2,1)}, u32[]{:S(2)}, u32[]{:S(2)}) collective-permute-start(bf16[1024,768]{1,0:T(8,128)(2,1)} %get-tuple-element.94), channel_id=1, source_target_pairs={{0,2},{2,0},{4,6},{6,4},{8,10},{10,8},{12,14},{14,12},{16,18},{18,... | collective-permute-start | bytes 4718600 | tf_op jit(solution)/shard_map/ppermute | solution.py:934
  203.3 1.6 add_convert_fusion.1.refs_0_
  208.5 3.3 %collective-permute-done.24 = bf16[1,1,48,1536]{3,2,1,0:T(8,128)(2,1)S(1)} collective-permute-done((bf16[1,1,48,1536]{3,2,1,0:T(8,128)(2,1)S(1)}, bf16[1,1,48,1536]{3,2,1,0:T(8,128)(2,1)S(1)}, u32[]{:S(2)}, u32[]{:S(2)}) %collective-permute-start.24) | collective-permute-done | bytes 147488 | tf_op jit(solution)/shard_map/ppermute | solution.py:1032
  215.1 6.3 %all-to-all-start.3 = ((bf16[16,2,16,768]{3,2,1,0:T(8,128)(2,1)}), bf16[16,2,16,768]{3,2,1,0:T(8,128)(2,1)}, u32[]{:S(2)}, u32[]{:S(2)}) async-start(bf16[16,2,16,768]{3,2,1,0:T(8,128)(2,1)} %bitcast.27), calls=%async_computation.3 | async-start | bytes 1572864 | tf_op jit(solution)/shard_map/all_to_all | solution.py:1096
  223.3 3.5 %add_convert_fusion = bf16[1024,768]{1,0:T(8,128)(2,1)S(1)} fusion(f32[1024,768]{1,0:T(8,128)} %get-tuple-element.72, bf16[1024,768]{1,0:T(8,128)(2,1)} %collective-permute-done.16, bf16[1024,768]{1,0:T(8,128)(2,1)} %get-tuple-element.94, f32[768]{0:T(1024)S(1)} %copy-done.16), kind=kLoop, calls=%fused_computation.2 | loop fusion | flops 4718592 | bytes 7867392 | tf_op jit(solution)/shard_map/convert_element_type | solution.py:1086
  226.8 4.0 %collective-permute-start.20 = (bf16[1024,768]{1,0:T(8,128)(2,1)S(1)}, bf16[1024,768]{1,0:T(8,128)(2,1)}, u32[]{:S(2)}, u32[]{:S(2)}) collective-permute-start(bf16[1024,768]{1,0:T(8,128)(2,1)S(1)} %add_convert_fusion), channel_id=1, source_target_pairs={{0,1},{3,2},{4,5},{7,6},{8,9},{11,10},{12,13},{15,14},{16,17},{19,... | collective-permute-start | bytes 4718600 | tf_op jit(solution)/shard_map/ppermute | solution.py:943
  234.1 2.9 %collective-permute-start.31 = (bf16[1,1,48,3200]{3,2,1,0:T(8,128)(2,1)}, bf16[1,1,48,3200]{3,2,1,0:T(8,128)(2,1)}, u32[]{:S(2)}, u32[]{:S(2)}) collective-permute-start(bf16[1,1,48,3200]{3,2,1,0:T(8,128)(2,1)} %get-tuple-element.168), channel_id=1, source_target_pairs={{0,16},{2,18},{4,20},{6,22},{8,24},{10,26},{12,28},{14,30},{16,0},... | collective-permute-start | bytes 921608 | tf_op jit(solution)/shard_map/ppermute | solution.py:1032
  237.5 3.0 %all-to-all-done.3 = bf16[16,2,16,768]{3,2,1,0:T(8,128)(2,1)} async-done(((bf16[16,2,16,768]{3,2,1,0:T(8,128)(2,1)}), bf16[16,2,16,768]{3,2,1,0:T(8,128)(2,1)}, u32[]{:S(2)}, u32[]{:S(2)}) %all-to-all-start.3) | async-done | bytes 786464 | tf_op jit(solution)/shard_map/all_to_all | solution.py:1096
  243.9 8.5 %collective-permute-done.20 = bf16[1024,768]{1,0:T(8,128)(2,1)} collective-permute-done((bf16[1024,768]{1,0:T(8,128)(2,1)S(1)}, bf16[1024,768]{1,0:T(8,128)(2,1)}, u32[]{:S(2)}, u32[]{:S(2)}) %collective-permute-start.20) | collective-permute-done | bytes 1572896 | tf_op jit(solution)/shard_map/ppermute | solution.py:943
  253.7 5.7 %collective-permute-done.31 = bf16[1,1,48,3200]{3,2,1,0:T(8,128)(2,1)} collective-permute-done((bf16[1,1,48,3200]{3,2,1,0:T(8,128)(2,1)}, bf16[1,1,48,3200]{3,2,1,0:T(8,128)(2,1)}, u32[]{:S(2)}, u32[]{:S(2)}) %collective-permute-start.31) | collective-permute-done | bytes 307232 | tf_op jit(solution)/shard_map/ppermute | solution.py:1032
  259.4 8.1 %collective-permute-done.32 = bf16[1,1,48,3200]{3,2,1,0:T(8,128)(2,1)} collective-permute-done((bf16[1,1,48,3200]{3,2,1,0:T(8,128)(2,1)S(1)}, bf16[1,1,48,3200]{3,2,1,0:T(8,128)(2,1)}, u32[]{:S(2)}, u32[]{:S(2)}) %collective-permute-start.32) | collective-permute-done | bytes 307232 | tf_op jit(solution)/shard_map/ppermute | solution.py:1032
  (167 shorter events, 58.4 us)
Async XLA Ops:
  0.6 28.9 %collective-permute-start.3 = (bf16[3,768,384]{2,1,0:T(8,128)(2,1)}, bf16[3,768,384]{2,1,0:T(8,128)(2,1)S(1)}, u32[]{:S(2)}, u32[]{:S(2)}) collective-permute-start(bf16[3,768,384]{2,1,0:T(8,128)(2,1)} %bitcast.130), channel_id=1, source_target_pairs={{0,1},{3,2},{4,5},{7,6},{8,9},{11,10},{12,13},{15,14},{16,17},{19,... | collective-permute-start | bytes 5308424 | tf_op jit(solution)/shard_map/ppermute | solution.py:943
  4.3 25.2 %all-to-all-start = ((bf16[16,2,16,768]{3,2,1,0:T(8,128)(2,1)}), bf16[16,2,16,768]{3,2,1,0:T(8,128)(2,1)S(1)}, u32[]{:S(2)}, u32[]{:S(2)}) async-start(bf16[16,2,16,768]{3,2,1,0:T(8,128)(2,1)} %copy_bitcast_fusion), calls=%async_computation | async-start | bytes 1572864 | tf_op jit(solution)/shard_map/all_to_all | solution.py:976
  10.6 36.8 %collective-permute-start.2 = (bf16[1024,768]{1,0:T(8,128)(2,1)}, bf16[1024,768]{1,0:T(8,128)(2,1)}, u32[]{:S(2)}, u32[]{:S(2)}) collective-permute-start(bf16[1024,768]{1,0:T(8,128)(2,1)} %param.17), channel_id=1, source_target_pairs={{0,2},{2,0},{4,6},{6,4},{8,10},{10,8},{12,14},{14,12},{16,18},{18,... | collective-permute-start | bytes 4718600 | tf_op jit(solution)/shard_map/ppermute | solution.py:934
  10.8 11.7 %collective-permute-start = (f32[2304]{0:T(1024)S(1)}, f32[2304]{0:T(1024)S(1)}, u32[]{:S(2)}, u32[]{:S(2)}) collective-permute-start(f32[2304]{0:T(1024)S(1)} %constant_dynamic-update-slice_fusion), channel_id=1, source_target_pairs={{0,1},{3,2},{4,5},{7,6},{8,9},{11,10},{12,13},{15,14},{16,17},{19,... | collective-permute-start | bytes 27656 | tf_op jit(solution)/shard_map/ppermute | solution.py:943
  10.9 18.1 %collective-permute-start.4 = (bf16[384,768]{1,0:T(8,128)(2,1)}, bf16[384,768]{1,0:T(8,128)(2,1)S(1)}, u32[]{:S(2)}, u32[]{:S(2)}) collective-permute-start(bf16[384,768]{1,0:T(8,128)(2,1)} %param.25), channel_id=1, source_target_pairs={{0,1},{3,2},{4,5},{7,6},{8,9},{11,10},{12,13},{15,14},{16,17},{19,... | collective-permute-start | bytes 1769480 | tf_op jit(solution)/shard_map/ppermute | solution.py:943
  11.2 34.6 %collective-permute-start.5 = (bf16[1024,768]{1,0:T(8,128)(2,1)}, bf16[1024,768]{1,0:T(8,128)(2,1)}, u32[]{:S(2)}, u32[]{:S(2)}) collective-permute-start(bf16[1024,768]{1,0:T(8,128)(2,1)} %param.33), channel_id=1, source_target_pairs={{0,2},{2,0},{4,6},{6,4},{8,10},{10,8},{12,14},{14,12},{16,18},{18,... | collective-permute-start | bytes 4718600 | tf_op jit(solution)/shard_map/ppermute | solution.py:934
  22.6 22.5 %collective-permute-start.7 = (bf16[768,768]{1,0:T(8,128)(2,1)}, bf16[768,768]{1,0:T(8,128)(2,1)}, u32[]{:S(2)}, u32[]{:S(2)}) collective-permute-start(bf16[768,768]{1,0:T(8,128)(2,1)} %dynamic-slice_bitcast_fusion), channel_id=1, source_target_pairs={{0,1},{3,2},{4,5},{7,6},{8,9},{11,10},{12,13},{15,14},{16,17},{19,... | collective-permute-start | bytes 3538952 | tf_op jit(solution)/shard_map/ppermute | solution.py:943
  31.7 26.0 %all-to-all-start.1 = ((bf16[32,16,768]{2,1,0:T(8,128)(2,1)}), bf16[32,16,768]{2,1,0:T(8,128)(2,1)}, u32[]{:S(2)}, u32[]{:S(2)}) async-start(bf16[32,16,768]{2,1,0:T(8,128)(2,1)} %copy-done.2), calls=%async_computation.1 | async-start | bytes 1572864 | tf_op jit(solution)/shard_map/all_to_all | solution.py:986
  45.1 18.3 %collective-permute-start.8 = (bf16[768,768]{1,0:T(8,128)(2,1)}, bf16[768,768]{1,0:T(8,128)(2,1)S(1)}, u32[]{:S(2)}, u32[]{:S(2)}) collective-permute-start(bf16[768,768]{1,0:T(8,128)(2,1)} %collective-permute-done.7.w_out_one), channel_id=1, source_target_pairs={{1,5},{2,6},{5,1},{6,2},{9,13},{10,14},{13,9},{14,10},{17,21},{18,... | collective-permute-start | bytes 3538952 | tf_op jit(solution)/shard_map/ppermute | solution.py:970
  59.3 27.4 %collective-permute-start.10 = (bf16[768,1536]{1,0:T(8,128)(2,1)}, bf16[768,1536]{1,0:T(8,128)(2,1)}, u32[]{:S(2)}, u32[]{:S(2)}) collective-permute-start(bf16[768,1536]{1,0:T(8,128)(2,1)} %param.29), channel_id=1, source_target_pairs={{0,1},{3,2},{4,5},{7,6},{8,9},{11,10},{12,13},{15,14},{16,17},{19,... | collective-permute-start | bytes 7077896 | tf_op jit(solution)/shard_map/ppermute | solution.py:943
  120.0 35.0 %collective-permute-start.12 = (bf16[384,1536]{1,0:T(8,128)(2,1)}, bf16[384,1536]{1,0:T(8,128)(2,1)}, u32[]{:S(2)}, u32[]{:S(2)}) collective-permute-start(bf16[384,1536]{1,0:T(8,128)(2,1)} %get-tuple-element.88), channel_id=1, source_target_pairs={{0,4},{2,6},{4,0},{6,2},{8,12},{10,14},{12,8},{14,10},{16,20},{18,... | collective-permute-start | bytes 3538952 | tf_op jit(solution)/shard_map/ppermute | solution.py:1015
  121.0 34.0 %collective-permute-start.13 = (bf16[384,1536]{1,0:T(8,128)(2,1)}, bf16[384,1536]{1,0:T(8,128)(2,1)}, u32[]{:S(2)}, u32[]{:S(2)}) collective-permute-start(bf16[384,1536]{1,0:T(8,128)(2,1)} %get-tuple-element.90), channel_id=1, source_target_pairs={{1,0},{2,3},{5,4},{6,7},{9,8},{10,11},{13,12},{14,15},{17,16},{18,... | collective-permute-start | bytes 3538952 | tf_op jit(solution)/shard_map/ppermute | solution.py:1046
  121.2 33.8 %collective-permute-start.14 = (bf16[384,1536]{1,0:T(8,128)(2,1)}, bf16[384,1536]{1,0:T(8,128)(2,1)}, u32[]{:S(2)}, u32[]{:S(2)}) collective-permute-start(bf16[384,1536]{1,0:T(8,128)(2,1)} %get-tuple-element.89), channel_id=1, source_target_pairs={{1,2},{2,1},{5,6},{6,5},{9,10},{10,9},{13,14},{14,13},{17,18},{18,... | collective-permute-start | bytes 3538952 | tf_op jit(solution)/shard_map/ppermute | solution.py:1047
  155.0 9.2 %collective-permute-start.15 = (bf16[1024,768]{1,0:T(8,128)(2,1)}, bf16[1024,768]{1,0:T(8,128)(2,1)}, u32[]{:S(2)}, u32[]{:S(2)}) collective-permute-start(bf16[1024,768]{1,0:T(8,128)(2,1)} %get-tuple-element.91.g_own), channel_id=1, source_target_pairs={{0,2},{2,0},{4,6},{6,4},{8,10},{10,8},{12,14},{14,12},{16,18},{18,... | collective-permute-start | bytes 4718600 | tf_op jit(solution)/shard_map/ppermute | solution.py:934
  162.2 17.6 %collective-permute-start.18 = (bf16[4,1,48,1536]{3,2,1,0:T(8,128)(2,1)}, bf16[4,1,48,1536]{3,2,1,0:T(8,128)(2,1)S(1)}, u32[]{:S(2)}, u32[]{:S(2)}) collective-permute-start(bf16[4,1,48,1536]{3,2,1,0:T(8,128)(2,1)} %get-tuple-element.172), channel_id=1, source_target_pairs={{1,0},{2,3},{5,4},{6,7},{9,8},{10,11},{13,12},{14,15},{17,16},{18,... | collective-permute-start | bytes 1769480 | tf_op jit(solution)/shard_map/ppermute | solution.py:1019
  162.2 17.6 %collective-permute-start.19 = (bf16[4,1,48,1536]{3,2,1,0:T(8,128)(2,1)}, bf16[4,1,48,1536]{3,2,1,0:T(8,128)(2,1)}, u32[]{:S(2)}, u32[]{:S(2)}) collective-permute-start(bf16[4,1,48,1536]{3,2,1,0:T(8,128)(2,1)} %get-tuple-element.171), channel_id=1, source_target_pairs={{1,2},{2,1},{5,6},{6,5},{9,10},{10,9},{13,14},{14,13},{17,18},{18,... | collective-permute-start | bytes 1769480 | tf_op jit(solution)/shard_map/ppermute | solution.py:1020
  163.9 35.7 %collective-permute-start.17 = (bf16[384,1664]{1,0:T(8,128)(2,1)}, bf16[384,1664]{1,0:T(8,128)(2,1)}, u32[]{:S(2)}, u32[]{:S(2)}) collective-permute-start(bf16[384,1664]{1,0:T(8,128)(2,1)} %get-tuple-element.96), channel_id=1, source_target_pairs={{0,4},{2,6},{4,0},{6,2},{8,12},{10,14},{12,8},{14,10},{16,20},{18,... | collective-permute-start | bytes 3833864 | tf_op jit(solution)/shard_map/ppermute | solution.py:1015
  171.2 40.8 %all-to-all-start.2 = ((bf16[32,16,768]{2,1,0:T(8,128)(2,1)}), bf16[32,16,768]{2,1,0:T(8,128)(2,1)S(1)}, u32[]{:S(2)}, u32[]{:S(2)}) async-start(bf16[32,16,768]{2,1,0:T(8,128)(2,1)} %bitcast.122), calls=%async_computation.2 | async-start | bytes 1572864 | tf_op jit(solution)/shard_map/all_to_all | solution.py:1076
  181.2 25.8 %collective-permute-start.22 = (bf16[1,1,48,1536]{3,2,1,0:T(8,128)(2,1)S(1)}, bf16[1,1,48,1536]{3,2,1,0:T(8,128)(2,1)S(1)}, u32[]{:S(2)}, u32[]{:S(2)}) collective-permute-start(bf16[1,1,48,1536]{3,2,1,0:T(8,128)(2,1)S(1)} %get-tuple-element.181), channel_id=1, source_target_pairs={{0,8},{2,10},{4,12},{6,14},{8,0},{10,2},{12,4},{14,6},{16,24},{18,... | collective-permute-start | bytes 442376 | tf_op jit(solution)/shard_map/ppermute | solution.py:1032
  181.5 25.5 %collective-permute-start.23 = (bf16[1,1,48,1536]{3,2,1,0:T(8,128)(2,1)S(1)}, bf16[1,1,48,1536]{3,2,1,0:T(8,128)(2,1)S(1)}, u32[]{:S(2)}, u32[]{:S(2)}) collective-permute-start(bf16[1,1,48,1536]{3,2,1,0:T(8,128)(2,1)S(1)} %get-tuple-element.180), channel_id=1, source_target_pairs={{0,16},{2,18},{4,20},{6,22},{8,24},{10,26},{12,28},{14,30},{16,0},... | collective-permute-start | bytes 442376 | tf_op jit(solution)/shard_map/ppermute | solution.py:1032
  184.2 27.7 %collective-permute-start.24 = (bf16[1,1,48,1536]{3,2,1,0:T(8,128)(2,1)S(1)}, bf16[1,1,48,1536]{3,2,1,0:T(8,128)(2,1)S(1)}, u32[]{:S(2)}, u32[]{:S(2)}) collective-permute-start(bf16[1,1,48,1536]{3,2,1,0:T(8,128)(2,1)S(1)} %get-tuple-element.179), channel_id=1, source_target_pairs={{0,24},{2,26},{4,28},{6,30},{8,16},{10,18},{12,20},{14,22},{16,8},... | collective-permute-start | bytes 442376 | tf_op jit(solution)/shard_map/ppermute | solution.py:1032
  188.1 35.2 %collective-permute-start.26 = (bf16[4,1,48,1536]{3,2,0,1:T(8,128)(2,1)}, bf16[4,1,48,1536]{3,2,0,1:T(8,128)(2,1)}, u32[]{:S(2)}, u32[]{:S(2)}) collective-permute-start(bf16[4,1,48,1536]{3,2,0,1:T(8,128)(2,1)} %get-tuple-element.170), channel_id=1, source_target_pairs={{0,4},{2,6},{4,0},{6,2},{8,12},{10,14},{12,8},{14,10},{16,20},{18,... | collective-permute-start | bytes 1769480 | tf_op jit(solution)/shard_map/ppermute | solution.py:1015
  199.6 23.7 %collective-permute-start.16 = (bf16[1024,768]{1,0:T(8,128)(2,1)}, bf16[1024,768]{1,0:T(8,128)(2,1)}, u32[]{:S(2)}, u32[]{:S(2)}) collective-permute-start(bf16[1024,768]{1,0:T(8,128)(2,1)} %get-tuple-element.94), channel_id=1, source_target_pairs={{0,2},{2,0},{4,6},{6,4},{8,10},{10,8},{12,14},{14,12},{16,18},{18,... | collective-permute-start | bytes 4718600 | tf_op jit(solution)/shard_map/ppermute | solution.py:934
  207.0 14.5 %collective-permute-start.28 = (bf16[4,1,48,1664]{3,2,0,1:T(8,128)(2,1)}, bf16[4,1,48,1664]{3,2,0,1:T(8,128)(2,1)}, u32[]{:S(2)}, u32[]{:S(2)}) collective-permute-start(bf16[4,1,48,1664]{3,2,0,1:T(8,128)(2,1)} %get-tuple-element.165), channel_id=1, source_target_pairs={{1,0},{2,3},{5,4},{6,7},{9,8},{10,11},{13,12},{14,15},{17,16},{18,... | collective-permute-start | bytes 1916936 | tf_op jit(solution)/shard_map/ppermute | solution.py:1019
  207.0 14.7 %collective-permute-start.29 = (bf16[4,1,48,1664]{3,2,0,1:T(8,128)(2,1)}, bf16[4,1,48,1664]{3,2,0,1:T(8,128)(2,1)}, u32[]{:S(2)}, u32[]{:S(2)}) collective-permute-start(bf16[4,1,48,1664]{3,2,0,1:T(8,128)(2,1)} %get-tuple-element.164), channel_id=1, source_target_pairs={{1,2},{2,1},{5,6},{6,5},{9,10},{10,9},{13,14},{14,13},{17,18},{18,... | collective-permute-start | bytes 1916936 | tf_op jit(solution)/shard_map/ppermute | solution.py:1020
  215.1 25.4 %all-to-all-start.3 = ((bf16[16,2,16,768]{3,2,1,0:T(8,128)(2,1)}), bf16[16,2,16,768]{3,2,1,0:T(8,128)(2,1)}, u32[]{:S(2)}, u32[]{:S(2)}) async-start(bf16[16,2,16,768]{3,2,1,0:T(8,128)(2,1)} %bitcast.27), calls=%async_computation.3 | async-start | bytes 1572864 | tf_op jit(solution)/shard_map/all_to_all | solution.py:1096
  221.5 16.1 %collective-permute-start.21 = (bf16[512,768]{1,0:T(8,128)(2,1)}, bf16[512,768]{1,0:T(8,128)(2,1)}, u32[]{:S(2)}, u32[]{:S(2)}) collective-permute-start(bf16[512,768]{1,0:T(8,128)(2,1)} %dynamic-slice_bitcast_fusion.1), channel_id=1, source_target_pairs={{0,1},{3,2},{4,5},{7,6},{8,9},{11,10},{12,13},{15,14},{16,17},{19,... | collective-permute-start | bytes 2359304 | tf_op jit(solution)/shard_map/ppermute | solution.py:943
  226.8 25.7 %collective-permute-start.20 = (bf16[1024,768]{1,0:T(8,128)(2,1)S(1)}, bf16[1024,768]{1,0:T(8,128)(2,1)}, u32[]{:S(2)}, u32[]{:S(2)}) collective-permute-start(bf16[1024,768]{1,0:T(8,128)(2,1)S(1)} %add_convert_fusion), channel_id=1, source_target_pairs={{0,1},{3,2},{4,5},{7,6},{8,9},{11,10},{12,13},{15,14},{16,17},{19,... | collective-permute-start | bytes 4718600 | tf_op jit(solution)/shard_map/ppermute | solution.py:943
  233.0 20.8 %collective-permute-start.30 = (bf16[1,1,48,3200]{3,2,1,0:T(8,128)(2,1)}, bf16[1,1,48,3200]{3,2,1,0:T(8,128)(2,1)S(1)}, u32[]{:S(2)}, u32[]{:S(2)}) collective-permute-start(bf16[1,1,48,3200]{3,2,1,0:T(8,128)(2,1)} %get-tuple-element.167), channel_id=1, source_target_pairs={{0,8},{2,10},{4,12},{6,14},{8,0},{10,2},{12,4},{14,6},{16,24},{18,... | collective-permute-start | bytes 921608 | tf_op jit(solution)/shard_map/ppermute | solution.py:1032
  234.1 25.4 %collective-permute-start.31 = (bf16[1,1,48,3200]{3,2,1,0:T(8,128)(2,1)}, bf16[1,1,48,3200]{3,2,1,0:T(8,128)(2,1)}, u32[]{:S(2)}, u32[]{:S(2)}) collective-permute-start(bf16[1,1,48,3200]{3,2,1,0:T(8,128)(2,1)} %get-tuple-element.168), channel_id=1, source_target_pairs={{0,16},{2,18},{4,20},{6,22},{8,24},{10,26},{12,28},{14,30},{16,0},... | collective-permute-start | bytes 921608 | tf_op jit(solution)/shard_map/ppermute | solution.py:1032
  236.9 30.6 %collective-permute-start.32 = (bf16[1,1,48,3200]{3,2,1,0:T(8,128)(2,1)S(1)}, bf16[1,1,48,3200]{3,2,1,0:T(8,128)(2,1)}, u32[]{:S(2)}, u32[]{:S(2)}) collective-permute-start(bf16[1,1,48,3200]{3,2,1,0:T(8,128)(2,1)S(1)} %get-tuple-element.166), channel_id=1, source_target_pairs={{0,24},{2,26},{4,28},{6,30},{8,16},{10,18},{12,20},{14,22},{16,8},... | collective-permute-start | bytes 921608 | tf_op jit(solution)/shard_map/ppermute | solution.py:1032
  242.6 31.5 %collective-permute-start.25 = (bf16[512,768]{1,0:T(8,128)(2,1)S(1)}, bf16[512,768]{1,0:T(8,128)(2,1)S(1)}, u32[]{:S(2)}, u32[]{:S(2)}) collective-permute-start(bf16[512,768]{1,0:T(8,128)(2,1)S(1)} %fusion), channel_id=1, source_target_pairs={{0,1},{1,0},{2,3},{3,2},{4,5},{5,4},{6,7},{7,6},{8,9},{9,8},{10,11... | collective-permute-start | bytes 2359304 | tf_op jit(solution)/shard_map/ppermute | solution.py:1103
  (30 other events, 161.9 us)
